TPU v7x, 256 devices: a whole 4x4x8 slice. The times are simulated.
256 devices in a mesh: wide: 8 (over x, core), narrow: 32 (over z, y).
Axes of the slice: x: 4, y: 4, z: 8, core: 2. Of those that a mesh axis runs over, the one named last changes fastest.
Arguments:
- rhs: float32 [65536, 2, 128], P(('wide', 'narrow')), may hold values from -6 to 6
- fine_face: float32 [65536, 2, 128], P(('wide', 'narrow')), may hold values from 0.2 to 2
- fine_sink: float32 [65536, 2, 128], P(('wide', 'narrow')), may hold values from 0.01 to 0.5
- fine_kap: float32 [65536, 128], P(('wide', 'narrow')), may hold values from -0.9 to 0.9
- cell_mask: int32 [65536, 128], P(('wide', 'narrow')), may hold values 0 or 1
- block_aggregate: int32 [65536], P(('wide', 'narrow')), may hold values from 0 to 2047, as said below
- coarse_face: float32 [16384, 2, 128], P(('wide', 'narrow')), may hold values from 0.2 to 2
- coarse_sink: float32 [16384, 2, 128], P(('wide', 'narrow')), may hold values from 0.02 to 1
- coarse_kap: float32 [16384, 128], P(('wide', 'narrow')), may hold values from -0.9 to 0.9
Outputs:
- solution: float32 [65536, 2, 128], P(('wide', 'narrow'))
Inputs may be any that keep to these rules, and one draw needn't show every extreme that they name: `block_aggregate`: aggregates are numbered within the group of devices sharing a wide index; aggregate a lives on the device with narrow index a // 64; the 256 blocks of one device name aggregates of any one such owner at most 16 times, and in every group one owner is named exactly 16 times by the blocks of every device of the group.
All inputs are finite; a program needn't handle non-finite values. No bound on the sum of `cell_mask` on one device may be relied on, other than what follows from the above.
Results may differ from a plain program's by a relative error of at most 0.00005.
Values sent between devices are 32-bit elements; how exact they have to be, the bound alone decides.
No kernel may reach another device: no remote copies, remote signals or barrier semaphores. Data moves between devices by JAX's collectives and lax.ppermute only.
A program may use at most 192 MiB of HBM per device.

v0:
```python
import jax
import jax.numpy as jnp
from jax import lax
from jax.sharding import PartitionSpec as P

PRE = 2
POST = 2
CSWEEPS = 4
LEVELS = 4


OMEGA = 0.8


def with_halo(value, sides, width):
    for axis, dim in sides:
        count, length = (lax.axis_size(axis), value.shape[dim])
        up = [(i, (i + 1) % count) for i in range(count - 1)]
        down = [(j, i) for i, j in up]
        last = lax.slice_in_dim(value, length - width, length, axis=dim)
        leading = lax.slice_in_dim(value, 0, width, axis=dim)
        before = lax.ppermute(last, axis, up)
        after = lax.ppermute(leading, axis, down)
        value = jnp.concatenate([before, value, after], axis=dim)
    return value


def from_partner(value, axis, bit):
    return lax.ppermute(value, axis, [(i, i ^ 1 << bit) for i in range(lax.axis_size(axis))])


def prev_cells(field, before):
    lastcol = field[..., -1]
    carried = jnp.concatenate([before[None], lastcol[:-1]], axis=0)
    return jnp.concatenate([carried[..., None], field[..., :-1]], axis=-1)


def next_cells(field, after):
    firstcol = field[..., 0]
    carried = jnp.concatenate([firstcol[1:], after[None]], axis=0)
    return jnp.concatenate([field[..., 1:], carried[..., None]], axis=-1)


def operate(field, behind, ahead, faces, faces_left, diagonal, coupling):
    crossed = jnp.stack([field[:, 1], field[:, 0]], axis=1)
    return diagonal * field - faces_left * behind - faces * ahead - coupling[:, None, :] * crossed


def inverse_parts(diagonal, coupling):
    determinant = diagonal[:, 0] * diagonal[:, 1] - coupling * coupling
    return (diagonal[:, 1] / determinant, diagonal[:, 0] / determinant, coupling / determinant)


def relax(field, misfit, inverse):
    first_part = inverse[0] * misfit[:, 0] + inverse[2] * misfit[:, 1]
    second_part = inverse[2] * misfit[:, 0] + inverse[1] * misfit[:, 1]
    return field + OMEGA * jnp.stack([first_part, second_part], axis=1)


def closed_apply(field, data):
    edge = jnp.zeros(field.shape[1:-1], jnp.float32)
    return operate(
        field, prev_cells(field, edge), next_cells(field, edge), data[0], data[1], data[2], data[3]
    )


def level_setup(faces, sinks, coupling):
    faces_left = prev_cells(faces, jnp.zeros(faces.shape[1:-1], jnp.float32))
    diagonal = sinks + faces_left + faces
    return (faces, faces_left, diagonal, coupling, inverse_parts(diagonal, coupling))


def smooth(field, source, data, sweeps):
    for _ in range(sweeps):
        field = relax(field, source - closed_apply(field, data), data[4])
    return field


def start_smooth(source, data, sweeps):
    field = relax(jnp.zeros_like(source), source, data[4])
    return smooth(field, source, data, sweeps - 1)


def on_device(
    rhs,
    fine_face,
    fine_sink,
    fine_kap,
    cell_mask,
    block_aggregate,
    coarse_face,
    coarse_sink,
    coarse_kap,
):
    live = cell_mask.astype(jnp.float32)
    edges = jnp.stack(
        [
            jnp.stack([live[0, 0], live[-1, -1]]),
            jnp.stack([fine_face[0, 0, 0], fine_face[-1, 0, -1]]),
            jnp.stack([fine_face[0, 1, 0], fine_face[-1, 1, -1]]),
        ]
    )
    rims = with_halo(edges, (("narrow", 1),), 1)
    live_next = next_cells(live, rims[0, 3])
    faces = fine_face * live[:, None, :] * live_next[:, None, :]
    faces_before = rims[1:, 0] * rims[0, 0] * live[0, 0]
    faces_left = prev_cells(faces, faces_before)
    diagonal = fine_sink + faces_left + faces
    coupling = fine_kap * jnp.sqrt(fine_sink[:, 0] * fine_sink[:, 1]) * live
    inverse = inverse_parts(diagonal, coupling)
    source = rhs * live[:, None, :]

    def fine_apply(field):
        outer = jnp.stack([field[0, :, 0], field[-1, :, -1]], axis=1)
        padded = with_halo(outer, (("narrow", 1),), 1)
        return operate(
            field,
            prev_cells(field, padded[:, 0]),
            next_cells(field, padded[:, 3]),
            faces,
            faces_left,
            diagonal,
            coupling,
        )

    field = relax(jnp.zeros_like(source), source, inverse)
    field = relax(field, source - fine_apply(field), inverse)
    misfit = source - fine_apply(field)
    owned = coarse_face.shape[0]
    labels = lax.iota(jnp.int32, lax.axis_size("narrow") * owned)
    onehot = (block_aggregate[:, None] == labels[None, :]).astype(jnp.float32)
    source_c = lax.psum_scatter(
        jnp.einsum("ba,bfc->afc", onehot, misfit, precision=lax.Precision.HIGHEST),
        "narrow",
        scatter_dimension=0,
        tiled=True,
    )
    faces_c = coarse_face.at[-1, :, -1].set(0.0)
    sinks_c = coarse_sink
    coupling_c = coarse_kap * jnp.sqrt(sinks_c[:, 0] * sinks_c[:, 1])
    saved = []
    correction = source_c
    for level in range(LEVELS):
        data = level_setup(faces_c, sinks_c, coupling_c)
        if level < LEVELS - 1:
            correction = start_smooth(source_c, data, PRE)
            leftover = source_c - closed_apply(correction, data)
            saved.append((correction, source_c, data))
            partner = from_partner((leftover, faces_c, sinks_c, coupling_c), "wide", level)
            source_c = leftover + partner[0]
            faces_c = faces_c + partner[1]
            sinks_c = sinks_c + partner[2]
            coupling_c = coupling_c + partner[3]
        else:
            correction = start_smooth(source_c, data, CSWEEPS)
    for level in reversed(range(LEVELS - 1)):
        below, level_source, data = saved[level]
        correction = smooth(below + correction, level_source, data, POST)
    piece = lax.all_gather(correction, "narrow", axis=0, tiled=True)
    labels = lax.iota(jnp.int32, piece.shape[0])
    onehot = (block_aggregate[:, None] == labels[None, :]).astype(jnp.float32)
    lifted = jnp.einsum("ba,afc->bfc", onehot, piece, precision=lax.Precision.HIGHEST)
    field = field + lifted
    for _ in range(POST):
        field = relax(field, source - fine_apply(field), inverse)
    return field


def solution(mesh):
    placed = (
        P(("wide", "narrow"), None, None),
        P(("wide", "narrow"), None, None),
        P(("wide", "narrow"), None, None),
        P(("wide", "narrow"), None),
        P(("wide", "narrow"), None),
        P(("wide", "narrow")),
        P(("wide", "narrow"), None, None),
        P(("wide", "narrow"), None, None),
        P(("wide", "narrow"), None),
    )
    return jax.shard_map(
        on_device,
        mesh=mesh,
        in_specs=placed,
        out_specs=P(("wide", "narrow"), None, None),
        check_vma=False,
    )
```

profile of v0, /device:TPU:32, one launch (start us, length us, event | category | flops | bytes accessed | tf_op | source)
XLA Modules:
  0.0 431.5 jit_solution(3261914342522702997)
XLA Ops:
  10.9 2.5 maximum_bitcast_fusion.2
  13.5 3.5 collective-permute-start
  17.0 4.5 %collective-permute-start.1 = (f32[3,1]{1,0:T(4,128)S(1)}, f32[3,1]{1,0:T(4,128)S(1)}, u32[]{:S(2)}, u32[]{:S(2)}) collective-permute-start(f32[3,1]{1,0:T(4,128)S(1)} %get-tuple-element.227), channel_id=1, source_target_pairs={{1,0},{2,1},{3,2},{4,3},{5,4},{6,5},{7,6},{8,7},{9,8},{10,9},{11,1... | collective-permute-start | bytes 44 | tf_op jit(solution)/shard_map/ppermute | solution.py:23
  28.7 4.1 collective-permute-start.3
  32.8 1.9 collective-permute-start.2
  34.9 5.4 %collective-permute-done.2 = f32[2,1]{0,1:T(1,128)S(1)} collective-permute-done((f32[2,1]{0,1:T(1,128)S(1)}, f32[2,1]{0,1:T(1,128)S(1)}, u32[]{:S(2)}, u32[]{:S(2)}) %collective-permute-start.2) | collective-permute-done | bytes 40 | tf_op jit(solution)/shard_map/ppermute | solution.py:22
  41.1 1.9 collective-permute-start.5
  43.0 3.9 collective-permute-start.4
  47.2 3.4 collective-permute-done.4
  50.8 2.8 fusion.7
  56.6 217.2 %reduce-scatter.2.cloned.1.call-done = f32[64,2,128]{2,0,1:T(8,128)} async-done(((f32[2048,2,128]{2,0,1:T(8,128)}), f32[64,2,128]{2,0,1:T(8,128)}) %reduce-scatter.2.cloned.1.call-update) | async-done | bytes 65552 | tf_op jit(solution)/shard_map/reduce_scatter | solution.py:132
  281.2 1.9 collective-permute-done.11
  286.5 3.3 collective-permute-start.15
  290.7 2.0 collective-permute-done.15
  298.5 1.9 collective-permute-start.16
  300.4 2.2 collective-permute-done.17
  322.5 75.3 %all-gather.2.cloned.1.call-done = f32[2048,2,128]{2,0,1:T(8,128)} async-done(((f32[64,2,128]{2,0,1:T(8,128)}), f32[2048,2,128]{2,0,1:T(8,128)}) %all-gather.2.cloned.1.call-update) | async-done | bytes 2097168 | tf_op jit(solution)/shard_map/all_gather | solution.py:159
  397.9 3.5 fusion.4
  401.7 3.9 collective-permute-start.19
  405.6 2.0 collective-permute-start.18
  407.8 5.4 %collective-permute-done.18 = f32[2,1]{0,1:T(1,128)S(1)} collective-permute-done((f32[2,1]{0,1:T(1,128)S(1)}, f32[2,1]{0,1:T(1,128)S(1)}, u32[]{:S(2)}, u32[]{:S(2)}) %collective-permute-start.18) | collective-permute-done | bytes 40 | tf_op jit(solution)/shard_map/ppermute | solution.py:22
  413.9 1.9 collective-permute-start.21
  415.8 3.9 collective-permute-start.20
  420.0 3.4 collective-permute-done.20
  (323 shorter events, 54.8 us)
Async XLA Ops:
  6.5 267.3 %reduce-scatter.2.cloned.1.call-start = ((), (), s32[]{:S(2)}) async-start(), calls=%async_computation.1 | async-start | bytes 2162688 | tf_op jit(solution)/shard_map/reduce_scatter | solution.py:132
  13.5 12.8 %collective-permute-start = (f32[3,1]{1,0:T(4,128)S(1)}, f32[3,1]{1,0:T(4,128)S(1)}, u32[]{:S(2)}, u32[]{:S(2)}) collective-permute-start(f32[3,1]{1,0:T(4,128)S(1)} %get-tuple-element.226), channel_id=1, source_target_pairs={{0,1},{1,2},{2,3},{3,4},{4,5},{5,6},{6,7},{7,8},{8,9},{9,10},{10,1... | collective-permute-start | bytes 44 | tf_op jit(solution)/shard_map/ppermute | solution.py:22
  17.0 7.9 %collective-permute-start.1 = (f32[3,1]{1,0:T(4,128)S(1)}, f32[3,1]{1,0:T(4,128)S(1)}, u32[]{:S(2)}, u32[]{:S(2)}) collective-permute-start(f32[3,1]{1,0:T(4,128)S(1)} %get-tuple-element.227), channel_id=1, source_target_pairs={{1,0},{2,1},{3,2},{4,3},{5,4},{6,5},{7,6},{8,7},{9,8},{10,9},{11,1... | collective-permute-start | bytes 44 | tf_op jit(solution)/shard_map/ppermute | solution.py:23
  28.7 6.1 %collective-permute-start.3 = (f32[2,1]{0,1:T(1,128)S(1)}, f32[2,1]{0,1:T(1,128)S(1)}, u32[]{:S(2)}, u32[]{:S(2)}) collective-permute-start(f32[2,1]{0,1:T(1,128)S(1)} %bitcast.669), channel_id=1, source_target_pairs={{1,0},{2,1},{3,2},{4,3},{5,4},{6,5},{7,6},{8,7},{9,8},{10,9},{11,1... | collective-permute-start | bytes 32 | tf_op jit(solution)/shard_map/ppermute | solution.py:23
  32.8 7.5 %collective-permute-start.2 = (f32[2,1]{0,1:T(1,128)S(1)}, f32[2,1]{0,1:T(1,128)S(1)}, u32[]{:S(2)}, u32[]{:S(2)}) collective-permute-start(f32[2,1]{0,1:T(1,128)S(1)} %bitcast.665), channel_id=1, source_target_pairs={{0,1},{1,2},{2,3},{3,4},{4,5},{5,6},{6,7},{7,8},{8,9},{9,10},{10,1... | collective-permute-start | bytes 32 | tf_op jit(solution)/shard_map/ppermute | solution.py:22
  41.1 5.9 %collective-permute-start.5 = (f32[2,1]{0,1:T(1,128)S(1)}, f32[2,1]{0,1:T(1,128)S(1)}, u32[]{:S(2)}, u32[]{:S(2)}) collective-permute-start(f32[2,1]{0,1:T(1,128)S(1)} %bitcast.671), channel_id=1, source_target_pairs={{1,0},{2,1},{3,2},{4,3},{5,4},{6,5},{7,6},{8,7},{9,8},{10,9},{11,1... | collective-permute-start | bytes 32 | tf_op jit(solution)/shard_map/ppermute | solution.py:23
  43.0 7.5 %collective-permute-start.4 = (f32[2,1]{0,1:T(1,128)S(1)}, f32[2,1]{0,1:T(1,128)S(1)}, u32[]{:S(2)}, u32[]{:S(2)}) collective-permute-start(f32[2,1]{0,1:T(1,128)S(1)} %bitcast.667), channel_id=1, source_target_pairs={{0,1},{1,2},{2,3},{3,4},{4,5},{5,6},{6,7},{7,8},{8,9},{9,10},{10,1... | collective-permute-start | bytes 32 | tf_op jit(solution)/shard_map/ppermute | solution.py:22
  53.6 344.3 %all-gather.2.cloned.1.call-start = ((), (), s32[]{:S(2)}) async-start(), calls=%async_computation.2 | async-start | bytes 2162688 | tf_op jit(solution)/shard_map/all_gather | solution.py:159
  54.6 1.3 collective-permute-start.7
  56.4 219.8 %collective-permute-start.6 = (f32[64,2,128]{2,0,1:T(8,128)S(1)}, f32[64,2,128]{2,0,1:T(8,128)S(1)}, u32[]{:S(2)}, u32[]{:S(2)}) collective-permute-start(f32[64,2,128]{2,0,1:T(8,128)S(1)} %get-tuple-element.217), channel_id=1, source_target_pairs={{0,32},{32,0},{64,96},{96,64},{128,160},{160,128},{192,224},{224,1... | collective-permute-start | bytes 196616 | tf_op jit(solution)/shard_map/ppermute | solution.py:29
  277.9 2.6 collective-permute-start.9
  278.0 2.5 collective-permute-start.8
  278.5 4.6 %collective-permute-start.11 = (f32[64,2,128]{2,0,1:T(8,128)S(1)}, f32[64,2,128]{2,0,1:T(8,128)S(1)}, u32[]{:S(2)}, u32[]{:S(2)}) collective-permute-start(f32[64,2,128]{2,0,1:T(8,128)S(1)} %get-tuple-element.216), channel_id=1, source_target_pairs={{0,64},{32,96},{64,0},{96,32},{128,192},{160,224},{192,128},{224,1... | collective-permute-start | bytes 196616 | tf_op jit(solution)/shard_map/ppermute | solution.py:29
  279.9 4.3 collective-permute-start.10
  284.4 5.6 %collective-permute-start.13 = (f32[64,2,128]{2,0,1:T(8,128)S(1)}, f32[64,2,128]{2,0,1:T(8,128)S(1)}, u32[]{:S(2)}, u32[]{:S(2)}) collective-permute-start(f32[64,2,128]{2,0,1:T(8,128)S(1)} %get-tuple-element.204), channel_id=1, source_target_pairs={{0,64},{32,96},{64,0},{96,32},{128,192},{160,224},{192,128},{224,1... | collective-permute-start | bytes 196616 | tf_op jit(solution)/shard_map/ppermute | solution.py:29
  286.1 4.0 collective-permute-start.12
  286.5 6.3 %collective-permute-start.15 = (f32[64,2,128]{2,0,1:T(8,128)S(1)}, f32[64,2,128]{2,0,1:T(8,128)S(1)}, u32[]{:S(2)}, u32[]{:S(2)}) collective-permute-start(f32[64,2,128]{2,0,1:T(8,128)S(1)} %get-tuple-element.205), channel_id=1, source_target_pairs={{0,128},{32,160},{64,192},{96,224},{128,0},{160,32},{192,64},{224,... | collective-permute-start | bytes 196616 | tf_op jit(solution)/shard_map/ppermute | solution.py:29
  289.8 5.9 %collective-permute-start.14 = (f32[64,2,128]{2,0,1:T(8,128)S(1)}, f32[64,2,128]{2,0,1:T(8,128)}, u32[]{:S(2)}, u32[]{:S(2)}) collective-permute-start(f32[64,2,128]{2,0,1:T(8,128)S(1)} %get-tuple-element.71), channel_id=1, source_target_pairs={{0,128},{32,160},{64,192},{96,224},{128,0},{160,32},{192,64},{224,... | collective-permute-start | bytes 196616 | tf_op jit(solution)/shard_map/ppermute | solution.py:29
  296.6 6.0 %collective-permute-start.17 = (f32[64,2,128]{2,0,1:T(8,128)S(1)}, f32[64,2,128]{2,0,1:T(8,128)S(1)}, u32[]{:S(2)}, u32[]{:S(2)}) collective-permute-start(f32[64,2,128]{2,0,1:T(8,128)S(1)} %get-tuple-element.193), channel_id=1, source_target_pairs={{0,128},{32,160},{64,192},{96,224},{128,0},{160,32},{192,64},{224,... | collective-permute-start | bytes 196616 | tf_op jit(solution)/shard_map/ppermute | solution.py:29
  298.5 5.4 %collective-permute-start.16 = (f32[64,128]{1,0:T(8,128)S(1)}, f32[64,128]{1,0:T(8,128)S(1)}, u32[]{:S(2)}, u32[]{:S(2)}) collective-permute-start(f32[64,128]{1,0:T(8,128)S(1)} %get-tuple-element.66), channel_id=1, source_target_pairs={{0,128},{32,160},{64,192},{96,224},{128,0},{160,32},{192,64},{224,... | collective-permute-start | bytes 98312 | tf_op jit(solution)/shard_map/ppermute | solution.py:29
  401.7 5.9 %collective-permute-start.19 = (f32[2,1]{0,1:T(1,128)S(1)}, f32[2,1]{0,1:T(1,128)S(1)}, u32[]{:S(2)}, u32[]{:S(2)}) collective-permute-start(f32[2,1]{0,1:T(1,128)S(1)} %bitcast.672), channel_id=1, source_target_pairs={{1,0},{2,1},{3,2},{4,3},{5,4},{6,5},{7,6},{8,7},{9,8},{10,9},{11,1... | collective-permute-start | bytes 32 | tf_op jit(solution)/shard_map/ppermute | solution.py:23
  405.6 7.5 %collective-permute-start.18 = (f32[2,1]{0,1:T(1,128)S(1)}, f32[2,1]{0,1:T(1,128)S(1)}, u32[]{:S(2)}, u32[]{:S(2)}) collective-permute-start(f32[2,1]{0,1:T(1,128)S(1)} %bitcast.668), channel_id=1, source_target_pairs={{0,1},{1,2},{2,3},{3,4},{4,5},{5,6},{6,7},{7,8},{8,9},{9,10},{10,1... | collective-permute-start | bytes 32 | tf_op jit(solution)/shard_map/ppermute | solution.py:22
  413.9 5.9 %collective-permute-start.21 = (f32[2,1]{0,1:T(1,128)S(1)}, f32[2,1]{0,1:T(1,128)S(1)}, u32[]{:S(2)}, u32[]{:S(2)}) collective-permute-start(f32[2,1]{0,1:T(1,128)S(1)} %bitcast.670), channel_id=1, source_target_pairs={{1,0},{2,1},{3,2},{4,3},{5,4},{6,5},{7,6},{8,7},{9,8},{10,9},{11,1... | collective-permute-start | bytes 32 | tf_op jit(solution)/shard_map/ppermute | solution.py:23
  415.8 7.5 %collective-permute-start.20 = (f32[2,1]{0,1:T(1,128)S(1)}, f32[2,1]{0,1:T(1,128)S(1)}, u32[]{:S(2)}, u32[]{:S(2)}) collective-permute-start(f32[2,1]{0,1:T(1,128)S(1)} %bitcast.666), channel_id=1, source_target_pairs={{0,1},{1,2},{2,3},{3,4},{4,5},{5,6},{6,7},{7,8},{8,9},{9,10},{10,1... | collective-permute-start | bytes 32 | tf_op jit(solution)/shard_map/ppermute | solution.py:22
  (17 other events, 302.0 us)
Sparse Core Ops, SparseCore 0:
  53.7 220.1 reduce-scatter.1
  322.7 75.1 all-gather.1
where the time goes:
time: 434 us; the launch traced here: 432 us
  waiting for transfers between devices  320 us (74%)
  starting transfers between devices  43.9 us (10%)
  local copies, waits for them, and re-layouts  28.5 us (7%)
  other arithmetic  18.2 us (4%)
  between operations  14.8 us (3%)
  matrix products  6.28 us (1%)
    reduce_scatter x1, waiting for transfers between devices, on_device(): lax.psum_scatter(jnp.einsum('ba,bfc->afc', onehot, misfit, precision=lax....  217 us
    all_gather x1, waiting for transfers between devices, on_device(): piece = lax.all_gather(correction, 'narrow', axis=0, tiled=True)  75.3 us
    ppermute x5, waiting for transfers between devices, with_halo(): before = lax.ppermute(last, axis, up)  17.6 us
    ppermute x5, starting transfers between devices, with_halo(): after = lax.ppermute(leading, axis, down)  16.3 us
    ppermute x5, starting transfers between devices, with_halo(): before = lax.ppermute(last, axis, up)  15.2 us
    ppermute x12, starting transfers between devices, from_partner(): lax.ppermute(value, axis, [(i, i ^ 1 << bit) for i in range(lax.axis_size...  12.4 us
    ppermute x12, waiting for transfers between devices, from_partner(): lax.ppermute(value, axis, [(i, i ^ 1 << bit) for i in range(lax.axis_size...  9.58 us
  transfers between devices with their start and end apart: 24, of which 12 were waited for; matrix products, arithmetic and copies ran while one was open for 3% of the time, Pallas kernels for 0%

commit v1 on v0

v1 whole, which is shorter than its diff:
```python
import jax
import jax.numpy as jnp
from jax import lax
from jax.experimental import pallas as pl
from jax.experimental.pallas import tpu as pltpu
from jax.sharding import PartitionSpec as P

OMEGA = 0.8
LANES = 128
BLK = 256
AGG = 64
NARROW = 32
CAP = 16
UNIT = 2 * (CAP + 1)
F32, BF16, I32 = jnp.float32, jnp.bfloat16, jnp.int32


def iota(shape, dim):
    return lax.broadcasted_iota(I32, shape, dim)


def chain_next(v):
    ahead = pltpu.roll(v, LANES - 1, 1)
    below = pltpu.roll(ahead, v.shape[0] - 1, 0)
    return jnp.where(iota(v.shape, 1) == LANES - 1, below, ahead)


def chain_prev(v):
    behind = pltpu.roll(v, 1, 1)
    above = pltpu.roll(behind, 1, 0)
    return jnp.where(iota(v.shape, 1) == 0, above, behind)


def row_next(v):
    return pltpu.roll(v, LANES - 1, 1)


def row_prev(v):
    return pltpu.roll(v, 1, 1)


class Level:
    def __init__(self, faces, sinks, coupling, prev, nxt):
        self.prev, self.nxt = prev, nxt
        self.faces = faces
        self.left = [prev(f) for f in faces]
        self.diag = [s + l + f for s, l, f in zip(sinks, self.left, faces)]
        self.coupling = coupling
        scale = OMEGA / (self.diag[0] * self.diag[1] - coupling * coupling)
        self.inv = (self.diag[1] * scale, self.diag[0] * scale, coupling * scale)

    def misfit(self, v, source):
        return [
            source[f]
            - (
                self.diag[f] * v[f]
                - self.left[f] * self.prev(v[f])
                - self.faces[f] * self.nxt(v[f])
                - self.coupling * v[1 - f]
            )
            for f in (0, 1)
        ]

    def step(self, r):
        return [
            self.inv[0] * r[0] + self.inv[2] * r[1],
            self.inv[2] * r[0] + self.inv[1] * r[1],
        ]

    def smooth(self, v, source, sweeps):
        for _ in range(sweeps):
            d = self.step(self.misfit(v, source))
            v = [v[0] + d[0], v[1] + d[1]]
        return v

    def start(self, source, sweeps):
        return self.smooth(self.step(source), source, sweeps - 1)


def fine_level(face, sink, kap, live, prev, nxt, last):
    live_next = jnp.where(last, 0.0, nxt(live))
    both = live * live_next
    faces = [f * both for f in face]
    coupling = kap * jnp.sqrt(sink[0] * sink[1]) * live
    return Level(faces, sink, coupling, prev, nxt)


def last_cell(shape):
    return (iota(shape, 0) == shape[0] - 1) & (iota(shape, 1) == LANES - 1)


def split3(x):
    hi = x.astype(BF16)
    rest = x - hi.astype(F32)
    mid = rest.astype(BF16)
    return hi, mid, (rest - mid.astype(F32)).astype(BF16)


def select_rows(onehot, x):
    total = None
    for part in split3(x):
        term = jnp.dot(onehot, part, preferred_element_type=F32)
        total = term if total is None else total + term
    return total


def as_bf16(mask):
    return jnp.where(mask, 1.0, 0.0).astype(BF16)


def planar(ref, rows):
    return [ref[pl.ds(f, rows, stride=2), :] for f in (0, 1)]


def fine_inputs(rhs, face, sink, kap, mask):
    live = mask[...].astype(F32)
    shape = (BLK, LANES)
    data = fine_level(
        planar(face, BLK), planar(sink, BLK), kap[...], live, chain_prev, chain_next, last_cell(shape)
    )
    source = [r * live for r in planar(rhs, BLK)]
    return data, source


def pre_kernel(narrow, rhs, face, sink, kap, mask, agg, out, slots):
    n = narrow[0]
    data, source = fine_inputs(rhs, face, sink, kap, mask)
    field = data.start(source, 2)
    misfit = data.misfit(field, source)
    row, lane = iota((BLK, LANES), 0), iota((BLK, LANES), 1)
    drop = ((row == BLK - 1) & (lane >= LANES - 3) & (n < NARROW - 1)) | (
        (row == 0) & (lane < 3) & (n > 0)
    )
    misfit = jnp.concatenate([jnp.where(drop, 0.0, m) for m in misfit], axis=1)

    label = agg[...]
    owner = label // AGG
    within = label - owner * AGG
    owned = iota((NARROW, BLK), 0) == owner
    before = as_bf16(iota((BLK, BLK), 0) < iota((BLK, BLK), 1))
    counts = jnp.dot(as_bf16(owned), before, preferred_element_type=F32)
    rank = jnp.sum(jnp.where(owned, counts, 0.0), axis=0, keepdims=True).astype(I32)
    slot = owner * CAP + rank
    put = as_bf16(iota((NARROW * CAP, BLK), 0) == slot)
    rows = select_rows(put, misfit)
    for o in range(NARROW):
        for f in (0, 1):
            out[pl.ds(o * UNIT + f, CAP, stride=2), :] = rows[
                o * CAP : (o + 1) * CAP, f * LANES : (f + 1) * LANES
            ]

    block = iota((1, BLK), 1)
    code = within + 1 + jnp.where(block == 0, 64, 0) + jnp.where(block == BLK - 1, 128, 0)
    coded = jnp.where(owned, code.astype(F32), 0.0).astype(BF16)
    at_rank = as_bf16(iota((LANES, BLK), 0) % CAP == rank)
    labels = lax.dot_general(
        coded, at_rank, (((1,), (1,)), ((), ())), preferred_element_type=F32
    )
    out[pl.ds(2 * CAP, NARROW, stride=UNIT), :] = labels

    lane1 = iota((1, LANES), 1)
    edges = jnp.zeros((1, LANES), F32)
    quantities = [(ref, 2, f) for ref in (rhs, face, sink) for f in (0, 1)]
    quantities += [(kap, 1, 0), (mask, 1, 0)]
    for q, (ref, stride, f) in enumerate(quantities):
        final = (BLK - 1) * stride + f
        cells = jnp.where(
            lane1 >= LANES // 2, ref[final : final + 1, :], ref[f : f + 1, :]
        ).astype(F32)
        moved = pltpu.roll(cells, (16 * q + 8) % LANES, 1)
        edges = jnp.where(lane1 // 16 == q, moved, edges)
    out[pl.ds(2 * CAP + 1, NARROW, stride=UNIT), :] = jnp.broadcast_to(edges, (NARROW, LANES))

    slots[...] = jnp.transpose(jnp.broadcast_to(slot.astype(F32), (LANES, BLK)), (1, 0))


def interface_level(cells):
    lane = iota(cells.shape, 1)

    def quantity(q, fill):
        moved = cells if q == 0 else pltpu.roll(cells, LANES - 16 * q, 1)
        return jnp.where(lane < 16, moved, fill)

    rhs = [quantity(0, 0.0), quantity(1, 0.0)]
    face = [quantity(2, 0.0), quantity(3, 0.0)]
    sink = [quantity(4, 1.0), quantity(5, 1.0)]
    kap, live = quantity(6, 0.0), quantity(7, 0.0)
    data = fine_level(face, sink, kap, live, row_prev, row_next, lane == LANES - 1)
    source = [r * live for r in rhs]
    return data, source


def coarse_level(ref):
    part = [ref[k * AGG : (k + 1) * AGG, :] for k in range(5)]
    return Level(part[0:2], part[2:4], part[4], chain_prev, chain_next)


def store2(ref, v):
    ref[0:AGG, :] = v[0]
    ref[AGG : 2 * AGG, :] = v[1]


def load2(ref):
    return [ref[0:AGG, :], ref[AGG : 2 * AGG, :]]


def coef_kernel(face, sink, kap, out):
    faces, sinks = planar(face, AGG), planar(sink, AGG)
    last = last_cell((AGG, LANES))
    for f in (0, 1):
        out[f * AGG : (f + 1) * AGG, :] = jnp.where(last, 0.0, faces[f])
        out[(2 + f) * AGG : (3 + f) * AGG, :] = sinks[f]
    out[4 * AGG : 5 * AGG, :] = kap[...] * jnp.sqrt(sinks[0] * sinks[1])


def restrict_kernel(narrow, recv, coef, leftover, below, source_out, marks, own_edges):
    n = narrow[0]
    lane = iota((NARROW, LANES), 1)
    src = iota((NARROW, LANES), 0)
    labels = recv[pl.ds(2 * CAP, NARROW, stride=UNIT), :]
    raw = recv[pl.ds(2 * CAP + 1, NARROW, stride=UNIT), :]
    code = labels.astype(I32)
    plain = (code - 1) % AGG
    plain = jnp.where(code > 0, plain, -1)

    cells = jnp.where(lane % 16 < 8, raw, pltpu.roll(raw, NARROW - 1, 0))
    data, source = interface_level(cells)
    field = data.start(source, 2)
    mis = [pltpu.roll(m, LANES - 8, 1) for m in data.misfit(field, source)]
    mis = jnp.concatenate(mis, axis=1)
    wide_lane = iota((NARROW, 2 * LANES), 1) % LANES
    real = iota((NARROW, 2 * LANES), 0) < NARROW - 1
    after_end = jnp.where((wide_lane >= LANES - 3) & real, mis, 0.0)
    at_start = jnp.where((wide_lane < 3) & real, mis, 0.0)
    is_end = (code > 128) & (lane < CAP)
    is_start = (code > 64) & (code <= 128) & (lane < CAP)
    end_at = jnp.max(jnp.where(is_end, plain, -1), axis=1, keepdims=True)
    start_at = jnp.max(jnp.where(is_start, plain, -1), axis=1, keepdims=True)
    end_hot = jnp.where(lane == end_at, 1.0, 0.0)
    start_hot = jnp.where(lane == start_at, 1.0, 0.0)
    start_next = pltpu.roll(start_hot, NARROW - 1, 0)
    zeros = jnp.zeros((2 * NARROW, LANES), F32)
    hot = jnp.transpose(jnp.concatenate([end_hot, start_next, zeros], axis=0), (1, 0))
    edge_hot = hot[0:AGG, :].astype(BF16)
    edge_rows = jnp.concatenate(
        [after_end, at_start, jnp.zeros((2 * NARROW, 2 * LANES), F32)], axis=0
    )

    rows = []
    for t in range(NARROW // 8):
        mine = jnp.where(lane[0:8] // CAP == src[0:8], plain[8 * t : 8 * t + 8], 0)
        rows.append(jnp.sum(mine, axis=0, keepdims=True))
    total = select_rows(edge_hot, edge_rows)
    for half in (0, 1):
        hots, parts = [], []
        for t in (2 * half, 2 * half + 1):
            hots.append(iota((AGG, LANES), 0) == rows[t])
            for s in range(8 * t, 8 * t + 8):
                parts.append(
                    jnp.concatenate(
                        [recv[pl.ds(s * UNIT + f, CAP, stride=2), :] for f in (0, 1)], axis=1
                    )
                )
        total = total + select_rows(
            as_bf16(jnp.concatenate(hots, axis=1)), jnp.concatenate(parts, axis=0)
        )
    source_c = [total[:, 0:LANES], total[:, LANES:]]
    level = coarse_level(coef)
    correction = level.start(source_c, 2)
    store2(leftover, level.misfit(correction, source_c))
    store2(below, correction)
    store2(source_out, source_c)

    for t in range(NARROW // 8):
        marks[t : t + 1, :] = rows[t].astype(F32)
    marks[8 : 8 + NARROW, :] = pltpu.roll(end_hot, 1, 0)
    marks[8 + NARROW : 8 + 2 * NARROW, :] = start_next
    own_edges[0:1, :] = jnp.sum(jnp.where(src == n - 1, cells, 0.0), axis=0, keepdims=True)
    own_edges[1:2, :] = jnp.sum(jnp.where(src == n, cells, 0.0), axis=0, keepdims=True)


def second_kernel(mine, other, coef, leftover, below, source_out):
    source = [a + b for a, b in zip(load2(mine), load2(other))]
    level = coarse_level(coef)
    correction = level.start(source, 2)
    store2(leftover, level.misfit(correction, source))
    store2(below, correction)
    store2(source_out, source)


def top_kernel(
    left2, left2_a, left2_b, left2_c,
    coef2, coef2_a, coef2_b, coef2_c,
    below2, source2, coef1, below1, source1, marks, out, near, far, top,
):
    near[...] = coef2[...] + coef2_a[...]
    far[...] = coef2_b[...] + coef2_c[...]
    top[...] = near[...] + far[...]
    source3 = [a + b for a, b in zip(load2(left2), load2(left2_a))]
    source3_far = [a + b for a, b in zip(load2(left2_b), load2(left2_c))]
    level3, level3_far, level4 = coarse_level(near), coarse_level(far), coarse_level(top)
    below3 = level3.start(source3, 2)
    below3_far = level3_far.start(source3_far, 2)
    source4 = [
        a + b
        for a, b in zip(
            level3.misfit(below3, source3), level3_far.misfit(below3_far, source3_far)
        )
    ]
    v = level4.start(source4, 4)
    v = level3.smooth([a + b for a, b in zip(below3, v)], source3, 2)
    v = coarse_level(coef2).smooth([a + b for a, b in zip(load2(below2), v)], load2(source2), 2)
    v = coarse_level(coef1).smooth([a + b for a, b in zip(load2(below1), v)], load2(source1), 2)

    both = jnp.concatenate([v[0], v[1]], axis=1)
    both = jnp.concatenate([both, jnp.zeros((LANES - AGG, 2 * LANES), F32)], axis=0)
    lane = iota((LANES, LANES), 1)
    for t in range(NARROW // 8):
        mark = jnp.broadcast_to(marks[t : t + 1, :], (LANES, LANES))
        hot = as_bf16(jnp.transpose(mark, (1, 0)).astype(I32) == lane)
        rows = select_rows(hot, both)
        for s in range(8):
            for f in (0, 1):
                out[pl.ds((8 * t + s) * UNIT + f, CAP, stride=2), :] = rows[
                    s * CAP : (s + 1) * CAP, f * LANES : (f + 1) * LANES
                ]
    ends = select_rows(marks[8 : 8 + 2 * NARROW, :].astype(BF16), both)
    for f in (0, 1):
        part = ends[:, f * LANES : (f + 1) * LANES]
        out[pl.ds(2 * CAP + f, NARROW, stride=UNIT), :] = jnp.where(
            iota((NARROW, LANES), 1) >= LANES // 2, part[0:NARROW], part[NARROW:]
        )


def post_kernel(narrow, rhs, face, sink, kap, mask, slots, recv, own_edges, out):
    n = narrow[0]
    data, source = fine_inputs(rhs, face, sink, kap, mask)
    field = data.start(source, 2)
    slot = slots[...].astype(I32)
    lane = iota((BLK, LANES), 1)
    lifted = None
    for half in (0, 1):
        hots, parts = [], []
        for t in (2 * half, 2 * half + 1):
            hots.append(slot == lane + t * LANES)
            for s in range(8 * t, 8 * t + 8):
                parts.append(
                    jnp.concatenate(
                        [recv[pl.ds(s * UNIT + f, CAP, stride=2), :] for f in (0, 1)], axis=1
                    )
                )
        term = select_rows(as_bf16(jnp.concatenate(hots, axis=1)), jnp.concatenate(parts, axis=0))
        lifted = term if lifted is None else lifted + term
    lifted = [lifted[:, 0:LANES], lifted[:, LANES:]]
    v = data.smooth([a + b for a, b in zip(field, lifted)], source, 2)

    edge_data, edge_source = interface_level(own_edges[...])
    edge_field = edge_data.start(edge_source, 2)
    lane1 = iota((1, LANES), 1)
    row8 = iota((8, LANES), 0)
    edge_v = []
    for f in (0, 1):
        beyond = jnp.sum(recv[pl.ds(2 * CAP + f, NARROW, stride=UNIT), :], axis=0, keepdims=True)
        first = jnp.where(lane1 >= LANES // 2, beyond, lifted[f][0:1, :])
        final = jnp.where(lane1 >= LANES // 2, lifted[f][BLK - 1 : BLK, :], beyond)
        lift = jnp.where(row8 == 0, first, jnp.where(row8 == 1, final, 0.0))
        lift = jnp.where(iota((8, LANES), 1) < 16, pltpu.roll(lift, 8, 1), 0.0)
        edge_v.append(edge_field[f] + lift)
    edge_v = edge_data.smooth(edge_v, edge_source, 2)
    for f in (0, 1):
        out[pl.ds(f, BLK, stride=2), :] = v[f]
        moved = pltpu.roll(edge_v[f], LANES - 8, 1)
        out[f : f + 1, :] = jnp.where((lane1 < 4) & (n > 0), moved[0:1, :], v[f][0:1, :])
        final = 2 * (BLK - 1) + f
        out[final : final + 1, :] = jnp.where(
            (lane1 >= LANES - 4) & (n < NARROW - 1), moved[1:2, :], v[f][BLK - 1 : BLK, :]
        )


def call(kernel, outs, *args, smem=0, scratch=()):
    space = lambda k: pltpu.SMEM if k < smem else pltpu.VMEM
    return pl.pallas_call(
        kernel,
        out_shape=[jax.ShapeDtypeStruct(s, F32) for s in outs],
        in_specs=[pl.BlockSpec(memory_space=space(k)) for k in range(len(args))],
        out_specs=[pl.BlockSpec(memory_space=pltpu.VMEM) for _ in outs],
        scratch_shapes=[pltpu.VMEM(s, F32) for s in scratch],
        compiler_params=pltpu.CompilerParams(vmem_limit_bytes=32 * 1024 * 1024),
    )(*args)


def exchange(value, bits):
    return lax.ppermute(value, "wide", [(i, i ^ bits) for i in range(lax.axis_size("wide"))])


def to_all(units):
    shape = (NARROW * UNIT // 2, 2, LANES)
    moved = lax.all_to_all(units.reshape(shape), "narrow", 0, 0, tiled=True)
    return moved.reshape(NARROW * UNIT, LANES)


def on_device(
    rhs, fine_face, fine_sink, fine_kap, cell_mask, block_aggregate, coarse_face, coarse_sink, coarse_kap
):
    narrow = lax.axis_index("narrow").astype(I32).reshape(1)
    fine = (
        rhs.reshape(2 * BLK, LANES),
        fine_face.reshape(2 * BLK, LANES),
        fine_sink.reshape(2 * BLK, LANES),
        fine_kap,
        cell_mask,
    )
    five, two, units = (5 * AGG, LANES), (2 * AGG, LANES), (NARROW * UNIT, LANES)
    (coef1,) = call(
        coef_kernel,
        [five],
        coarse_face.reshape(2 * AGG, LANES),
        coarse_sink.reshape(2 * AGG, LANES),
        coarse_kap,
    )
    coef2 = coef1 + exchange(coef1, 1)
    coef2_x = [exchange(coef2, b) for b in (2, 4, 6)]

    sent, slots = call(
        pre_kernel,
        [units, (BLK, LANES)],
        narrow,
        *fine,
        block_aggregate.reshape(1, BLK),
        smem=1,
    )
    recv = to_all(sent)
    left1, below1, source1, marks, own_edges = call(
        restrict_kernel,
        [two, two, two, (8 + 2 * NARROW, LANES), (8, LANES)],
        narrow,
        recv,
        coef1,
        smem=1,
    )
    left2, below2, source2 = call(
        second_kernel, [two, two, two], left1, exchange(left1, 1), coef2
    )
    left2_x = [exchange(left2, b) for b in (2, 4, 6)]
    (back,) = call(
        top_kernel,
        [units],
        left2, *left2_x, coef2, *coef2_x, below2, source2, coef1, below1, source1, marks,
        scratch=(five, five, five),
    )
    recv = to_all(back)
    (out,) = call(
        post_kernel, [(2 * BLK, LANES)], narrow, *fine, slots, recv, own_edges, smem=1
    )
    return out.reshape(BLK, 2, LANES)


def solution(mesh):
    both = ("wide", "narrow")
    placed = (
        P(both, None, None),
        P(both, None, None),
        P(both, None, None),
        P(both, None),
        P(both, None),
        P(both),
        P(both, None, None),
        P(both, None, None),
        P(both, None),
    )
    return jax.shard_map(
        on_device,
        mesh=mesh,
        in_specs=placed,
        out_specs=P(both, None, None),
        check_vma=False,
    )
```

time: 434 us -> 75 us (0.17)
  waiting for transfers between devices: 320 us -> 19.1 us
  local copies, waits for them, and re-layouts: 28.5 us -> 5.38 us
  starting transfers between devices: 43.9 us -> 21.2 us
  blocking collectives: 0 us -> 21.9 us
  other arithmetic: 18.2 us -> 0.02 us
  between operations: 14.8 us -> 0.16 us
  Pallas kernels: 0 us -> 6.88 us
  matrix products: 6.28 us -> 0 us
    reduce_scatter x1 -> x0, waiting for transfers between devices: 217 us -> none  [on_device(): lax.psum_scatter(jnp.einsum('ba,bfc->afc', onehot, misfit, precision=lax....]
    all_gather x1 -> x0, waiting for transfers between devices: 75.3 us -> none  [on_device(): piece = lax.all_gather(correction, 'narrow', axis=0, tiled=True)]
    ppermute x22 -> x8, starting transfers between devices: 43.9 us -> 9.76 us  [exchange(): lax.ppermute(value, 'wide', [(i, i ^ bits) for i in range(lax.axis_size('...]
    all_to_all x0 -> x1, blocking collectives: none -> 21.9 us  [to_all(): moved = lax.all_to_all(units.reshape(shape), 'narrow', 0, 0, tiled=True)]
    ppermute x22 -> x8, waiting for transfers between devices: 27.2 us -> 7.62 us  [exchange(): lax.ppermute(value, 'wide', [(i, i ^ bits) for i in range(lax.axis_size('...]
    slice x73 -> x0, local copies, waits for them, and re-layouts: 13.3 us -> none  [the longest x20 3.31 us: next_cells(): return jnp.concatenate([field[..., 1:], carried[..., None]], axis=-1)]
    all_to_all x0 -> x1, starting transfers between devices: none -> 11.5 us  [to_all(): moved = lax.all_to_all(units.reshape(shape), 'narrow', 0, 0, tiled=True)]
    all_to_all x0 -> x1, waiting for transfers between devices: none -> 11.5 us  [to_all(): moved = lax.all_to_all(units.reshape(shape), 'narrow', 0, 0, tiled=True)]
  transfers between devices with their start and end apart: 24 -> 9, of which waited for: 12 -> 5; matrix products, arithmetic and copies ran while one was open for 3% -> 0% of each run, Pallas kernels for 0% -> 2%
where the time goes in v1:
time: 75 us; the launch traced here: 74.6 us
  blocking collectives  21.9 us (29%)
  starting transfers between devices  21.2 us (28%)
  waiting for transfers between devices  19.1 us (25%)
  Pallas kernels  6.88 us (9%)
  local copies, waits for them, and re-layouts  5.38 us (7%)
    all_to_all x1, blocking collectives, to_all(): moved = lax.all_to_all(units.reshape(shape), 'narrow', 0, 0, tiled=True)  21.9 us
    all_to_all x1, starting transfers between devices, to_all(): moved = lax.all_to_all(units.reshape(shape), 'narrow', 0, 0, tiled=True)  11.5 us
    all_to_all x1, waiting for transfers between devices, to_all(): moved = lax.all_to_all(units.reshape(shape), 'narrow', 0, 0, tiled=True)  11.5 us
    ppermute x8, starting transfers between devices, exchange(): lax.ppermute(value, 'wide', [(i, i ^ bits) for i in range(lax.axis_size('...  9.76 us
    ppermute x8, waiting for transfers between devices, exchange(): lax.ppermute(value, 'wide', [(i, i ^ bits) for i in range(lax.axis_size('...  7.62 us
    pallas_call x6, Pallas kernels, call(): pl.pallas_call(kernel, out_shape=[jax.ShapeDtypeStruct(s, F32) for s in o...  6.88 us
    unnamed x28, local copies, waits for them, and re-layouts  5.38 us
  transfers between devices with their start and end apart: 9, of which 5 were waited for; matrix products, arithmetic and copies ran while one was open for 0% of the time, Pallas kernels for 2%

profile of v1, /device:TPU:32, one launch (start us, length us, event | category | flops | bytes accessed | tf_op | source)
XLA Modules:
  0.0 74.6 jit_solution(491529933784789958)
XLA Ops:
  0.0 0.7 copy-done.13
  0.7 0.9 %copy-done = f32[256,2,128]{2,1,0:T(2,128)S(1)} copy-done((f32[256,2,128]{2,1,0:T(2,128)S(1)}, f32[256,2,128]{2,1,0:T(2,128)}, u32[]{:S(2)}) %copy-start) | copy-done | bytes 262168
  1.6 0.9 %copy-done.2 = f32[256,2,128]{2,1,0:T(2,128)S(1)} copy-done((f32[256,2,128]{2,1,0:T(2,128)S(1)}, f32[256,2,128]{2,1,0:T(2,128)}, u32[]{:S(2)}) %copy-start.2) | copy-done | bytes 262168
  2.6 0.9 %copy-done.4 = f32[256,2,128]{2,1,0:T(2,128)S(1)} copy-done((f32[256,2,128]{2,1,0:T(2,128)S(1)}, f32[256,2,128]{2,1,0:T(2,128)}, u32[]{:S(2)}) %copy-start.4) | copy-done | bytes 262168
  3.5 0.9 %copy-done.6 = f32[256,128]{1,0:T(8,128)S(1)} copy-done((f32[256,128]{1,0:T(8,128)S(1)}, f32[256,128]{1,0:T(8,128)}, u32[]{:S(2)}) %copy-start.6) | copy-done | bytes 131096
  4.4 0.9 %copy-done.8 = s32[256,128]{1,0:T(8,128)S(1)} copy-done((s32[256,128]{1,0:T(8,128)S(1)}, s32[256,128]{1,0:T(8,128)}, u32[]{:S(2)}) %copy-start.8) | copy-done | bytes 131096
  5.3 1.8 %shard_map.91 = (f32[1088,128]{1,0:T(8,128)}, f32[256,128]{1,0:T(8,128)S(1)}) custom-call(s32[1]{0:T(128)} %bitcast.narrow, f32[512,128]{1,0:T(8,128)S(1)} %bitcast.15, f32[512,128]{1,0:T(8,128)S(1)} %bitcast.17, f32[512,128]{1,0:T(8,128)S(1)} %bitcast.19, f32[256,128]{1,0:T(8,128)S(1)} %copy-done.6, s32[256,128]{1,0:T(8,128)S(1)} %copy-done.8, ...), custom_call_target="tpu_custom_call" | custom-call | tf_op jit(solution)/shard_map/pallas_call | solution.py:382
  7.2 11.5 %all-to-all-start = ((f32[544,2,128]{2,1,0:T(2,128)}), f32[544,2,128]{2,1,0:T(2,128)S(1)}, u32[]{:S(2)}, u32[]{:S(2)}) async-start(f32[544,2,128]{2,1,0:T(2,128)} %bitcast.5), calls=%async_computation | async-start | bytes 1114112 | tf_op jit(solution)/shard_map/all_to_all | solution.py:398
  18.9 1.4 %collective-permute-done.1 = f32[320,128]{1,0:T(8,128)S(1)} collective-permute-done((f32[320,128]{1,0:T(8,128)S(1)}, f32[320,128]{1,0:T(8,128)S(1)}, u32[]{:S(2)}, u32[]{:S(2)}) %collective-permute-start.1) | collective-permute-done | bytes 163872 | tf_op jit(solution)/shard_map/ppermute | solution.py:393
  20.3 1.6 %collective-permute-start.5 = (f32[320,128]{1,0:T(8,128)S(1)}, f32[320,128]{1,0:T(8,128)S(1)}, u32[]{:S(2)}, u32[]{:S(2)}) collective-permute-start(f32[320,128]{1,0:T(8,128)S(1)} %add.3.coef.coef2), channel_id=1, source_target_pairs={{0,64},{32,96},{64,0},{96,32},{128,192},{160,224},{192,128},{224,1... | collective-permute-start | bytes 491528 | tf_op jit(solution)/shard_map/ppermute | solution.py:393
  21.8 2.7 %collective-permute-start.6 = (f32[320,128]{1,0:T(8,128)S(1)}, f32[320,128]{1,0:T(8,128)S(1)}, u32[]{:S(2)}, u32[]{:S(2)}) collective-permute-start(f32[320,128]{1,0:T(8,128)S(1)} %add.3.coef.coef2), channel_id=1, source_target_pairs={{0,128},{32,160},{64,192},{96,224},{128,0},{160,32},{192,64},{224,... | collective-permute-start | bytes 491528 | tf_op jit(solution)/shard_map/ppermute | solution.py:393
  24.6 0.5 collective-permute-start.7
  25.0 11.5 %all-to-all-done = f32[544,2,128]{2,1,0:T(2,128)S(1)} async-done(((f32[544,2,128]{2,1,0:T(2,128)}), f32[544,2,128]{2,1,0:T(2,128)S(1)}, u32[]{:S(2)}, u32[]{:S(2)}) %all-to-all-start) | async-done | bytes 557088 | tf_op jit(solution)/shard_map/all_to_all | solution.py:398
  36.5 1.0 %shard_map.93 = (f32[128,128]{1,0:T(8,128)S(1)}, f32[128,128]{1,0:T(8,128)S(1)}, f32[128,128]{1,0:T(8,128)S(1)}, f32[72,128]{1,0:T(8,128)S(1)}, f32[8,128]{1,0:T(8,128)S(1)}) custom-call(s32[1]{0:T(128)} %bitcast.narrow, f32[1088,128]{1,0:T(8,128)S(1)} %bitcast.12, f32[320,128]{1,0:T(8,128)S(1)} %shard_map.92.coef.coef1), custom_call_target="tpu_custom_call" | custom-call | tf_op jit(solution)/shard_map/pallas_call | solution.py:382
  37.6 1.2 %collective-permute-done.other = f32[128,128]{1,0:T(8,128)S(1)} collective-permute-done((f32[128,128]{1,0:T(8,128)S(1)}, f32[128,128]{1,0:T(8,128)S(1)}, u32[]{:S(2)}, u32[]{:S(2)}) %collective-permute-start) | collective-permute-done | bytes 65568 | tf_op jit(solution)/shard_map/ppermute | solution.py:393
  38.9 0.3 shard_map.94
  39.2 1.6 %collective-permute-start.2 = (f32[128,128]{1,0:T(8,128)S(1)}, f32[128,128]{1,0:T(8,128)S(1)}, u32[]{:S(2)}, u32[]{:S(2)}) collective-permute-start(f32[128,128]{1,0:T(8,128)S(1)} %get-tuple-element.18.left2), channel_id=1, source_target_pairs={{0,64},{32,96},{64,0},{96,32},{128,192},{160,224},{192,128},{224,1... | collective-permute-start | bytes 196616 | tf_op jit(solution)/shard_map/ppermute | solution.py:393
  40.8 2.7 %collective-permute-start.3 = (f32[128,128]{1,0:T(8,128)S(1)}, f32[128,128]{1,0:T(8,128)S(1)}, u32[]{:S(2)}, u32[]{:S(2)}) collective-permute-start(f32[128,128]{1,0:T(8,128)S(1)} %get-tuple-element.18.left2), channel_id=1, source_target_pairs={{0,128},{32,160},{64,192},{96,224},{128,0},{160,32},{192,64},{224,... | collective-permute-start | bytes 196616 | tf_op jit(solution)/shard_map/ppermute | solution.py:393
  43.5 0.5 collective-permute-start.4
  44.0 3.0 %collective-permute-done.3.left2_b = f32[128,128]{1,0:T(8,128)S(1)} collective-permute-done((f32[128,128]{1,0:T(8,128)S(1)}, f32[128,128]{1,0:T(8,128)S(1)}, u32[]{:S(2)}, u32[]{:S(2)}) %collective-permute-start.3) | collective-permute-done | bytes 65568 | tf_op jit(solution)/shard_map/ppermute | solution.py:393
  47.0 1.9 %collective-permute-done.4.left2_c = f32[128,128]{1,0:T(8,128)S(1)} collective-permute-done((f32[128,128]{1,0:T(8,128)S(1)}, f32[128,128]{1,0:T(8,128)S(1)}, u32[]{:S(2)}, u32[]{:S(2)}) %collective-permute-start.4) | collective-permute-done | bytes 65568 | tf_op jit(solution)/shard_map/ppermute | solution.py:393
  49.0 1.8 %shard_map.95 = f32[1088,128]{1,0:T(8,128)S(1)} custom-call(f32[128,128]{1,0:T(8,128)S(1)} %get-tuple-element.18.left2, f32[128,128]{1,0:T(8,128)S(1)} %collective-permute-done.2.left2_a, f32[128,128]{1,0:T(8,128)S(1)} %collective-permute-done.3.left2_b, f32[128,128]{1,0:T(8,128)S(1)} %collective-permute-done.4.left2_c, f32[320,128]{1,0:T(8,128)S(1)} %add.3.coef.coef2, ...), custom_call_target="tpu_custom_call" | custom-call | tf_op jit(solution)/shard_map/pallas_call | solution.py:382
  50.8 21.9 %all_to_all.10 = f32[544,2,128]{2,1,0:T(2,128)S(1)} all-to-all(f32[544,2,128]{2,1,0:T(2,128)S(1)} %bitcast.13), channel_id=1, replica_groups=mesh['wide'=8,'narrow'=32] {'narrow'}, dimensions={0} | all-to-all | bytes 1114112 | tf_op jit(solution)/shard_map/all_to_all | solution.py:398
  72.7 2.0 %shard_map.96 = f32[512,128]{1,0:T(8,128)} custom-call(s32[1]{0:T(128)} %bitcast.narrow, f32[512,128]{1,0:T(8,128)S(1)} %bitcast.16, f32[512,128]{1,0:T(8,128)S(1)} %bitcast.18, f32[512,128]{1,0:T(8,128)S(1)} %bitcast.20, f32[256,128]{1,0:T(8,128)S(1)} %copy-done.7, s32[256,128]{1,0:T(8,128)S(1)} %copy-done.9, f32[256,128]{1,0:T(8,128)S(1)} %get-tuple-element.15.slots, ...), custom_call_target="tpu_custom_call" | custom-call | tf_op jit(solution)/shard_map/pallas_call | solution.py:382
  (30 shorter events, 0.3 us)
Async XLA Ops:
  0.0 0.7 copy-start.13
  0.7 0.9 %copy-start = (f32[256,2,128]{2,1,0:T(2,128)S(1)}, f32[256,2,128]{2,1,0:T(2,128)}, u32[]{:S(2)}) copy-start(f32[256,2,128]{2,1,0:T(2,128)} %param.9) | copy-start | bytes 786436
  1.6 0.9 %copy-start.2 = (f32[256,2,128]{2,1,0:T(2,128)S(1)}, f32[256,2,128]{2,1,0:T(2,128)}, u32[]{:S(2)}) copy-start(f32[256,2,128]{2,1,0:T(2,128)} %param.10) | copy-start | bytes 786436
  2.6 0.9 %copy-start.4 = (f32[256,2,128]{2,1,0:T(2,128)S(1)}, f32[256,2,128]{2,1,0:T(2,128)}, u32[]{:S(2)}) copy-start(f32[256,2,128]{2,1,0:T(2,128)} %param.11) | copy-start | bytes 786436
  3.5 0.9 %copy-start.6 = (f32[256,128]{1,0:T(8,128)S(1)}, f32[256,128]{1,0:T(8,128)}, u32[]{:S(2)}) copy-start(f32[256,128]{1,0:T(8,128)} %kap.5) | copy-start | bytes 393220
  4.4 0.9 %copy-start.8 = (s32[256,128]{1,0:T(8,128)S(1)}, s32[256,128]{1,0:T(8,128)}, u32[]{:S(2)}) copy-start(s32[256,128]{1,0:T(8,128)} %mask.3) | copy-start | bytes 393220
  7.2 11.5 %copy-start.10 = (f32[64,2,128]{2,1,0:T(2,128)S(1)}, f32[64,2,128]{2,1,0:T(2,128)}, u32[]{:S(2)}) copy-start(f32[64,2,128]{2,1,0:T(2,128)} %param.15) | copy-start | bytes 196612
  7.2 11.5 %copy-start.11 = (f32[64,2,128]{2,1,0:T(2,128)S(1)}, f32[64,2,128]{2,1,0:T(2,128)}, u32[]{:S(2)}) copy-start(f32[64,2,128]{2,1,0:T(2,128)} %param.16) | copy-start | bytes 196612
  7.2 11.5 %copy-start.12 = (f32[64,128]{1,0:T(8,128)S(1)}, f32[64,128]{1,0:T(8,128)}, u32[]{:S(2)}) copy-start(f32[64,128]{1,0:T(8,128)} %kap.4) | copy-start | bytes 98308
  7.2 29.3 %all-to-all-start = ((f32[544,2,128]{2,1,0:T(2,128)}), f32[544,2,128]{2,1,0:T(2,128)S(1)}, u32[]{:S(2)}, u32[]{:S(2)}) async-start(f32[544,2,128]{2,1,0:T(2,128)} %bitcast.5), calls=%async_computation | async-start | bytes 1114112 | tf_op jit(solution)/shard_map/all_to_all | solution.py:398
  18.8 1.5 %collective-permute-start.1 = (f32[320,128]{1,0:T(8,128)S(1)}, f32[320,128]{1,0:T(8,128)S(1)}, u32[]{:S(2)}, u32[]{:S(2)}) collective-permute-start(f32[320,128]{1,0:T(8,128)S(1)} %shard_map.92.coef.coef1), channel_id=1, source_target_pairs={{0,32},{32,0},{64,96},{96,64},{128,160},{160,128},{192,224},{224,1... | collective-permute-start | bytes 491528 | tf_op jit(solution)/shard_map/ppermute | solution.py:393
  20.3 23.2 %collective-permute-start.5 = (f32[320,128]{1,0:T(8,128)S(1)}, f32[320,128]{1,0:T(8,128)S(1)}, u32[]{:S(2)}, u32[]{:S(2)}) collective-permute-start(f32[320,128]{1,0:T(8,128)S(1)} %add.3.coef.coef2), channel_id=1, source_target_pairs={{0,64},{32,96},{64,0},{96,32},{128,192},{160,224},{192,128},{224,1... | collective-permute-start | bytes 491528 | tf_op jit(solution)/shard_map/ppermute | solution.py:393
  21.8 22.1 %collective-permute-start.6 = (f32[320,128]{1,0:T(8,128)S(1)}, f32[320,128]{1,0:T(8,128)S(1)}, u32[]{:S(2)}, u32[]{:S(2)}) collective-permute-start(f32[320,128]{1,0:T(8,128)S(1)} %add.3.coef.coef2), channel_id=1, source_target_pairs={{0,128},{32,160},{64,192},{96,224},{128,0},{160,32},{192,64},{224,... | collective-permute-start | bytes 491528 | tf_op jit(solution)/shard_map/ppermute | solution.py:393
  24.6 19.4 %collective-permute-start.7 = (f32[320,128]{1,0:T(8,128)S(1)}, f32[320,128]{1,0:T(8,128)S(1)}, u32[]{:S(2)}, u32[]{:S(2)}) collective-permute-start(f32[320,128]{1,0:T(8,128)S(1)} %add.3.coef.coef2), channel_id=1, source_target_pairs={{0,192},{32,224},{64,128},{96,160},{128,64},{160,96},{192,0},{224,... | collective-permute-start | bytes 491528 | tf_op jit(solution)/shard_map/ppermute | solution.py:393
  37.5 1.3 %collective-permute-start = (f32[128,128]{1,0:T(8,128)S(1)}, f32[128,128]{1,0:T(8,128)S(1)}, u32[]{:S(2)}, u32[]{:S(2)}) collective-permute-start(f32[128,128]{1,0:T(8,128)S(1)} %get-tuple-element.17.mine), channel_id=1, source_target_pairs={{0,32},{32,0},{64,96},{96,64},{128,160},{160,128},{192,224},{224,1... | collective-permute-start | bytes 196616 | tf_op jit(solution)/shard_map/ppermute | solution.py:393
  39.2 4.8 %collective-permute-start.2 = (f32[128,128]{1,0:T(8,128)S(1)}, f32[128,128]{1,0:T(8,128)S(1)}, u32[]{:S(2)}, u32[]{:S(2)}) collective-permute-start(f32[128,128]{1,0:T(8,128)S(1)} %get-tuple-element.18.left2), channel_id=1, source_target_pairs={{0,64},{32,96},{64,0},{96,32},{128,192},{160,224},{192,128},{224,1... | collective-permute-start | bytes 196616 | tf_op jit(solution)/shard_map/ppermute | solution.py:393
  40.8 6.3 %collective-permute-start.3 = (f32[128,128]{1,0:T(8,128)S(1)}, f32[128,128]{1,0:T(8,128)S(1)}, u32[]{:S(2)}, u32[]{:S(2)}) collective-permute-start(f32[128,128]{1,0:T(8,128)S(1)} %get-tuple-element.18.left2), channel_id=1, source_target_pairs={{0,128},{32,160},{64,192},{96,224},{128,0},{160,32},{192,64},{224,... | collective-permute-start | bytes 196616 | tf_op jit(solution)/shard_map/ppermute | solution.py:393
  43.5 5.5 %collective-permute-start.4 = (f32[128,128]{1,0:T(8,128)S(1)}, f32[128,128]{1,0:T(8,128)S(1)}, u32[]{:S(2)}, u32[]{:S(2)}) collective-permute-start(f32[128,128]{1,0:T(8,128)S(1)} %get-tuple-element.18.left2), channel_id=1, source_target_pairs={{0,192},{32,224},{64,128},{96,160},{128,64},{160,96},{192,0},{224,... | collective-permute-start | bytes 196616 | tf_op jit(solution)/shard_map/ppermute | solution.py:393
  50.7 21.9 %copy-start.1 = (f32[256,2,128]{2,1,0:T(2,128)S(1)}, f32[256,2,128]{2,1,0:T(2,128)}, u32[]{:S(2)}) copy-start(f32[256,2,128]{2,1,0:T(2,128)} %param.9) | copy-start | bytes 786436
  50.7 21.9 %copy-start.3 = (f32[256,2,128]{2,1,0:T(2,128)S(1)}, f32[256,2,128]{2,1,0:T(2,128)}, u32[]{:S(2)}) copy-start(f32[256,2,128]{2,1,0:T(2,128)} %param.10) | copy-start | bytes 786436
  50.8 21.9 %copy-start.5 = (f32[256,2,128]{2,1,0:T(2,128)S(1)}, f32[256,2,128]{2,1,0:T(2,128)}, u32[]{:S(2)}) copy-start(f32[256,2,128]{2,1,0:T(2,128)} %param.11) | copy-start | bytes 786436
  50.8 21.9 %copy-start.7 = (f32[256,128]{1,0:T(8,128)S(1)}, f32[256,128]{1,0:T(8,128)}, u32[]{:S(2)}) copy-start(f32[256,128]{1,0:T(8,128)} %kap.5) | copy-start | bytes 393220
  50.8 21.9 %copy-start.9 = (s32[256,128]{1,0:T(8,128)S(1)}, s32[256,128]{1,0:T(8,128)}, u32[]{:S(2)}) copy-start(s32[256,128]{1,0:T(8,128)} %mask.3) | copy-start | bytes 393220

commit v2 on v1

--- a/solution.py
+++ b/solution.py
@@ -48,6 +48,17 @@
         self.coupling = coupling
         scale = OMEGA / (self.diag[0] * self.diag[1] - coupling * coupling)
         self.inv = (self.diag[1] * scale, self.diag[0] * scale, coupling * scale)
+
+    def parts(self):
+        return [*self.faces, *self.left, *self.diag, self.coupling, *self.inv]
+
+    @classmethod
+    def load(cls, part, prev, nxt):
+        level = cls.__new__(cls)
+        level.prev, level.nxt = prev, nxt
+        level.faces, level.left, level.diag = part[0:2], part[2:4], part[4:6]
+        level.coupling, level.inv = part[6], part[7:10]
+        return level
 
     def misfit(self, v, source):
         return [
@@ -85,6 +96,16 @@
     return Level(faces, sink, coupling, prev, nxt)
 
 
+def store(ref, parts, at=0):
+    for part in parts:
+        ref[at : at + part.shape[0], :] = part
+        at += part.shape[0]
+
+
+def load(ref, count, rows, at=0):
+    return [ref[at + k * rows : at + (k + 1) * rows, :] for k in range(count)]
+
+
 def last_cell(shape):
     return (iota(shape, 0) == shape[0] - 1) & (iota(shape, 1) == LANES - 1)
 
@@ -112,26 +133,38 @@
     return [ref[pl.ds(f, rows, stride=2), :] for f in (0, 1)]
 
 
-def fine_inputs(rhs, face, sink, kap, mask):
+def start_copies(sources, targets, sems):
+    copies = [
+        pltpu.make_async_copy(a, b, sems.at[k]) for k, (a, b) in enumerate(zip(sources, targets))
+    ]
+    for copy in copies:
+        copy.start()
+    return copies
+
+
+def fine_start(rhs, face, sink, kap, mask):
     live = mask[...].astype(F32)
-    shape = (BLK, LANES)
     data = fine_level(
-        planar(face, BLK), planar(sink, BLK), kap[...], live, chain_prev, chain_next, last_cell(shape)
+        planar(face, BLK), planar(sink, BLK), kap[...], live, chain_prev, chain_next, last_cell((BLK, LANES))
     )
     source = [r * live for r in planar(rhs, BLK)]
-    return data, source
-
-
-def pre_kernel(narrow, rhs, face, sink, kap, mask, agg, out, slots):
+    return data, source, data.start(source, 2)
+
+
+def ready_kernel(token, *refs):
+    inputs, fine, held, sems = refs[0:5], refs[5], refs[6:11], refs[11]
+    for copy in start_copies(inputs, held, sems):
+        copy.wait()
+    data, source, field = fine_start(*held)
+    store(fine, [*field, *source, *data.parts()])
+
+
+def pre_kernel(narrow, agg_hbm, *refs):
+    inputs, out, slots, held, sems = refs[0:5], refs[5], refs[6], refs[7:13], refs[13]
+    rhs, face, sink, kap, mask, agg = held
     n = narrow[0]
-    data, source = fine_inputs(rhs, face, sink, kap, mask)
-    field = data.start(source, 2)
-    misfit = data.misfit(field, source)
-    row, lane = iota((BLK, LANES), 0), iota((BLK, LANES), 1)
-    drop = ((row == BLK - 1) & (lane >= LANES - 3) & (n < NARROW - 1)) | (
-        (row == 0) & (lane < 3) & (n > 0)
-    )
-    misfit = jnp.concatenate([jnp.where(drop, 0.0, m) for m in misfit], axis=1)
+    copies = start_copies((*inputs, agg_hbm), held, sems)
+    copies.pop().wait()
 
     label = agg[...]
     owner = label // AGG
@@ -142,21 +175,33 @@
     rank = jnp.sum(jnp.where(owned, counts, 0.0), axis=0, keepdims=True).astype(I32)
     slot = owner * CAP + rank
     put = as_bf16(iota((NARROW * CAP, BLK), 0) == slot)
+
+    block = iota((1, BLK), 1)
+    code = within + 1 + jnp.where(block == 0, 64, 0) + jnp.where(block == BLK - 1, 128, 0)
+    coded = jnp.where(owned, code.astype(F32), 0.0).astype(BF16)
+    at_rank = as_bf16(iota((LANES, BLK), 0) % CAP == rank)
+    labels = lax.dot_general(
+        coded, at_rank, (((1,), (1,)), ((), ())), preferred_element_type=F32
+    )
+    out[pl.ds(2 * CAP, NARROW, stride=UNIT), :] = labels
+    slots[...] = jnp.transpose(jnp.broadcast_to(slot.astype(F32), (LANES, BLK)), (1, 0))
+
+    for copy in copies:
+        copy.wait()
+    data, source, field = fine_start(rhs, face, sink, kap, mask)
+    misfit = data.misfit(field, source)
+    row, lane = iota((BLK, LANES), 0), iota((BLK, LANES), 1)
+    drop = ((row == BLK - 1) & (lane >= LANES - 3) & (n < NARROW - 1)) | (
+        (row == 0) & (lane < 3) & (n > 0)
+    )
+    misfit = jnp.concatenate([jnp.where(drop, 0.0, m) for m in misfit], axis=1)
+
     rows = select_rows(put, misfit)
     for o in range(NARROW):
         for f in (0, 1):
             out[pl.ds(o * UNIT + f, CAP, stride=2), :] = rows[
                 o * CAP : (o + 1) * CAP, f * LANES : (f + 1) * LANES
             ]
-
-    block = iota((1, BLK), 1)
-    code = within + 1 + jnp.where(block == 0, 64, 0) + jnp.where(block == BLK - 1, 128, 0)
-    coded = jnp.where(owned, code.astype(F32), 0.0).astype(BF16)
-    at_rank = as_bf16(iota((LANES, BLK), 0) % CAP == rank)
-    labels = lax.dot_general(
-        coded, at_rank, (((1,), (1,)), ((), ())), preferred_element_type=F32
-    )
-    out[pl.ds(2 * CAP, NARROW, stride=UNIT), :] = labels
 
     lane1 = iota((1, LANES), 1)
     edges = jnp.zeros((1, LANES), F32)
@@ -171,8 +216,6 @@
         edges = jnp.where(lane1 // 16 == q, moved, edges)
     out[pl.ds(2 * CAP + 1, NARROW, stride=UNIT), :] = jnp.broadcast_to(edges, (NARROW, LANES))
 
-    slots[...] = jnp.transpose(jnp.broadcast_to(slot.astype(F32), (LANES, BLK)), (1, 0))
-
 
 def interface_level(cells):
     lane = iota(cells.shape, 1)
@@ -190,9 +233,16 @@
     return data, source
 
 
+PARTS = 10
+
+
 def coarse_level(ref):
-    part = [ref[k * AGG : (k + 1) * AGG, :] for k in range(5)]
+    part = load(ref, 5, AGG)
     return Level(part[0:2], part[2:4], part[4], chain_prev, chain_next)
+
+
+def ready_level(ref, at=0):
+    return Level.load(load(ref, PARTS, AGG, at * PARTS * AGG), chain_prev, chain_next)
 
 
 def store2(ref, v):
@@ -204,16 +254,32 @@
     return [ref[0:AGG, :], ref[AGG : 2 * AGG, :]]
 
 
-def coef_kernel(face, sink, kap, out):
+def coef_kernel(token, face_hbm, sink_hbm, kap_hbm, out, level, face, sink, kap, sems):
+    for copy in start_copies((face_hbm, sink_hbm, kap_hbm), (face, sink, kap), sems):
+        copy.wait()
     faces, sinks = planar(face, AGG), planar(sink, AGG)
     last = last_cell((AGG, LANES))
     for f in (0, 1):
         out[f * AGG : (f + 1) * AGG, :] = jnp.where(last, 0.0, faces[f])
         out[(2 + f) * AGG : (3 + f) * AGG, :] = sinks[f]
     out[4 * AGG : 5 * AGG, :] = kap[...] * jnp.sqrt(sinks[0] * sinks[1])
-
-
-def restrict_kernel(narrow, recv, coef, leftover, below, source_out, marks, own_edges):
+    store(level, coarse_level(out).parts())
+
+
+def pair_kernel(mine, other, out, level):
+    out[...] = mine[...] + other[...]
+    store(level, coarse_level(out).parts())
+
+
+def upper_kernel(coef2, coef2_a, coef2_b, coef2_c, levels, near, far, top):
+    near[...] = coef2[...] + coef2_a[...]
+    far[...] = coef2_b[...] + coef2_c[...]
+    top[...] = near[...] + far[...]
+    for k, ref in enumerate((near, far, top)):
+        store(levels, coarse_level(ref).parts(), k * PARTS * AGG)
+
+
+def restrict_kernel(narrow, recv, level1, token, leftover, below, source_out, marks, own_edges):
     n = narrow[0]
     lane = iota((NARROW, LANES), 1)
     src = iota((NARROW, LANES), 0)
@@ -265,7 +331,7 @@
             as_bf16(jnp.concatenate(hots, axis=1)), jnp.concatenate(parts, axis=0)
         )
     source_c = [total[:, 0:LANES], total[:, LANES:]]
-    level = coarse_level(coef)
+    level = ready_level(level1)
     correction = level.start(source_c, 2)
     store2(leftover, level.misfit(correction, source_c))
     store2(below, correction)
@@ -279,26 +345,38 @@
     own_edges[1:2, :] = jnp.sum(jnp.where(src == n, cells, 0.0), axis=0, keepdims=True)
 
 
-def second_kernel(mine, other, coef, leftover, below, source_out):
+def second_kernel(mine, other, level2, leftover, below, source_out):
     source = [a + b for a, b in zip(load2(mine), load2(other))]
-    level = coarse_level(coef)
+    level = ready_level(level2)
     correction = level.start(source, 2)
     store2(leftover, level.misfit(correction, source))
     store2(below, correction)
     store2(source_out, source)
 
 
+def side_kernel(marks, own_edges, hot, edges):
+    lane = iota((LANES, LANES), 1)
+    for t in range(NARROW // 8):
+        mark = jnp.broadcast_to(marks[t : t + 1, :], (LANES, LANES))
+        mark = jnp.transpose(mark, (1, 0)).astype(I32)
+        once = as_bf16(mark == lane % AGG)
+        last = as_bf16((mark == lane) & (lane < AGG))
+        hot[t * LANES : (t + 1) * LANES, 0:LANES] = once
+        hot[t * LANES : (t + 1) * LANES, LANES:] = last
+    ends = marks[8 : 8 + 2 * NARROW, :]
+    hot[NARROW * CAP :, 0:LANES] = (ends + pltpu.roll(ends, AGG, 1)).astype(BF16)
+    hot[NARROW * CAP :, LANES:] = ends.astype(BF16)
+    data, source = interface_level(own_edges[...])
+    field = data.start(source, 2)
+    store(edges, [*field, *source, *data.parts()])
+
+
 def top_kernel(
-    left2, left2_a, left2_b, left2_c,
-    coef2, coef2_a, coef2_b, coef2_c,
-    below2, source2, coef1, below1, source1, marks, out, near, far, top,
+    left2, left2_a, left2_b, left2_c, levels, level2, below2, source2, level1, below1, source1, hot, out
 ):
-    near[...] = coef2[...] + coef2_a[...]
-    far[...] = coef2_b[...] + coef2_c[...]
-    top[...] = near[...] + far[...]
     source3 = [a + b for a, b in zip(load2(left2), load2(left2_a))]
     source3_far = [a + b for a, b in zip(load2(left2_b), load2(left2_c))]
-    level3, level3_far, level4 = coarse_level(near), coarse_level(far), coarse_level(top)
+    level3, level3_far, level4 = [ready_level(levels, k) for k in range(3)]
     below3 = level3.start(source3, 2)
     below3_far = level3_far.start(source3_far, 2)
     source4 = [
@@ -309,22 +387,18 @@
     ]
     v = level4.start(source4, 4)
     v = level3.smooth([a + b for a, b in zip(below3, v)], source3, 2)
-    v = coarse_level(coef2).smooth([a + b for a, b in zip(load2(below2), v)], load2(source2), 2)
-    v = coarse_level(coef1).smooth([a + b for a, b in zip(load2(below1), v)], load2(source1), 2)
+    v = ready_level(level2).smooth([a + b for a, b in zip(load2(below2), v)], load2(source2), 2)
+    v = ready_level(level1).smooth([a + b for a, b in zip(load2(below1), v)], load2(source1), 2)
 
     both = jnp.concatenate([v[0], v[1]], axis=1)
-    both = jnp.concatenate([both, jnp.zeros((LANES - AGG, 2 * LANES), F32)], axis=0)
-    lane = iota((LANES, LANES), 1)
-    for t in range(NARROW // 8):
-        mark = jnp.broadcast_to(marks[t : t + 1, :], (LANES, LANES))
-        hot = as_bf16(jnp.transpose(mark, (1, 0)).astype(I32) == lane)
-        rows = select_rows(hot, both)
-        for s in range(8):
-            for f in (0, 1):
-                out[pl.ds((8 * t + s) * UNIT + f, CAP, stride=2), :] = rows[
-                    s * CAP : (s + 1) * CAP, f * LANES : (f + 1) * LANES
-                ]
-    ends = select_rows(marks[8 : 8 + 2 * NARROW, :].astype(BF16), both)
+    both = jnp.concatenate([*split3(both), jnp.zeros((AGG, 2 * LANES), BF16)], axis=0)
+    rows = jnp.dot(hot[...], both, preferred_element_type=F32)
+    for s in range(NARROW):
+        for f in (0, 1):
+            out[pl.ds(s * UNIT + f, CAP, stride=2), :] = rows[
+                s * CAP : (s + 1) * CAP, f * LANES : (f + 1) * LANES
+            ]
+    ends = rows[NARROW * CAP :, :]
     for f in (0, 1):
         part = ends[:, f * LANES : (f + 1) * LANES]
         out[pl.ds(2 * CAP + f, NARROW, stride=UNIT), :] = jnp.where(
@@ -332,10 +406,10 @@
         )
 
 
-def post_kernel(narrow, rhs, face, sink, kap, mask, slots, recv, own_edges, out):
+def post_kernel(narrow, fine, slots, recv, edges, out):
     n = narrow[0]
-    data, source = fine_inputs(rhs, face, sink, kap, mask)
-    field = data.start(source, 2)
+    field, source = load(fine, 2, BLK), load(fine, 2, BLK, 2 * BLK)
+    data = Level.load(load(fine, PARTS, BLK, 4 * BLK), chain_prev, chain_next)
     slot = slots[...].astype(I32)
     lane = iota((BLK, LANES), 1)
     lifted = None
@@ -354,8 +428,8 @@
     lifted = [lifted[:, 0:LANES], lifted[:, LANES:]]
     v = data.smooth([a + b for a, b in zip(field, lifted)], source, 2)
 
-    edge_data, edge_source = interface_level(own_edges[...])
-    edge_field = edge_data.start(edge_source, 2)
+    edge_field, edge_source = load(edges, 2, 8), load(edges, 2, 8, 16)
+    edge_data = Level.load(load(edges, PARTS, 8, 32), row_prev, row_next)
     lane1 = iota((1, LANES), 1)
     row8 = iota((8, LANES), 0)
     edge_v = []
@@ -377,14 +451,19 @@
         )
 
 
-def call(kernel, outs, *args, smem=0, scratch=()):
-    space = lambda k: pltpu.SMEM if k < smem else pltpu.VMEM
+def call(kernel, outs, *args, spaces=(), scratch=(), cost=None):
+    spaces = (*spaces, *[pltpu.VMEM] * (len(args) - len(spaces)))
+    args = [
+        pltpu.with_memory_space_constraint(a, s) if s == pltpu.HBM else a
+        for a, s in zip(args, spaces)
+    ]
     return pl.pallas_call(
         kernel,
-        out_shape=[jax.ShapeDtypeStruct(s, F32) for s in outs],
-        in_specs=[pl.BlockSpec(memory_space=space(k)) for k in range(len(args))],
+        out_shape=[jax.ShapeDtypeStruct(s, k) for s, k in outs],
+        in_specs=[pl.BlockSpec(memory_space=space) for space in spaces],
         out_specs=[pl.BlockSpec(memory_space=pltpu.VMEM) for _ in outs],
-        scratch_shapes=[pltpu.VMEM(s, F32) for s in scratch],
+        scratch_shapes=scratch,
+        cost_estimate=cost,
         compiler_params=pltpu.CompilerParams(vmem_limit_bytes=32 * 1024 * 1024),
     )(*args)
 
@@ -403,55 +482,93 @@
     rhs, fine_face, fine_sink, fine_kap, cell_mask, block_aggregate, coarse_face, coarse_sink, coarse_kap
 ):
     narrow = lax.axis_index("narrow").astype(I32).reshape(1)
-    fine = (
+    cells = ((2 * BLK, LANES), F32)
+    five, level, two = ((k * AGG, LANES) for k in (5, PARTS, 2))
+    five, level, two = (five, F32), (level, F32), (two, F32)
+    units = ((NARROW * UNIT, LANES), F32)
+    vmem = lambda *rows: [pltpu.VMEM((r, LANES), F32) for r in rows]
+    held = vmem(2 * BLK, 2 * BLK, 2 * BLK, BLK) + [pltpu.VMEM((BLK, LANES), I32)]
+    beside = pl.CostEstimate(flops=0, bytes_accessed=4 * 1024 * 1024, transcendentals=0)
+    fine_args = (
         rhs.reshape(2 * BLK, LANES),
         fine_face.reshape(2 * BLK, LANES),
         fine_sink.reshape(2 * BLK, LANES),
         fine_kap,
         cell_mask,
     )
-    five, two, units = (5 * AGG, LANES), (2 * AGG, LANES), (NARROW * UNIT, LANES)
-    (coef1,) = call(
+    sent, slots = call(
+        pre_kernel,
+        [units, ((BLK, LANES), F32)],
+        narrow,
+        block_aggregate.reshape(1, BLK),
+        *fine_args,
+        spaces=(pltpu.SMEM, *[pltpu.HBM] * 6),
+        scratch=held + [pltpu.VMEM((1, BLK), I32), pltpu.SemaphoreType.DMA((6,))],
+    )
+    recv = to_all(sent)
+    coef1, level1 = call(
         coef_kernel,
-        [five],
+        [five, level],
+        slots,
         coarse_face.reshape(2 * AGG, LANES),
         coarse_sink.reshape(2 * AGG, LANES),
         coarse_kap,
-    )
-    coef2 = coef1 + exchange(coef1, 1)
-    coef2_x = [exchange(coef2, b) for b in (2, 4, 6)]
-
-    sent, slots = call(
-        pre_kernel,
-        [units, (BLK, LANES)],
-        narrow,
-        *fine,
-        block_aggregate.reshape(1, BLK),
-        smem=1,
-    )
-    recv = to_all(sent)
+        spaces=(pltpu.VMEM, *[pltpu.HBM] * 3),
+        scratch=vmem(2 * AGG, 2 * AGG, AGG) + [pltpu.SemaphoreType.DMA((3,))],
+        cost=beside,
+    )
+    (fine,) = call(
+        ready_kernel,
+        [((14 * BLK, LANES), F32)],
+        slots,
+        *fine_args,
+        spaces=(pltpu.VMEM, *[pltpu.HBM] * 5),
+        scratch=held + [pltpu.SemaphoreType.DMA((5,))],
+        cost=beside,
+    )
+    coef2, level2 = call(pair_kernel, [five, level], coef1, exchange(coef1, 1), cost=beside)
+    (levels,) = call(
+        upper_kernel,
+        [((3 * PARTS * AGG, LANES), F32)],
+        coef2,
+        *[exchange(coef2, b) for b in (2, 6, 4)],
+        scratch=vmem(5 * AGG, 5 * AGG, 5 * AGG),
+        cost=beside,
+    )
     left1, below1, source1, marks, own_edges = call(
         restrict_kernel,
-        [two, two, two, (8 + 2 * NARROW, LANES), (8, LANES)],
+        [two, two, two, ((8 + 2 * NARROW, LANES), F32), ((8, LANES), F32)],
         narrow,
         recv,
-        coef1,
-        smem=1,
+        level1,
+        fine,
+        spaces=(pltpu.SMEM,),
+    )
+    hot, edges = call(
+        side_kernel,
+        [((NARROW * CAP + 2 * NARROW, 2 * LANES), BF16), ((14 * 8, LANES), F32)],
+        marks,
+        own_edges,
     )
     left2, below2, source2 = call(
-        second_kernel, [two, two, two], left1, exchange(left1, 1), coef2
-    )
-    left2_x = [exchange(left2, b) for b in (2, 4, 6)]
+        second_kernel, [two, two, two], left1, exchange(left1, 1), level2
+    )
     (back,) = call(
         top_kernel,
         [units],
-        left2, *left2_x, coef2, *coef2_x, below2, source2, coef1, below1, source1, marks,
-        scratch=(five, five, five),
+        left2,
+        *[exchange(left2, b) for b in (2, 6, 4)],
+        levels,
+        level2,
+        below2,
+        source2,
+        level1,
+        below1,
+        source1,
+        hot,
     )
     recv = to_all(back)
-    (out,) = call(
-        post_kernel, [(2 * BLK, LANES)], narrow, *fine, slots, recv, own_edges, smem=1
-    )
+    (out,) = call(post_kernel, [cells], narrow, fine, slots, recv, edges, spaces=(pltpu.SMEM,))
     return out.reshape(BLK, 2, LANES)
 
 

time: 75 us -> 69.1 us (0.921)
  local copies, waits for them, and re-layouts: 5.38 us -> 0 us
  Pallas kernels: 6.88 us -> 11.7 us
  waiting for transfers between devices: 19.1 us -> 14.7 us
  starting transfers between devices: 21.2 us -> 20.1 us
    unnamed x28 -> x0, local copies, waits for them, and re-layouts: 5.38 us -> none
    pallas_call x6 -> x10, Pallas kernels: 6.88 us -> 11.7 us  [call(): pl.pallas_call(kernel, out_shape=[jax.ShapeDtypeStruct(s, k) for s, k in...]
    all_to_all x1, waiting for transfers between devices: 11.5 us -> 9.23 us  [to_all(): moved = lax.all_to_all(units.reshape(shape), 'narrow', 0, 0, tiled=True)]
    ppermute x8, waiting for transfers between devices: 7.62 us -> 5.5 us  [exchange(): lax.ppermute(value, 'wide', [(i, i ^ bits) for i in range(lax.axis_size('...]
    ppermute x8, starting transfers between devices: 9.76 us -> 8.69 us  [exchange(): lax.ppermute(value, 'wide', [(i, i ^ bits) for i in range(lax.axis_size('...]
  transfers between devices with their start and end apart: 9 -> 9, of which waited for: 5 -> 5; matrix products, arithmetic and copies ran while one was open for 0% -> 0% of each run, Pallas kernels for 2% -> 8%
where the time goes in v2:
time: 69.1 us; the launch traced here: 68.4 us
  blocking collectives  21.9 us (32%)
  starting transfers between devices  20.1 us (29%)
  waiting for transfers between devices  14.7 us (21%)
  Pallas kernels  11.7 us (17%)
    all_to_all x1, blocking collectives, to_all(): moved = lax.all_to_all(units.reshape(shape), 'narrow', 0, 0, tiled=True)  21.9 us
    pallas_call x10, Pallas kernels, call(): pl.pallas_call(kernel, out_shape=[jax.ShapeDtypeStruct(s, k) for s, k in...  11.7 us
    all_to_all x1, starting transfers between devices, to_all(): moved = lax.all_to_all(units.reshape(shape), 'narrow', 0, 0, tiled=True)  11.4 us
    all_to_all x1, waiting for transfers between devices, to_all(): moved = lax.all_to_all(units.reshape(shape), 'narrow', 0, 0, tiled=True)  9.23 us
    ppermute x8, starting transfers between devices, exchange(): lax.ppermute(value, 'wide', [(i, i ^ bits) for i in range(lax.axis_size('...  8.69 us
    ppermute x8, waiting for transfers between devices, exchange(): lax.ppermute(value, 'wide', [(i, i ^ bits) for i in range(lax.axis_size('...  5.5 us
  transfers between devices with their start and end apart: 9, of which 5 were waited for; matrix products, arithmetic and copies ran while one was open for 0% of the time, Pallas kernels for 8%

profile of v2, /device:TPU:32, one launch (start us, length us, event | category | flops | bytes accessed | tf_op | source)
XLA Modules:
  0.0 68.4 jit_solution(4677017230726177640)
XLA Ops:
  0.0 3.2 %shard_map.91 = (f32[1088,128]{1,0:T(8,128)}, f32[256,128]{1,0:T(8,128)S(1)}) custom-call(s32[1]{0:T(128)} %bitcast.narrow, s32[1,256]{1,0:T(1,128)} %bitcast.23, f32[512,128]{1,0:T(8,128)} %bitcast.15, f32[512,128]{1,0:T(8,128)} %bitcast.17, f32[512,128]{1,0:T(8,128)} %bitcast.19, f32[256,128]{1,0:T(8,128)} %refs_3_.3, s32[256,128]{1,0:T(8,128)} %refs_4_.3), custom_call_target="tpu_custom_call" | custom-call | tf_op jit(solution)/shard_map/pallas_call | solution.py:460
  3.2 11.4 %all-to-all-start = ((f32[544,2,128]{2,1,0:T(2,128)}), f32[544,2,128]{2,1,0:T(2,128)S(1)}, u32[]{:S(2)}, u32[]{:S(2)}) async-start(f32[544,2,128]{2,1,0:T(2,128)} %bitcast.5), calls=%async_computation | async-start | bytes 1114112 | tf_op jit(solution)/shard_map/all_to_all | solution.py:477
  14.6 1.0 %shard_map.93 = (f32[320,128]{1,0:T(8,128)S(1)}, f32[640,128]{1,0:T(8,128)S(1)}) custom-call(f32[256,128]{1,0:T(8,128)S(1)} %get-tuple-element.21.token.slots, f32[128,128]{1,0:T(8,128)} %bitcast.21, f32[128,128]{1,0:T(8,128)} %bitcast.22, f32[64,128]{1,0:T(8,128)} %kap_hbm.1), custom_call_target="tpu_custom_call" | custom-call | bytes 4194304 | tf_op jit(solution)/shard_map/pallas_call | solution.py:460
  15.6 0.1 collective-permute-start.1
  15.7 1.4 %collective-permute-done.1.other = f32[320,128]{1,0:T(8,128)S(1)} collective-permute-done((f32[320,128]{1,0:T(8,128)S(1)}, f32[320,128]{1,0:T(8,128)S(1)}, u32[]{:S(2)}, u32[]{:S(2)}) %collective-permute-start.1) | collective-permute-done | bytes 163872 | tf_op jit(solution)/shard_map/ppermute | solution.py:472
  17.1 0.1 shard_map.95
  17.2 3.1 %collective-permute-start.7 = (f32[320,128]{1,0:T(8,128)S(1)}, f32[320,128]{1,0:T(8,128)S(1)}, u32[]{:S(2)}, u32[]{:S(2)}) collective-permute-start(f32[320,128]{1,0:T(8,128)S(1)} %get-tuple-element.28.coef2), channel_id=1, source_target_pairs={{0,128},{32,160},{64,192},{96,224},{128,0},{160,32},{192,64},{224,... | collective-permute-start | bytes 491528 | tf_op jit(solution)/shard_map/ppermute | solution.py:472
  20.3 1.1 %collective-permute-start.6 = (f32[320,128]{1,0:T(8,128)S(1)}, f32[320,128]{1,0:T(8,128)}, u32[]{:S(2)}, u32[]{:S(2)}) collective-permute-start(f32[320,128]{1,0:T(8,128)S(1)} %get-tuple-element.28.coef2), channel_id=1, source_target_pairs={{0,192},{32,224},{64,128},{96,160},{128,64},{160,96},{192,0},{224,... | collective-permute-start | bytes 491528 | tf_op jit(solution)/shard_map/ppermute | solution.py:472
  21.4 1.8 %shard_map.92.token.fine = f32[3584,128]{1,0:T(8,128)S(1)} custom-call(f32[256,128]{1,0:T(8,128)S(1)} %get-tuple-element.21.token.slots, f32[512,128]{1,0:T(8,128)} %bitcast.16, f32[512,128]{1,0:T(8,128)} %bitcast.18, f32[512,128]{1,0:T(8,128)} %bitcast.20, f32[256,128]{1,0:T(8,128)} %refs_3_.3, s32[256,128]{1,0:T(8,128)} %refs_4_.3), custom_call_target="tpu_custom_call" | custom-call | bytes 4194304 | tf_op jit(solution)/shard_map/pallas_call | solution.py:460
  23.2 9.2 %all-to-all-done = f32[544,2,128]{2,1,0:T(2,128)S(1)} async-done(((f32[544,2,128]{2,1,0:T(2,128)}), f32[544,2,128]{2,1,0:T(2,128)S(1)}, u32[]{:S(2)}, u32[]{:S(2)}) %all-to-all-start) | async-done | bytes 557088 | tf_op jit(solution)/shard_map/all_to_all | solution.py:477
  32.4 1.0 %shard_map.94 = (f32[128,128]{1,0:T(8,128)S(1)}, f32[128,128]{1,0:T(8,128)S(1)}, f32[128,128]{1,0:T(8,128)S(1)}, f32[72,128]{1,0:T(8,128)S(1)}, f32[8,128]{1,0:T(8,128)S(1)}) custom-call(s32[1]{0:T(128)} %bitcast.narrow, f32[1088,128]{1,0:T(8,128)S(1)} %bitcast.12, f32[640,128]{1,0:T(8,128)S(1)} %get-tuple-element.23.level1, ...), custom_call_target="tpu_custom_call" | custom-call | tf_op jit(solution)/shard_map/pallas_call | solution.py:460
  33.4 0.1 collective-permute-start
  33.5 1.2 %collective-permute-done.other = f32[128,128]{1,0:T(8,128)S(1)} collective-permute-done((f32[128,128]{1,0:T(8,128)S(1)}, f32[128,128]{1,0:T(8,128)S(1)}, u32[]{:S(2)}, u32[]{:S(2)}) %collective-permute-start) | collective-permute-done | bytes 65568 | tf_op jit(solution)/shard_map/ppermute | solution.py:472
  34.7 0.2 shard_map.96
  35.0 3.1 %collective-permute-start.4 = (f32[128,128]{1,0:T(8,128)S(1)}, f32[128,128]{1,0:T(8,128)S(1)}, u32[]{:S(2)}, u32[]{:S(2)}) collective-permute-start(f32[128,128]{1,0:T(8,128)S(1)} %get-tuple-element.27.left2), channel_id=1, source_target_pairs={{0,128},{32,160},{64,192},{96,224},{128,0},{160,32},{192,64},{224,... | collective-permute-start | bytes 196616 | tf_op jit(solution)/shard_map/ppermute | solution.py:472
  38.1 1.1 %collective-permute-start.3 = (f32[128,128]{1,0:T(8,128)S(1)}, f32[128,128]{1,0:T(8,128)S(1)}, u32[]{:S(2)}, u32[]{:S(2)}) collective-permute-start(f32[128,128]{1,0:T(8,128)S(1)} %get-tuple-element.27.left2), channel_id=1, source_target_pairs={{0,192},{32,224},{64,128},{96,160},{128,64},{160,96},{192,0},{224,... | collective-permute-start | bytes 196616 | tf_op jit(solution)/shard_map/ppermute | solution.py:472
  39.2 0.0 collective-permute-done.6.coef2_b
  39.3 1.1 %shard_map.97.levels = f32[1920,128]{1,0:T(8,128)S(1)} custom-call(f32[320,128]{1,0:T(8,128)S(1)} %get-tuple-element.28.coef2, f32[320,128]{1,0:T(8,128)} %collective-permute-done.5.coef2_a, f32[320,128]{1,0:T(8,128)} %collective-permute-done.6.coef2_b, f32[320,128]{1,0:T(8,128)S(1)} %collective-permute-done.7.coef2_c), custom_call_target="tpu_custom_call" | custom-call | bytes 4194304 | tf_op jit(solution)/shard_map/pallas_call | solution.py:460
  40.4 0.3 shard_map.98
  40.7 0.1 collective-permute-done.4.left2_c
  40.8 2.7 %collective-permute-done.3.left2_b = f32[128,128]{1,0:T(8,128)S(1)} collective-permute-done((f32[128,128]{1,0:T(8,128)S(1)}, f32[128,128]{1,0:T(8,128)S(1)}, u32[]{:S(2)}, u32[]{:S(2)}) %collective-permute-start.3) | collective-permute-done | bytes 65568 | tf_op jit(solution)/shard_map/ppermute | solution.py:472
  43.6 1.5 %shard_map.99 = f32[1088,128]{1,0:T(8,128)S(1)} custom-call(f32[128,128]{1,0:T(8,128)S(1)} %get-tuple-element.27.left2, f32[128,128]{1,0:T(8,128)S(1)} %collective-permute-done.2.left2_a, f32[128,128]{1,0:T(8,128)S(1)} %collective-permute-done.3.left2_b, f32[128,128]{1,0:T(8,128)S(1)} %collective-permute-done.4.left2_c, f32[1920,128]{1,0:T(8,128)S(1)} %shard_map.97.levels, ...), custom_call_target="tpu_custom_call" | custom-call | tf_op jit(solution)/shard_map/pallas_call | solution.py:460
  45.0 21.9 %all_to_all.10 = f32[544,2,128]{2,1,0:T(2,128)S(1)} all-to-all(f32[544,2,128]{2,1,0:T(2,128)S(1)} %bitcast.13), channel_id=1, replica_groups=mesh['wide'=8,'narrow'=32] {'narrow'}, dimensions={0} | all-to-all | bytes 1114112 | tf_op jit(solution)/shard_map/all_to_all | solution.py:477
  66.9 1.5 %shard_map.100 = f32[512,128]{1,0:T(8,128)} custom-call(s32[1]{0:T(128)} %bitcast.narrow, f32[3584,128]{1,0:T(8,128)S(1)} %shard_map.92.token.fine, f32[256,128]{1,0:T(8,128)S(1)} %get-tuple-element.21.token.slots, f32[1088,128]{1,0:T(8,128)S(1)} %bitcast.14, f32[112,128]{1,0:T(8,128)S(1)} %get-tuple-element.36.edges), custom_call_target="tpu_custom_call" | custom-call | tf_op jit(solution)/shard_map/pallas_call | solution.py:460
  (5 shorter events, 0.0 us)
Async XLA Ops:
  3.2 29.2 %all-to-all-start = ((f32[544,2,128]{2,1,0:T(2,128)}), f32[544,2,128]{2,1,0:T(2,128)S(1)}, u32[]{:S(2)}, u32[]{:S(2)}) async-start(f32[544,2,128]{2,1,0:T(2,128)} %bitcast.5), calls=%async_computation | async-start | bytes 1114112 | tf_op jit(solution)/shard_map/all_to_all | solution.py:477
  15.6 1.5 %collective-permute-start.1 = (f32[320,128]{1,0:T(8,128)S(1)}, f32[320,128]{1,0:T(8,128)S(1)}, u32[]{:S(2)}, u32[]{:S(2)}) collective-permute-start(f32[320,128]{1,0:T(8,128)S(1)} %get-tuple-element.25.mine), channel_id=1, source_target_pairs={{0,32},{32,0},{64,96},{96,64},{128,160},{160,128},{192,224},{224,1... | collective-permute-start | bytes 491528 | tf_op jit(solution)/shard_map/ppermute | solution.py:472
  17.2 22.1 %collective-permute-start.7 = (f32[320,128]{1,0:T(8,128)S(1)}, f32[320,128]{1,0:T(8,128)S(1)}, u32[]{:S(2)}, u32[]{:S(2)}) collective-permute-start(f32[320,128]{1,0:T(8,128)S(1)} %get-tuple-element.28.coef2), channel_id=1, source_target_pairs={{0,128},{32,160},{64,192},{96,224},{128,0},{160,32},{192,64},{224,... | collective-permute-start | bytes 491528 | tf_op jit(solution)/shard_map/ppermute | solution.py:472
  20.3 19.0 %collective-permute-start.6 = (f32[320,128]{1,0:T(8,128)S(1)}, f32[320,128]{1,0:T(8,128)}, u32[]{:S(2)}, u32[]{:S(2)}) collective-permute-start(f32[320,128]{1,0:T(8,128)S(1)} %get-tuple-element.28.coef2), channel_id=1, source_target_pairs={{0,192},{32,224},{64,128},{96,160},{128,64},{160,96},{192,0},{224,... | collective-permute-start | bytes 491528 | tf_op jit(solution)/shard_map/ppermute | solution.py:472
  21.4 17.8 %collective-permute-start.5 = (f32[320,128]{1,0:T(8,128)S(1)}, f32[320,128]{1,0:T(8,128)}, u32[]{:S(2)}, u32[]{:S(2)}) collective-permute-start(f32[320,128]{1,0:T(8,128)S(1)} %get-tuple-element.28.coef2), channel_id=1, source_target_pairs={{0,64},{32,96},{64,0},{96,32},{128,192},{160,224},{192,128},{224,1... | collective-permute-start | bytes 491528 | tf_op jit(solution)/shard_map/ppermute | solution.py:472
  33.4 1.3 %collective-permute-start = (f32[128,128]{1,0:T(8,128)S(1)}, f32[128,128]{1,0:T(8,128)S(1)}, u32[]{:S(2)}, u32[]{:S(2)}) collective-permute-start(f32[128,128]{1,0:T(8,128)S(1)} %get-tuple-element.24.mine), channel_id=1, source_target_pairs={{0,32},{32,0},{64,96},{96,64},{128,160},{160,128},{192,224},{224,1... | collective-permute-start | bytes 196616 | tf_op jit(solution)/shard_map/ppermute | solution.py:472
  35.0 5.9 %collective-permute-start.4 = (f32[128,128]{1,0:T(8,128)S(1)}, f32[128,128]{1,0:T(8,128)S(1)}, u32[]{:S(2)}, u32[]{:S(2)}) collective-permute-start(f32[128,128]{1,0:T(8,128)S(1)} %get-tuple-element.27.left2), channel_id=1, source_target_pairs={{0,128},{32,160},{64,192},{96,224},{128,0},{160,32},{192,64},{224,... | collective-permute-start | bytes 196616 | tf_op jit(solution)/shard_map/ppermute | solution.py:472
  38.1 5.5 %collective-permute-start.3 = (f32[128,128]{1,0:T(8,128)S(1)}, f32[128,128]{1,0:T(8,128)S(1)}, u32[]{:S(2)}, u32[]{:S(2)}) collective-permute-start(f32[128,128]{1,0:T(8,128)S(1)} %get-tuple-element.27.left2), channel_id=1, source_target_pairs={{0,192},{32,224},{64,128},{96,160},{128,64},{160,96},{192,0},{224,... | collective-permute-start | bytes 196616 | tf_op jit(solution)/shard_map/ppermute | solution.py:472
  39.2 4.3 %collective-permute-start.2 = (f32[128,128]{1,0:T(8,128)S(1)}, f32[128,128]{1,0:T(8,128)S(1)}, u32[]{:S(2)}, u32[]{:S(2)}) collective-permute-start(f32[128,128]{1,0:T(8,128)S(1)} %get-tuple-element.27.left2), channel_id=1, source_target_pairs={{0,64},{32,96},{64,0},{96,32},{128,192},{160,224},{192,128},{224,1... | collective-permute-start | bytes 196616 | tf_op jit(solution)/shard_map/ppermute | solution.py:472

commit v3 on v2

--- a/solution.py
+++ b/solution.py
@@ -11,7 +11,9 @@
 AGG = 64
 NARROW = 32
 CAP = 16
-UNIT = 2 * (CAP + 1)
+UNIT = 2 * CAP + 1
+SIDE = 7
+LABEL = LANES - CAP
 F32, BF16, I32 = jnp.float32, jnp.bfloat16, jnp.int32
 
 
@@ -40,37 +42,35 @@
 
 
 class Level:
-    def __init__(self, faces, sinks, coupling, prev, nxt):
+    def __init__(self, faces, sinks, coupling, prev, nxt, left=None):
         self.prev, self.nxt = prev, nxt
         self.faces = faces
-        self.left = [prev(f) for f in faces]
+        self.left = [prev(f) for f in faces] if left is None else left
         self.diag = [s + l + f for s, l, f in zip(sinks, self.left, faces)]
         self.coupling = coupling
         scale = OMEGA / (self.diag[0] * self.diag[1] - coupling * coupling)
         self.inv = (self.diag[1] * scale, self.diag[0] * scale, coupling * scale)
 
     def parts(self):
-        return [*self.faces, *self.left, *self.diag, self.coupling, *self.inv]
+        return [*self.faces, *self.left, *self.inv, *self.diag, self.coupling]
 
     @classmethod
     def load(cls, part, prev, nxt):
         level = cls.__new__(cls)
         level.prev, level.nxt = prev, nxt
-        level.faces, level.left, level.diag = part[0:2], part[2:4], part[4:6]
-        level.coupling, level.inv = part[6], part[7:10]
+        level.faces, level.left, level.inv = part[0:2], part[2:4], part[4:7]
+        if len(part) > 7:
+            level.diag, level.coupling = part[7:9], part[9]
         return level
 
+    def flow(self, v):
+        return [self.left[f] * self.prev(v[f]) + self.faces[f] * self.nxt(v[f]) for f in (0, 1)]
+
     def misfit(self, v, source):
-        return [
-            source[f]
-            - (
-                self.diag[f] * v[f]
-                - self.left[f] * self.prev(v[f])
-                - self.faces[f] * self.nxt(v[f])
-                - self.coupling * v[1 - f]
-            )
-            for f in (0, 1)
+        cell = [
+            (source[f] - self.diag[f] * v[f]) + self.coupling * v[1 - f] for f in (0, 1)
         ]
+        return [a + b for a, b in zip(cell, self.flow(v))]
 
     def step(self, r):
         return [
@@ -78,22 +78,15 @@
             self.inv[2] * r[0] + self.inv[1] * r[1],
         ]
 
-    def smooth(self, v, source, sweeps):
+    def smooth(self, v, drive, sweeps):
         for _ in range(sweeps):
-            d = self.step(self.misfit(v, source))
-            v = [v[0] + d[0], v[1] + d[1]]
+            d = self.step(self.flow(v))
+            v = [((1.0 - OMEGA) * v[f] + drive[f]) + d[f] for f in (0, 1)]
         return v
 
     def start(self, source, sweeps):
-        return self.smooth(self.step(source), source, sweeps - 1)
-
-
-def fine_level(face, sink, kap, live, prev, nxt, last):
-    live_next = jnp.where(last, 0.0, nxt(live))
-    both = live * live_next
-    faces = [f * both for f in face]
-    coupling = kap * jnp.sqrt(sink[0] * sink[1]) * live
-    return Level(faces, sink, coupling, prev, nxt)
+        drive = self.step(source)
+        return self.smooth(drive, drive, sweeps - 1), drive
 
 
 def store(ref, parts, at=0):
@@ -118,11 +111,11 @@
 
 
 def select_rows(onehot, x):
-    total = None
-    for part in split3(x):
-        term = jnp.dot(onehot, part, preferred_element_type=F32)
-        total = term if total is None else total + term
-    return total
+    return jnp.dot(
+        jnp.concatenate([onehot] * 3, axis=1),
+        jnp.concatenate(split3(x), axis=0),
+        preferred_element_type=F32,
+    )
 
 
 def as_bf16(mask):
@@ -144,27 +137,31 @@
 
 def fine_start(rhs, face, sink, kap, mask):
     live = mask[...].astype(F32)
-    data = fine_level(
-        planar(face, BLK), planar(sink, BLK), kap[...], live, chain_prev, chain_next, last_cell((BLK, LANES))
-    )
+    live_next = jnp.where(last_cell((BLK, LANES)), 0.0, chain_next(live))
+    both = live * live_next
+    sinks = planar(sink, BLK)
+    coupling = kap[...] * jnp.sqrt(sinks[0] * sinks[1]) * live
+    data = Level([f * both for f in planar(face, BLK)], sinks, coupling, chain_prev, chain_next)
     source = [r * live for r in planar(rhs, BLK)]
-    return data, source, data.start(source, 2)
-
-
-def ready_kernel(token, *refs):
-    inputs, fine, held, sems = refs[0:5], refs[5], refs[6:11], refs[11]
-    for copy in start_copies(inputs, held, sems):
+    return data, source, *data.start(source, 2)
+
+
+def ready_kernel(slot_row, *refs):
+    inputs, fine, slots, held, sems = refs[0:5], refs[5], refs[6], refs[7:12], refs[12]
+    copies = start_copies(inputs, held, sems)
+    slots[...] = jnp.transpose(jnp.broadcast_to(slot_row[0:1, :], (LANES, BLK)), (1, 0))
+    for copy in copies:
         copy.wait()
-    data, source, field = fine_start(*held)
-    store(fine, [*field, *source, *data.parts()])
+    data, _, field, drive = fine_start(*held)
+    store(fine, [*field, *drive, *data.parts()[0:7]])
 
 
 def pre_kernel(narrow, agg_hbm, *refs):
     inputs, out, slots, held, sems = refs[0:5], refs[5], refs[6], refs[7:13], refs[13]
     rhs, face, sink, kap, mask, agg = held
     n = narrow[0]
-    copies = start_copies((*inputs, agg_hbm), held, sems)
-    copies.pop().wait()
+    for copy in start_copies((*inputs, agg_hbm), held, sems):
+        copy.wait()
 
     label = agg[...]
     owner = label // AGG
@@ -183,12 +180,9 @@
     labels = lax.dot_general(
         coded, at_rank, (((1,), (1,)), ((), ())), preferred_element_type=F32
     )
-    out[pl.ds(2 * CAP, NARROW, stride=UNIT), :] = labels
-    slots[...] = jnp.transpose(jnp.broadcast_to(slot.astype(F32), (LANES, BLK)), (1, 0))
-
-    for copy in copies:
-        copy.wait()
-    data, source, field = fine_start(rhs, face, sink, kap, mask)
+    slots[...] = jnp.broadcast_to(slot.astype(F32), (8, BLK))
+
+    data, source, field, _ = fine_start(rhs, face, sink, kap, mask)
     misfit = data.misfit(field, source)
     row, lane = iota((BLK, LANES), 0), iota((BLK, LANES), 1)
     drop = ((row == BLK - 1) & (lane >= LANES - 3) & (n < NARROW - 1)) | (
@@ -204,33 +198,57 @@
             ]
 
     lane1 = iota((1, LANES), 1)
+
+    def ends(final, first):
+        return jnp.where(lane1 >= LANES // 2, final, first)
+
+    def rows_of(v):
+        return ends(v[BLK - 1 : BLK, :], v[0:1, :])
+
+    live_first = mask[0:1, :].astype(F32)
+    live_final = mask[BLK - 1 : BLK, :].astype(F32)
+    faces = []
+    for f in (0, 1):
+        open_face = face[2 * (BLK - 1) + f : 2 * (BLK - 1) + f + 1, :] * live_final
+        final = jnp.where(lane1 == LANES - 1, open_face, data.faces[f][BLK - 1 : BLK, :])
+        faces.append(ends(final, data.faces[f][0:1, :]))
+    sinks = [
+        ends(sink[2 * (BLK - 1) + f : 2 * (BLK - 1) + f + 1, :], sink[f : f + 1, :]) for f in (0, 1)
+    ]
+    quantities = [*map(rows_of, source), *faces, *sinks, rows_of(data.coupling)]
     edges = jnp.zeros((1, LANES), F32)
-    quantities = [(ref, 2, f) for ref in (rhs, face, sink) for f in (0, 1)]
-    quantities += [(kap, 1, 0), (mask, 1, 0)]
-    for q, (ref, stride, f) in enumerate(quantities):
-        final = (BLK - 1) * stride + f
-        cells = jnp.where(
-            lane1 >= LANES // 2, ref[final : final + 1, :], ref[f : f + 1, :]
-        ).astype(F32)
-        moved = pltpu.roll(cells, (16 * q + 8) % LANES, 1)
-        edges = jnp.where(lane1 // 16 == q, moved, edges)
-    out[pl.ds(2 * CAP + 1, NARROW, stride=UNIT), :] = jnp.broadcast_to(edges, (NARROW, LANES))
+    for q, cells in enumerate(quantities):
+        here = (lane1 >= 2 * SIDE * q) & (lane1 < 2 * SIDE * (q + 1))
+        edges = jnp.where(here, pltpu.roll(cells, 2 * SIDE * q + SIDE, 1), edges)
+    spare = 2 * SIDE * len(quantities)
+    edges = jnp.where(lane1 == spare, pltpu.roll(live_first, spare, 1), edges)
+    for f in (0, 1):
+        before = pltpu.roll(faces[f], spare + 1 + f + SIDE + 1, 1)
+        edges = jnp.where(lane1 == spare + 1 + f, before, edges)
+    out[pl.ds(2 * CAP, NARROW, stride=UNIT), :] = jnp.where(
+        iota((NARROW, LANES), 1) >= LABEL, labels, edges
+    )
 
 
 def interface_level(cells):
     lane = iota(cells.shape, 1)
+    spare = 2 * SIDE * 7
+
+    def moved(start, to):
+        shift = (to - start) % LANES
+        return cells if shift == 0 else pltpu.roll(cells, shift, 1)
 
     def quantity(q, fill):
-        moved = cells if q == 0 else pltpu.roll(cells, LANES - 16 * q, 1)
-        return jnp.where(lane < 16, moved, fill)
-
-    rhs = [quantity(0, 0.0), quantity(1, 0.0)]
-    face = [quantity(2, 0.0), quantity(3, 0.0)]
-    sink = [quantity(4, 1.0), quantity(5, 1.0)]
-    kap, live = quantity(6, 0.0), quantity(7, 0.0)
-    data = fine_level(face, sink, kap, live, row_prev, row_next, lane == LANES - 1)
-    source = [r * live for r in rhs]
-    return data, source
+        return jnp.where(lane < 2 * SIDE, moved(2 * SIDE * q, 0), fill)
+
+    source = [quantity(0, 0.0), quantity(1, 0.0)]
+    live_next = jnp.where(lane == SIDE - 1, moved(spare, SIDE - 1), 1.0)
+    faces = [quantity(2, 0.0) * live_next, quantity(3, 0.0) * live_next]
+    left = [
+        jnp.where(lane == 0, moved(spare + 1 + f, 0), row_prev(faces[f])) for f in (0, 1)
+    ]
+    sinks = [quantity(4, 1.0), quantity(5, 1.0)]
+    return Level(faces, sinks, quantity(6, 0.0), row_prev, row_next, left), source
 
 
 PARTS = 10
@@ -279,27 +297,28 @@
         store(levels, coarse_level(ref).parts(), k * PARTS * AGG)
 
 
-def restrict_kernel(narrow, recv, level1, token, leftover, below, source_out, marks, own_edges):
+def restrict_kernel(narrow, recv, level1, token, leftover, below, drive_out, marks, own_edges):
     n = narrow[0]
     lane = iota((NARROW, LANES), 1)
     src = iota((NARROW, LANES), 0)
-    labels = recv[pl.ds(2 * CAP, NARROW, stride=UNIT), :]
-    raw = recv[pl.ds(2 * CAP + 1, NARROW, stride=UNIT), :]
-    code = labels.astype(I32)
-    plain = (code - 1) % AGG
-    plain = jnp.where(code > 0, plain, -1)
-
-    cells = jnp.where(lane % 16 < 8, raw, pltpu.roll(raw, NARROW - 1, 0))
+    raw = recv[pl.ds(2 * CAP, NARROW, stride=UNIT), :]
+    code = jnp.where(lane >= LABEL, raw, 0.0).astype(I32)
+    plain = jnp.where(code > 0, (code - 1) % AGG, -1)
+
+    from_end = lane > 2 * SIDE * 7
+    for q in range(7):
+        from_end = from_end | ((lane >= 2 * SIDE * q) & (lane < 2 * SIDE * q + SIDE))
+    cells = jnp.where(from_end, raw, pltpu.roll(raw, NARROW - 1, 0))
     data, source = interface_level(cells)
-    field = data.start(source, 2)
-    mis = [pltpu.roll(m, LANES - 8, 1) for m in data.misfit(field, source)]
+    field, _ = data.start(source, 2)
+    mis = [pltpu.roll(m, LANES - SIDE, 1) for m in data.misfit(field, source)]
     mis = jnp.concatenate(mis, axis=1)
     wide_lane = iota((NARROW, 2 * LANES), 1) % LANES
     real = iota((NARROW, 2 * LANES), 0) < NARROW - 1
     after_end = jnp.where((wide_lane >= LANES - 3) & real, mis, 0.0)
     at_start = jnp.where((wide_lane < 3) & real, mis, 0.0)
-    is_end = (code > 128) & (lane < CAP)
-    is_start = (code > 64) & (code <= 128) & (lane < CAP)
+    is_end = code > 128
+    is_start = (code > 64) & (code <= 128)
     end_at = jnp.max(jnp.where(is_end, plain, -1), axis=1, keepdims=True)
     start_at = jnp.max(jnp.where(is_start, plain, -1), axis=1, keepdims=True)
     end_hot = jnp.where(lane == end_at, 1.0, 0.0)
@@ -314,7 +333,8 @@
 
     rows = []
     for t in range(NARROW // 8):
-        mine = jnp.where(lane[0:8] // CAP == src[0:8], plain[8 * t : 8 * t + 8], 0)
+        spread = pltpu.roll(plain[8 * t : 8 * t + 8], CAP, 1, stride=CAP, stride_axis=0)
+        mine = jnp.where(lane[0:8] // CAP == src[0:8], spread, 0)
         rows.append(jnp.sum(mine, axis=0, keepdims=True))
     total = select_rows(edge_hot, edge_rows)
     for half in (0, 1):
@@ -332,10 +352,10 @@
         )
     source_c = [total[:, 0:LANES], total[:, LANES:]]
     level = ready_level(level1)
-    correction = level.start(source_c, 2)
+    correction, drive = level.start(source_c, 2)
     store2(leftover, level.misfit(correction, source_c))
     store2(below, correction)
-    store2(source_out, source_c)
+    store2(drive_out, drive)
 
     for t in range(NARROW // 8):
         marks[t : t + 1, :] = rows[t].astype(F32)
@@ -345,13 +365,13 @@
     own_edges[1:2, :] = jnp.sum(jnp.where(src == n, cells, 0.0), axis=0, keepdims=True)
 
 
-def second_kernel(mine, other, level2, leftover, below, source_out):
+def second_kernel(mine, other, level2, leftover, below, drive_out):
     source = [a + b for a, b in zip(load2(mine), load2(other))]
     level = ready_level(level2)
-    correction = level.start(source, 2)
+    correction, drive = level.start(source, 2)
     store2(leftover, level.misfit(correction, source))
     store2(below, correction)
-    store2(source_out, source)
+    store2(drive_out, drive)
 
 
 def side_kernel(marks, own_edges, hot, edges):
@@ -367,28 +387,28 @@
     hot[NARROW * CAP :, 0:LANES] = (ends + pltpu.roll(ends, AGG, 1)).astype(BF16)
     hot[NARROW * CAP :, LANES:] = ends.astype(BF16)
     data, source = interface_level(own_edges[...])
-    field = data.start(source, 2)
-    store(edges, [*field, *source, *data.parts()])
+    field, drive = data.start(source, 2)
+    store(edges, [*field, *drive, *data.parts()[0:7]])
 
 
 def top_kernel(
-    left2, left2_a, left2_b, left2_c, levels, level2, below2, source2, level1, below1, source1, hot, out
+    left2, left2_a, left2_b, left2_c, levels, level2, below2, drive2, level1, below1, drive1, hot, out
 ):
     source3 = [a + b for a, b in zip(load2(left2), load2(left2_a))]
     source3_far = [a + b for a, b in zip(load2(left2_b), load2(left2_c))]
     level3, level3_far, level4 = [ready_level(levels, k) for k in range(3)]
-    below3 = level3.start(source3, 2)
-    below3_far = level3_far.start(source3_far, 2)
+    below3, drive3 = level3.start(source3, 2)
+    below3_far, _ = level3_far.start(source3_far, 2)
     source4 = [
         a + b
         for a, b in zip(
             level3.misfit(below3, source3), level3_far.misfit(below3_far, source3_far)
         )
     ]
-    v = level4.start(source4, 4)
-    v = level3.smooth([a + b for a, b in zip(below3, v)], source3, 2)
-    v = ready_level(level2).smooth([a + b for a, b in zip(load2(below2), v)], load2(source2), 2)
-    v = ready_level(level1).smooth([a + b for a, b in zip(load2(below1), v)], load2(source1), 2)
+    v, _ = level4.start(source4, 4)
+    v = level3.smooth([a + b for a, b in zip(below3, v)], drive3, 2)
+    v = ready_level(level2).smooth([a + b for a, b in zip(load2(below2), v)], load2(drive2), 2)
+    v = ready_level(level1).smooth([a + b for a, b in zip(load2(below1), v)], load2(drive1), 2)
 
     both = jnp.concatenate([v[0], v[1]], axis=1)
     both = jnp.concatenate([*split3(both), jnp.zeros((AGG, 2 * LANES), BF16)], axis=0)
@@ -399,17 +419,21 @@
                 s * CAP : (s + 1) * CAP, f * LANES : (f + 1) * LANES
             ]
     ends = rows[NARROW * CAP :, :]
+    lane = iota((NARROW, LANES), 1)
+    halo = []
     for f in (0, 1):
         part = ends[:, f * LANES : (f + 1) * LANES]
-        out[pl.ds(2 * CAP + f, NARROW, stride=UNIT), :] = jnp.where(
-            iota((NARROW, LANES), 1) >= LANES // 2, part[0:NARROW], part[NARROW:]
-        )
+        halo.append(jnp.where(lane >= LANES // 2, part[0:NARROW], part[NARROW:]))
+    middle = (lane >= LANES // 4) & (lane < LANES * 3 // 4)
+    out[pl.ds(2 * CAP, NARROW, stride=UNIT), :] = jnp.where(
+        middle, pltpu.roll(halo[1], LANES // 2, 1), halo[0]
+    )
 
 
 def post_kernel(narrow, fine, slots, recv, edges, out):
     n = narrow[0]
-    field, source = load(fine, 2, BLK), load(fine, 2, BLK, 2 * BLK)
-    data = Level.load(load(fine, PARTS, BLK, 4 * BLK), chain_prev, chain_next)
+    field, drive = load(fine, 2, BLK), load(fine, 2, BLK, 2 * BLK)
+    data = Level.load(load(fine, 7, BLK, 4 * BLK), chain_prev, chain_next)
     slot = slots[...].astype(I32)
     lane = iota((BLK, LANES), 1)
     lifted = None
@@ -426,24 +450,25 @@
         term = select_rows(as_bf16(jnp.concatenate(hots, axis=1)), jnp.concatenate(parts, axis=0))
         lifted = term if lifted is None else lifted + term
     lifted = [lifted[:, 0:LANES], lifted[:, LANES:]]
-    v = data.smooth([a + b for a, b in zip(field, lifted)], source, 2)
-
-    edge_field, edge_source = load(edges, 2, 8), load(edges, 2, 8, 16)
-    edge_data = Level.load(load(edges, PARTS, 8, 32), row_prev, row_next)
+    v = data.smooth([a + b for a, b in zip(field, lifted)], drive, 2)
+
+    edge_field, edge_drive = load(edges, 2, 8), load(edges, 2, 8, 16)
+    edge_data = Level.load(load(edges, 7, 8, 32), row_prev, row_next)
     lane1 = iota((1, LANES), 1)
     row8 = iota((8, LANES), 0)
     edge_v = []
+    halo = jnp.sum(recv[pl.ds(2 * CAP, NARROW, stride=UNIT), :], axis=0, keepdims=True)
     for f in (0, 1):
-        beyond = jnp.sum(recv[pl.ds(2 * CAP + f, NARROW, stride=UNIT), :], axis=0, keepdims=True)
+        beyond = halo if f == 0 else pltpu.roll(halo, LANES // 2, 1)
         first = jnp.where(lane1 >= LANES // 2, beyond, lifted[f][0:1, :])
         final = jnp.where(lane1 >= LANES // 2, lifted[f][BLK - 1 : BLK, :], beyond)
         lift = jnp.where(row8 == 0, first, jnp.where(row8 == 1, final, 0.0))
-        lift = jnp.where(iota((8, LANES), 1) < 16, pltpu.roll(lift, 8, 1), 0.0)
+        lift = jnp.where(iota((8, LANES), 1) < 2 * SIDE, pltpu.roll(lift, SIDE, 1), 0.0)
         edge_v.append(edge_field[f] + lift)
-    edge_v = edge_data.smooth(edge_v, edge_source, 2)
+    edge_v = edge_data.smooth(edge_v, edge_drive, 2)
     for f in (0, 1):
         out[pl.ds(f, BLK, stride=2), :] = v[f]
-        moved = pltpu.roll(edge_v[f], LANES - 8, 1)
+        moved = pltpu.roll(edge_v[f], LANES - SIDE, 1)
         out[f : f + 1, :] = jnp.where((lane1 < 4) & (n > 0), moved[0:1, :], v[f][0:1, :])
         final = 2 * (BLK - 1) + f
         out[final : final + 1, :] = jnp.where(
@@ -473,7 +498,7 @@
 
 
 def to_all(units):
-    shape = (NARROW * UNIT // 2, 2, LANES)
+    shape = (NARROW * UNIT, 1, LANES)
     moved = lax.all_to_all(units.reshape(shape), "narrow", 0, 0, tiled=True)
     return moved.reshape(NARROW * UNIT, LANES)
 
@@ -496,9 +521,9 @@
         fine_kap,
         cell_mask,
     )
-    sent, slots = call(
+    sent, slot_row = call(
         pre_kernel,
-        [units, ((BLK, LANES), F32)],
+        [units, ((8, BLK), F32)],
         narrow,
         block_aggregate.reshape(1, BLK),
         *fine_args,
@@ -509,7 +534,7 @@
     coef1, level1 = call(
         coef_kernel,
         [five, level],
-        slots,
+        slot_row,
         coarse_face.reshape(2 * AGG, LANES),
         coarse_sink.reshape(2 * AGG, LANES),
         coarse_kap,
@@ -517,10 +542,10 @@
         scratch=vmem(2 * AGG, 2 * AGG, AGG) + [pltpu.SemaphoreType.DMA((3,))],
         cost=beside,
     )
-    (fine,) = call(
+    fine, slots = call(
         ready_kernel,
-        [((14 * BLK, LANES), F32)],
-        slots,
+        [((11 * BLK, LANES), F32), ((BLK, LANES), F32)],
+        slot_row,
         *fine_args,
         spaces=(pltpu.VMEM, *[pltpu.HBM] * 5),
         scratch=held + [pltpu.SemaphoreType.DMA((5,))],
@@ -535,7 +560,7 @@
         scratch=vmem(5 * AGG, 5 * AGG, 5 * AGG),
         cost=beside,
     )
-    left1, below1, source1, marks, own_edges = call(
+    left1, below1, drive1, marks, own_edges = call(
         restrict_kernel,
         [two, two, two, ((8 + 2 * NARROW, LANES), F32), ((8, LANES), F32)],
         narrow,
@@ -546,11 +571,11 @@
     )
     hot, edges = call(
         side_kernel,
-        [((NARROW * CAP + 2 * NARROW, 2 * LANES), BF16), ((14 * 8, LANES), F32)],
+        [((NARROW * CAP + 2 * NARROW, 2 * LANES), BF16), ((11 * 8, LANES), F32)],
         marks,
         own_edges,
     )
-    left2, below2, source2 = call(
+    left2, below2, drive2 = call(
         second_kernel, [two, two, two], left1, exchange(left1, 1), level2
     )
     (back,) = call(
@@ -561,10 +586,10 @@
         levels,
         level2,
         below2,
-        source2,
+        drive2,
         level1,
         below1,
-        source1,
+        drive1,
         hot,
     )
     recv = to_all(back)

time: 69.1 us -> 68 us (0.984)
  Pallas kernels: 11.7 us -> 10.3 us
  waiting for transfers between devices: 14.7 us -> 15.4 us
    pallas_call x10, Pallas kernels: 11.7 us -> 10.3 us  [call(): pl.pallas_call(kernel, out_shape=[jax.ShapeDtypeStruct(s, k) for s, k in...]
    ppermute x8, waiting for transfers between devices: 5.5 us -> 6.44 us  [exchange(): lax.ppermute(value, 'wide', [(i, i ^ bits) for i in range(lax.axis_size('...]
  transfers between devices with their start and end apart: 9 -> 9, of which waited for: 5 -> 5; matrix products, arithmetic and copies ran while one was open for 0% -> 0% of each run, Pallas kernels for 8% -> 7%
where the time goes in v3:
time: 68 us; the launch traced here: 67.4 us
  blocking collectives  21.5 us (32%)
  starting transfers between devices  20.1 us (30%)
  waiting for transfers between devices  15.4 us (23%)
  Pallas kernels  10.3 us (15%)
    all_to_all x1, blocking collectives, to_all(): moved = lax.all_to_all(units.reshape(shape), 'narrow', 0, 0, tiled=True)  21.5 us
    all_to_all x1, starting transfers between devices, to_all(): moved = lax.all_to_all(units.reshape(shape), 'narrow', 0, 0, tiled=True)  11.4 us
    pallas_call x10, Pallas kernels, call(): pl.pallas_call(kernel, out_shape=[jax.ShapeDtypeStruct(s, k) for s, k in...  10.3 us
    all_to_all x1, waiting for transfers between devices, to_all(): moved = lax.all_to_all(units.reshape(shape), 'narrow', 0, 0, tiled=True)  8.95 us
    ppermute x8, starting transfers between devices, exchange(): lax.ppermute(value, 'wide', [(i, i ^ bits) for i in range(lax.axis_size('...  8.69 us
    ppermute x8, waiting for transfers between devices, exchange(): lax.ppermute(value, 'wide', [(i, i ^ bits) for i in range(lax.axis_size('...  6.44 us
  transfers between devices with their start and end apart: 9, of which 5 were waited for; matrix products, arithmetic and copies ran while one was open for 0% of the time, Pallas kernels for 7%

profile of v3, /device:TPU:32, one launch (start us, length us, event | category | flops | bytes accessed | tf_op | source)
XLA Modules:
  0.0 67.4 jit_solution(10743212623352693100)
XLA Ops:
  0.0 3.0 %shard_map.91 = (f32[1056,128]{1,0:T(8,128)}, f32[8,256]{1,0:T(8,128)S(1)}) custom-call(s32[1]{0:T(128)} %bitcast.narrow, s32[1,256]{1,0:T(1,128)} %bitcast.27, f32[512,128]{1,0:T(8,128)} %bitcast.19, f32[512,128]{1,0:T(8,128)} %bitcast.21, f32[512,128]{1,0:T(8,128)} %bitcast.23, f32[256,128]{1,0:T(8,128)} %refs_3_.3, s32[256,128]{1,0:T(8,128)} %refs_4_.3), custom_call_target="tpu_custom_call" | custom-call | tf_op jit(solution)/shard_map/pallas_call | solution.py:485
  3.0 11.4 %all-to-all-start = ((f32[1056,1,128]{2,1,0:T(1,128)}), f32[1056,1,128]{2,1,0:T(1,128)S(1)}, u32[]{:S(2)}, u32[]{:S(2)}) async-start(f32[1056,1,128]{2,1,0:T(1,128)} %bitcast.6), calls=%async_computation | async-start | bytes 1081344 | tf_op jit(solution)/shard_map/all_to_all | solution.py:502
  14.4 1.0 %shard_map.93 = (f32[320,128]{1,0:T(8,128)S(1)}, f32[640,128]{1,0:T(8,128)S(1)}) custom-call(f32[8,256]{1,0:T(8,128)S(1)} %get-tuple-element.23.slot_row.token, f32[128,128]{1,0:T(8,128)} %bitcast.25, f32[128,128]{1,0:T(8,128)} %bitcast.26, f32[64,128]{1,0:T(8,128)} %kap_hbm.1), custom_call_target="tpu_custom_call" | custom-call | bytes 4194304 | tf_op jit(solution)/shard_map/pallas_call | solution.py:485
  15.4 0.1 collective-permute-start.1
  15.5 1.4 %collective-permute-done.1.other = f32[320,128]{1,0:T(8,128)S(1)} collective-permute-done((f32[320,128]{1,0:T(8,128)S(1)}, f32[320,128]{1,0:T(8,128)S(1)}, u32[]{:S(2)}, u32[]{:S(2)}) %collective-permute-start.1) | collective-permute-done | bytes 163872 | tf_op jit(solution)/shard_map/ppermute | solution.py:497
  16.9 0.1 shard_map.95
  17.0 3.1 %collective-permute-start.7 = (f32[320,128]{1,0:T(8,128)S(1)}, f32[320,128]{1,0:T(8,128)S(1)}, u32[]{:S(2)}, u32[]{:S(2)}) collective-permute-start(f32[320,128]{1,0:T(8,128)S(1)} %get-tuple-element.32.coef2), channel_id=1, source_target_pairs={{0,128},{32,160},{64,192},{96,224},{128,0},{160,32},{192,64},{224,... | collective-permute-start | bytes 491528 | tf_op jit(solution)/shard_map/ppermute | solution.py:497
  20.1 1.1 %collective-permute-start.6 = (f32[320,128]{1,0:T(8,128)S(1)}, f32[320,128]{1,0:T(8,128)S(1)}, u32[]{:S(2)}, u32[]{:S(2)}) collective-permute-start(f32[320,128]{1,0:T(8,128)S(1)} %get-tuple-element.32.coef2), channel_id=1, source_target_pairs={{0,192},{32,224},{64,128},{96,160},{128,64},{160,96},{192,0},{224,... | collective-permute-start | bytes 491528 | tf_op jit(solution)/shard_map/ppermute | solution.py:497
  21.2 1.7 %shard_map.92 = (f32[2816,128]{1,0:T(8,128)S(1)}, f32[256,128]{1,0:T(8,128)S(1)}) custom-call(f32[8,256]{1,0:T(8,128)S(1)} %get-tuple-element.23.slot_row.token, f32[512,128]{1,0:T(8,128)} %bitcast.20, f32[512,128]{1,0:T(8,128)} %bitcast.22, f32[512,128]{1,0:T(8,128)} %bitcast.24, f32[256,128]{1,0:T(8,128)} %refs_3_.3, s32[256,128]{1,0:T(8,128)} %refs_4_.3), custom_call_target="tpu_custom_call" | custom-call | bytes 4194304 | tf_op jit(solution)/shard_map/pallas_call | solution.py:485
  22.9 9.0 %all-to-all-done = f32[1056,1,128]{2,1,0:T(1,128)S(1)} async-done(((f32[1056,1,128]{2,1,0:T(1,128)}), f32[1056,1,128]{2,1,0:T(1,128)S(1)}, u32[]{:S(2)}, u32[]{:S(2)}) %all-to-all-start) | async-done | bytes 540704 | tf_op jit(solution)/shard_map/all_to_all | solution.py:502
  31.9 0.9 %shard_map.94 = (f32[128,128]{1,0:T(8,128)S(1)}, f32[128,128]{1,0:T(8,128)S(1)}, f32[128,128]{1,0:T(8,128)S(1)}, f32[72,128]{1,0:T(8,128)S(1)}, f32[8,128]{1,0:T(8,128)S(1)}) custom-call(s32[1]{0:T(128)} %bitcast.narrow, f32[1056,128]{1,0:T(8,128)S(1)} %bitcast.16, f32[640,128]{1,0:T(8,128)S(1)} %get-tuple-element.27.level1, ...), custom_call_target="tpu_custom_call" | custom-call | tf_op jit(solution)/shard_map/pallas_call | solution.py:485
  32.8 0.1 collective-permute-start
  32.9 1.2 %collective-permute-done.other = f32[128,128]{1,0:T(8,128)S(1)} collective-permute-done((f32[128,128]{1,0:T(8,128)S(1)}, f32[128,128]{1,0:T(8,128)S(1)}, u32[]{:S(2)}, u32[]{:S(2)}) %collective-permute-start) | collective-permute-done | bytes 65568 | tf_op jit(solution)/shard_map/ppermute | solution.py:497
  34.1 0.2 shard_map.96
  34.3 3.1 %collective-permute-start.4 = (f32[128,128]{1,0:T(8,128)S(1)}, f32[128,128]{1,0:T(8,128)S(1)}, u32[]{:S(2)}, u32[]{:S(2)}) collective-permute-start(f32[128,128]{1,0:T(8,128)S(1)} %get-tuple-element.31.left2), channel_id=1, source_target_pairs={{0,128},{32,160},{64,192},{96,224},{128,0},{160,32},{192,64},{224,... | collective-permute-start | bytes 196616 | tf_op jit(solution)/shard_map/ppermute | solution.py:497
  37.5 1.1 %collective-permute-start.3 = (f32[128,128]{1,0:T(8,128)S(1)}, f32[128,128]{1,0:T(8,128)S(1)}, u32[]{:S(2)}, u32[]{:S(2)}) collective-permute-start(f32[128,128]{1,0:T(8,128)S(1)} %get-tuple-element.31.left2), channel_id=1, source_target_pairs={{0,192},{32,224},{64,128},{96,160},{128,64},{160,96},{192,0},{224,... | collective-permute-start | bytes 196616 | tf_op jit(solution)/shard_map/ppermute | solution.py:497
  38.6 0.0 collective-permute-done.7.coef2_c
  38.6 0.1 shard_map.97.levels
  38.8 0.3 shard_map.98
  39.1 1.1 %collective-permute-done.4.left2_c = f32[128,128]{1,0:T(8,128)S(1)} collective-permute-done((f32[128,128]{1,0:T(8,128)S(1)}, f32[128,128]{1,0:T(8,128)S(1)}, u32[]{:S(2)}, u32[]{:S(2)}) %collective-permute-start.4) | collective-permute-done | bytes 65568 | tf_op jit(solution)/shard_map/ppermute | solution.py:497
  40.2 2.7 %collective-permute-done.3.left2_b = f32[128,128]{1,0:T(8,128)S(1)} collective-permute-done((f32[128,128]{1,0:T(8,128)S(1)}, f32[128,128]{1,0:T(8,128)S(1)}, u32[]{:S(2)}, u32[]{:S(2)}) %collective-permute-start.3) | collective-permute-done | bytes 65568 | tf_op jit(solution)/shard_map/ppermute | solution.py:497
  42.9 1.5 %shard_map.99 = f32[1056,128]{1,0:T(8,128)S(1)} custom-call(f32[128,128]{1,0:T(8,128)S(1)} %get-tuple-element.31.left2, f32[128,128]{1,0:T(8,128)S(1)} %collective-permute-done.2.left2_a, f32[128,128]{1,0:T(8,128)S(1)} %collective-permute-done.3.left2_b, f32[128,128]{1,0:T(8,128)S(1)} %collective-permute-done.4.left2_c, f32[1920,128]{1,0:T(8,128)S(1)} %shard_map.97.levels, ...), custom_call_target="tpu_custom_call" | custom-call | tf_op jit(solution)/shard_map/pallas_call | solution.py:485
  44.4 21.5 %all_to_all.10 = f32[1056,1,128]{2,1,0:T(1,128)S(1)} all-to-all(f32[1056,1,128]{2,1,0:T(1,128)S(1)} %bitcast.17), channel_id=1, replica_groups=mesh['wide'=8,'narrow'=32] {'narrow'}, dimensions={0} | all-to-all | bytes 1081344 | tf_op jit(solution)/shard_map/all_to_all | solution.py:502
  65.9 1.5 %shard_map.100 = f32[512,128]{1,0:T(8,128)} custom-call(s32[1]{0:T(128)} %bitcast.narrow, f32[2816,128]{1,0:T(8,128)S(1)} %get-tuple-element.24.token.fine, f32[256,128]{1,0:T(8,128)S(1)} %get-tuple-element.25.slots, f32[1056,128]{1,0:T(8,128)S(1)} %bitcast.18, f32[88,128]{1,0:T(8,128)S(1)} %get-tuple-element.40.edges), custom_call_target="tpu_custom_call" | custom-call | tf_op jit(solution)/shard_map/pallas_call | solution.py:485
  (5 shorter events, 0.0 us)
Async XLA Ops:
  3.0 28.9 %all-to-all-start = ((f32[1056,1,128]{2,1,0:T(1,128)}), f32[1056,1,128]{2,1,0:T(1,128)S(1)}, u32[]{:S(2)}, u32[]{:S(2)}) async-start(f32[1056,1,128]{2,1,0:T(1,128)} %bitcast.6), calls=%async_computation | async-start | bytes 1081344 | tf_op jit(solution)/shard_map/all_to_all | solution.py:502
  15.4 1.5 %collective-permute-start.1 = (f32[320,128]{1,0:T(8,128)S(1)}, f32[320,128]{1,0:T(8,128)S(1)}, u32[]{:S(2)}, u32[]{:S(2)}) collective-permute-start(f32[320,128]{1,0:T(8,128)S(1)} %get-tuple-element.29.mine), channel_id=1, source_target_pairs={{0,32},{32,0},{64,96},{96,64},{128,160},{160,128},{192,224},{224,1... | collective-permute-start | bytes 491528 | tf_op jit(solution)/shard_map/ppermute | solution.py:497
  17.0 21.6 %collective-permute-start.7 = (f32[320,128]{1,0:T(8,128)S(1)}, f32[320,128]{1,0:T(8,128)S(1)}, u32[]{:S(2)}, u32[]{:S(2)}) collective-permute-start(f32[320,128]{1,0:T(8,128)S(1)} %get-tuple-element.32.coef2), channel_id=1, source_target_pairs={{0,128},{32,160},{64,192},{96,224},{128,0},{160,32},{192,64},{224,... | collective-permute-start | bytes 491528 | tf_op jit(solution)/shard_map/ppermute | solution.py:497
  20.1 18.5 %collective-permute-start.6 = (f32[320,128]{1,0:T(8,128)S(1)}, f32[320,128]{1,0:T(8,128)S(1)}, u32[]{:S(2)}, u32[]{:S(2)}) collective-permute-start(f32[320,128]{1,0:T(8,128)S(1)} %get-tuple-element.32.coef2), channel_id=1, source_target_pairs={{0,192},{32,224},{64,128},{96,160},{128,64},{160,96},{192,0},{224,... | collective-permute-start | bytes 491528 | tf_op jit(solution)/shard_map/ppermute | solution.py:497
  21.2 17.4 %collective-permute-start.5 = (f32[320,128]{1,0:T(8,128)S(1)}, f32[320,128]{1,0:T(8,128)S(1)}, u32[]{:S(2)}, u32[]{:S(2)}) collective-permute-start(f32[320,128]{1,0:T(8,128)S(1)} %get-tuple-element.32.coef2), channel_id=1, source_target_pairs={{0,64},{32,96},{64,0},{96,32},{128,192},{160,224},{192,128},{224,1... | collective-permute-start | bytes 491528 | tf_op jit(solution)/shard_map/ppermute | solution.py:497
  32.8 1.3 %collective-permute-start = (f32[128,128]{1,0:T(8,128)S(1)}, f32[128,128]{1,0:T(8,128)S(1)}, u32[]{:S(2)}, u32[]{:S(2)}) collective-permute-start(f32[128,128]{1,0:T(8,128)S(1)} %get-tuple-element.28.mine), channel_id=1, source_target_pairs={{0,32},{32,0},{64,96},{96,64},{128,160},{160,128},{192,224},{224,1... | collective-permute-start | bytes 196616 | tf_op jit(solution)/shard_map/ppermute | solution.py:497
  34.3 5.9 %collective-permute-start.4 = (f32[128,128]{1,0:T(8,128)S(1)}, f32[128,128]{1,0:T(8,128)S(1)}, u32[]{:S(2)}, u32[]{:S(2)}) collective-permute-start(f32[128,128]{1,0:T(8,128)S(1)} %get-tuple-element.31.left2), channel_id=1, source_target_pairs={{0,128},{32,160},{64,192},{96,224},{128,0},{160,32},{192,64},{224,... | collective-permute-start | bytes 196616 | tf_op jit(solution)/shard_map/ppermute | solution.py:497
  37.5 5.5 %collective-permute-start.3 = (f32[128,128]{1,0:T(8,128)S(1)}, f32[128,128]{1,0:T(8,128)S(1)}, u32[]{:S(2)}, u32[]{:S(2)}) collective-permute-start(f32[128,128]{1,0:T(8,128)S(1)} %get-tuple-element.31.left2), channel_id=1, source_target_pairs={{0,192},{32,224},{64,128},{96,160},{128,64},{160,96},{192,0},{224,... | collective-permute-start | bytes 196616 | tf_op jit(solution)/shard_map/ppermute | solution.py:497
  38.6 4.3 %collective-permute-start.2 = (f32[128,128]{1,0:T(8,128)S(1)}, f32[128,128]{1,0:T(8,128)S(1)}, u32[]{:S(2)}, u32[]{:S(2)}) collective-permute-start(f32[128,128]{1,0:T(8,128)S(1)} %get-tuple-element.31.left2), channel_id=1, source_target_pairs={{0,64},{32,96},{64,0},{96,32},{128,192},{160,224},{192,128},{224,1... | collective-permute-start | bytes 196616 | tf_op jit(solution)/shard_map/ppermute | solution.py:497

commit v4 on v3

--- a/solution.py
+++ b/solution.py
@@ -6,6 +6,7 @@
 from jax.sharding import PartitionSpec as P
 
 OMEGA = 0.8
+KEEP = 1.0 - OMEGA
 LANES = 128
 BLK = 256
 AGG = 64
@@ -46,31 +47,22 @@
         self.prev, self.nxt = prev, nxt
         self.faces = faces
         self.left = [prev(f) for f in faces] if left is None else left
-        self.diag = [s + l + f for s, l, f in zip(sinks, self.left, faces)]
-        self.coupling = coupling
-        scale = OMEGA / (self.diag[0] * self.diag[1] - coupling * coupling)
-        self.inv = (self.diag[1] * scale, self.diag[0] * scale, coupling * scale)
+        diag = [s + l + f for s, l, f in zip(sinks, self.left, faces)]
+        scale = OMEGA / (diag[0] * diag[1] - coupling * coupling)
+        self.inv = [diag[1] * scale, diag[0] * scale, coupling * scale]
 
     def parts(self):
-        return [*self.faces, *self.left, *self.inv, *self.diag, self.coupling]
+        return [*self.faces, *self.left, *self.inv]
 
     @classmethod
     def load(cls, part, prev, nxt):
         level = cls.__new__(cls)
         level.prev, level.nxt = prev, nxt
         level.faces, level.left, level.inv = part[0:2], part[2:4], part[4:7]
-        if len(part) > 7:
-            level.diag, level.coupling = part[7:9], part[9]
         return level
 
     def flow(self, v):
         return [self.left[f] * self.prev(v[f]) + self.faces[f] * self.nxt(v[f]) for f in (0, 1)]
-
-    def misfit(self, v, source):
-        cell = [
-            (source[f] - self.diag[f] * v[f]) + self.coupling * v[1 - f] for f in (0, 1)
-        ]
-        return [a + b for a, b in zip(cell, self.flow(v))]
 
     def step(self, r):
         return [
@@ -78,15 +70,19 @@
             self.inv[2] * r[0] + self.inv[1] * r[1],
         ]
 
-    def smooth(self, v, drive, sweeps):
-        for _ in range(sweeps):
-            d = self.step(self.flow(v))
-            v = [((1.0 - OMEGA) * v[f] + drive[f]) + d[f] for f in (0, 1)]
-        return v
-
-    def start(self, source, sweeps):
-        drive = self.step(source)
-        return self.smooth(drive, drive, sweeps - 1), drive
+    def begin(self, source):
+        g = self.step(source)
+        w = self.step(self.flow(g))
+        field = [(1.0 + KEEP) * a + b for a, b in zip(g, w)]
+        return field, [(2.0 * KEEP) * a + b for a, b in zip(g, w)]
+
+    def leftover(self, source, inner):
+        return [(KEEP * KEEP) * a + b for a, b in zip(source, self.flow(inner))]
+
+    def again(self, v, field):
+        u = self.step(self.flow(v))
+        d = self.step(self.flow([(2.0 * KEEP) * a + b for a, b in zip(v, u)]))
+        return [(field[f] + (KEEP * KEEP) * v[f]) + d[f] for f in (0, 1)]
 
 
 def store(ref, parts, at=0):
@@ -143,7 +139,7 @@
     coupling = kap[...] * jnp.sqrt(sinks[0] * sinks[1]) * live
     data = Level([f * both for f in planar(face, BLK)], sinks, coupling, chain_prev, chain_next)
     source = [r * live for r in planar(rhs, BLK)]
-    return data, source, *data.start(source, 2)
+    return data, coupling, source, *data.begin(source)
 
 
 def ready_kernel(slot_row, *refs):
@@ -152,8 +148,8 @@
     slots[...] = jnp.transpose(jnp.broadcast_to(slot_row[0:1, :], (LANES, BLK)), (1, 0))
     for copy in copies:
         copy.wait()
-    data, _, field, drive = fine_start(*held)
-    store(fine, [*field, *drive, *data.parts()[0:7]])
+    data, _, _, field, _ = fine_start(*held)
+    store(fine, [*field, *data.parts()])
 
 
 def pre_kernel(narrow, agg_hbm, *refs):
@@ -182,8 +178,8 @@
     )
     slots[...] = jnp.broadcast_to(slot.astype(F32), (8, BLK))
 
-    data, source, field, _ = fine_start(rhs, face, sink, kap, mask)
-    misfit = data.misfit(field, source)
+    data, coupling, source, _, inner = fine_start(rhs, face, sink, kap, mask)
+    misfit = data.leftover(source, inner)
     row, lane = iota((BLK, LANES), 0), iota((BLK, LANES), 1)
     drop = ((row == BLK - 1) & (lane >= LANES - 3) & (n < NARROW - 1)) | (
         (row == 0) & (lane < 3) & (n > 0)
@@ -215,7 +211,7 @@
     sinks = [
         ends(sink[2 * (BLK - 1) + f : 2 * (BLK - 1) + f + 1, :], sink[f : f + 1, :]) for f in (0, 1)
     ]
-    quantities = [*map(rows_of, source), *faces, *sinks, rows_of(data.coupling)]
+    quantities = [*map(rows_of, source), *faces, *sinks, rows_of(coupling)]
     edges = jnp.zeros((1, LANES), F32)
     for q, cells in enumerate(quantities):
         here = (lane1 >= 2 * SIDE * q) & (lane1 < 2 * SIDE * (q + 1))
@@ -251,16 +247,86 @@
     return Level(faces, sinks, quantity(6, 0.0), row_prev, row_next, left), source
 
 
-PARTS = 10
-
-
-def coarse_level(ref):
-    part = load(ref, 5, AGG)
-    return Level(part[0:2], part[2:4], part[4], chain_prev, chain_next)
-
-
-def ready_level(ref, at=0):
-    return Level.load(load(ref, PARTS, AGG, at * PARTS * AGG), chain_prev, chain_next)
+PARTS = 7
+REACH = (2, 1, 0, -1, -2)
+TWICE = 4 * len(REACH)
+LEVEL_ROWS = (PARTS + TWICE) * AGG
+
+
+def shifted(v, cells):
+    if cells == 0:
+        return v
+    moved = pltpu.roll(v, cells % LANES, 1)
+    lane = iota(v.shape, 1)
+    if cells > 0:
+        return jnp.where(lane < cells, pltpu.roll(moved, 1, 0), moved)
+    return jnp.where(lane >= LANES + cells, pltpu.roll(moved, v.shape[0] - 1, 0), moved)
+
+
+def product(a, b):
+    return [
+        a[0] * b[0] + a[1] * b[2],
+        a[0] * b[1] + a[1] * b[3],
+        a[2] * b[0] + a[3] * b[2],
+        a[2] * b[1] + a[3] * b[3],
+    ]
+
+
+def plus(a, b):
+    return [x + y for x, y in zip(a, b)]
+
+
+def apply_blocks(blocks, v):
+    total = [None, None]
+    terms = [[], []]
+    for k, cells in enumerate(REACH):
+        block, at = blocks[4 * k : 4 * k + 4], [shifted(x, cells) for x in v]
+        for f in (0, 1):
+            terms[f].append(block[2 * f] * at[0] + block[2 * f + 1] * at[1])
+    for f in (0, 1):
+        a, b, c, d, e = terms[f]
+        total[f] = c + ((a + b) + (d + e))
+    return total
+
+
+class Coarse:
+    @staticmethod
+    def build(coef, out, at=0, again=True):
+        part = load(coef, 5, AGG)
+        level = Level(part[0:2], part[2:4], part[4], chain_prev, chain_next)
+        store(out, level.parts(), at * LEVEL_ROWS)
+        if not again:
+            return
+        (l0, l1), (r0, r1), (i0, i1, i2) = level.left, level.faces, level.inv
+        from_left = [i0 * l0, i2 * l1, i2 * l0, i1 * l1]
+        from_right = [i0 * r0, i2 * r1, i2 * r0, i1 * r1]
+        left_before, right_before = ([chain_prev(x) for x in b] for b in (from_left, from_right))
+        left_after, right_after = ([chain_next(x) for x in b] for b in (from_left, from_right))
+        keep = jnp.full_like(l0, KEEP * KEEP)
+        zero = jnp.zeros_like(l0)
+        double = 2.0 * KEEP
+        twice = [
+            *product(from_left, left_before),
+            *[double * x for x in from_left],
+            *plus(
+                [keep, zero, zero, keep],
+                plus(product(from_left, right_before), product(from_right, left_after)),
+            ),
+            *[double * x for x in from_right],
+            *product(from_right, right_after),
+        ]
+        store(out, twice, at * LEVEL_ROWS + PARTS * AGG)
+
+    def __init__(self, ref, at=0):
+        self.ref, self.at = ref, at * LEVEL_ROWS
+        self.level = Level.load(load(ref, PARTS, AGG, self.at), chain_prev, chain_next)
+
+    def begin(self, source):
+        field, inner = self.level.begin(source)
+        return field, self.level.leftover(source, inner)
+
+    def again(self, v, field):
+        return plus(field, apply_blocks(load(self.ref, TWICE, AGG, self.at + PARTS * AGG), v))
 
 
 def store2(ref, v):
@@ -281,23 +347,23 @@
         out[f * AGG : (f + 1) * AGG, :] = jnp.where(last, 0.0, faces[f])
         out[(2 + f) * AGG : (3 + f) * AGG, :] = sinks[f]
     out[4 * AGG : 5 * AGG, :] = kap[...] * jnp.sqrt(sinks[0] * sinks[1])
-    store(level, coarse_level(out).parts())
+    Coarse.build(out, level)
 
 
 def pair_kernel(mine, other, out, level):
     out[...] = mine[...] + other[...]
-    store(level, coarse_level(out).parts())
+    Coarse.build(out, level)
 
 
 def upper_kernel(coef2, coef2_a, coef2_b, coef2_c, levels, near, far, top):
     near[...] = coef2[...] + coef2_a[...]
     far[...] = coef2_b[...] + coef2_c[...]
     top[...] = near[...] + far[...]
-    for k, ref in enumerate((near, far, top)):
-        store(levels, coarse_level(ref).parts(), k * PARTS * AGG)
-
-
-def restrict_kernel(narrow, recv, level1, token, leftover, below, drive_out, marks, own_edges):
+    for k, ref in enumerate((near, top, far)):
+        Coarse.build(ref, levels, k, ref is not far)
+
+
+def restrict_kernel(narrow, recv, level1, token, leftover, below, marks, own_edges):
     n = narrow[0]
     lane = iota((NARROW, LANES), 1)
     src = iota((NARROW, LANES), 0)
@@ -310,8 +376,8 @@
         from_end = from_end | ((lane >= 2 * SIDE * q) & (lane < 2 * SIDE * q + SIDE))
     cells = jnp.where(from_end, raw, pltpu.roll(raw, NARROW - 1, 0))
     data, source = interface_level(cells)
-    field, _ = data.start(source, 2)
-    mis = [pltpu.roll(m, LANES - SIDE, 1) for m in data.misfit(field, source)]
+    _, inner = data.begin(source)
+    mis = [pltpu.roll(m, LANES - SIDE, 1) for m in data.leftover(source, inner)]
     mis = jnp.concatenate(mis, axis=1)
     wide_lane = iota((NARROW, 2 * LANES), 1) % LANES
     real = iota((NARROW, 2 * LANES), 0) < NARROW - 1
@@ -351,11 +417,9 @@
             as_bf16(jnp.concatenate(hots, axis=1)), jnp.concatenate(parts, axis=0)
         )
     source_c = [total[:, 0:LANES], total[:, LANES:]]
-    level = ready_level(level1)
-    correction, drive = level.start(source_c, 2)
-    store2(leftover, level.misfit(correction, source_c))
+    correction, rest = Coarse(level1).begin(source_c)
+    store2(leftover, rest)
     store2(below, correction)
-    store2(drive_out, drive)
 
     for t in range(NARROW // 8):
         marks[t : t + 1, :] = rows[t].astype(F32)
@@ -365,13 +429,11 @@
     own_edges[1:2, :] = jnp.sum(jnp.where(src == n, cells, 0.0), axis=0, keepdims=True)
 
 
-def second_kernel(mine, other, level2, leftover, below, drive_out):
+def second_kernel(mine, other, level2, leftover, below):
     source = [a + b for a, b in zip(load2(mine), load2(other))]
-    level = ready_level(level2)
-    correction, drive = level.start(source, 2)
-    store2(leftover, level.misfit(correction, source))
+    correction, rest = Coarse(level2).begin(source)
+    store2(leftover, rest)
     store2(below, correction)
-    store2(drive_out, drive)
 
 
 def side_kernel(marks, own_edges, hot, edges):
@@ -387,28 +449,26 @@
     hot[NARROW * CAP :, 0:LANES] = (ends + pltpu.roll(ends, AGG, 1)).astype(BF16)
     hot[NARROW * CAP :, LANES:] = ends.astype(BF16)
     data, source = interface_level(own_edges[...])
-    field, drive = data.start(source, 2)
-    store(edges, [*field, *drive, *data.parts()[0:7]])
+    field, _ = data.begin(source)
+    store(edges, [*field, *data.parts()])
 
 
 def top_kernel(
-    left2, left2_a, left2_b, left2_c, levels, level2, below2, drive2, level1, below1, drive1, hot, out
+    left2, left2_a, left2_b, left2_c, levels, level2, below2, level1, below1, hot, out
 ):
     source3 = [a + b for a, b in zip(load2(left2), load2(left2_a))]
     source3_far = [a + b for a, b in zip(load2(left2_b), load2(left2_c))]
-    level3, level3_far, level4 = [ready_level(levels, k) for k in range(3)]
-    below3, drive3 = level3.start(source3, 2)
-    below3_far, _ = level3_far.start(source3_far, 2)
-    source4 = [
-        a + b
-        for a, b in zip(
-            level3.misfit(below3, source3), level3_far.misfit(below3_far, source3_far)
-        )
-    ]
-    v, _ = level4.start(source4, 4)
-    v = level3.smooth([a + b for a, b in zip(below3, v)], drive3, 2)
-    v = ready_level(level2).smooth([a + b for a, b in zip(load2(below2), v)], load2(drive2), 2)
-    v = ready_level(level1).smooth([a + b for a, b in zip(load2(below1), v)], load2(drive1), 2)
+    level3, level4, level3_far = [Coarse(levels, k) for k in range(3)]
+    below3, rest = level3.begin(source3)
+    _, rest_far = level3_far.begin(source3_far)
+    v, _ = level4.begin(plus(rest, rest_far))
+    v = level4.again(v, v)
+    for level, field in (
+        (level3, below3),
+        (Coarse(level2), load2(below2)),
+        (Coarse(level1), load2(below1)),
+    ):
+        v = level.again(plus(field, v), field)
 
     both = jnp.concatenate([v[0], v[1]], axis=1)
     both = jnp.concatenate([*split3(both), jnp.zeros((AGG, 2 * LANES), BF16)], axis=0)
@@ -432,8 +492,8 @@
 
 def post_kernel(narrow, fine, slots, recv, edges, out):
     n = narrow[0]
-    field, drive = load(fine, 2, BLK), load(fine, 2, BLK, 2 * BLK)
-    data = Level.load(load(fine, 7, BLK, 4 * BLK), chain_prev, chain_next)
+    field = load(fine, 2, BLK)
+    data = Level.load(load(fine, PARTS, BLK, 2 * BLK), chain_prev, chain_next)
     slot = slots[...].astype(I32)
     lane = iota((BLK, LANES), 1)
     lifted = None
@@ -450,10 +510,10 @@
         term = select_rows(as_bf16(jnp.concatenate(hots, axis=1)), jnp.concatenate(parts, axis=0))
         lifted = term if lifted is None else lifted + term
     lifted = [lifted[:, 0:LANES], lifted[:, LANES:]]
-    v = data.smooth([a + b for a, b in zip(field, lifted)], drive, 2)
-
-    edge_field, edge_drive = load(edges, 2, 8), load(edges, 2, 8, 16)
-    edge_data = Level.load(load(edges, 7, 8, 32), row_prev, row_next)
+    v = data.again([a + b for a, b in zip(field, lifted)], field)
+
+    edge_field = load(edges, 2, 8)
+    edge_data = Level.load(load(edges, PARTS, 8, 16), row_prev, row_next)
     lane1 = iota((1, LANES), 1)
     row8 = iota((8, LANES), 0)
     edge_v = []
@@ -465,7 +525,7 @@
         lift = jnp.where(row8 == 0, first, jnp.where(row8 == 1, final, 0.0))
         lift = jnp.where(iota((8, LANES), 1) < 2 * SIDE, pltpu.roll(lift, SIDE, 1), 0.0)
         edge_v.append(edge_field[f] + lift)
-    edge_v = edge_data.smooth(edge_v, edge_drive, 2)
+    edge_v = edge_data.again(edge_v, edge_field)
     for f in (0, 1):
         out[pl.ds(f, BLK, stride=2), :] = v[f]
         moved = pltpu.roll(edge_v[f], LANES - SIDE, 1)
@@ -508,7 +568,7 @@
 ):
     narrow = lax.axis_index("narrow").astype(I32).reshape(1)
     cells = ((2 * BLK, LANES), F32)
-    five, level, two = ((k * AGG, LANES) for k in (5, PARTS, 2))
+    five, level, two = (5 * AGG, LANES), (LEVEL_ROWS, LANES), (2 * AGG, LANES)
     five, level, two = (five, F32), (level, F32), (two, F32)
     units = ((NARROW * UNIT, LANES), F32)
     vmem = lambda *rows: [pltpu.VMEM((r, LANES), F32) for r in rows]
@@ -544,7 +604,7 @@
     )
     fine, slots = call(
         ready_kernel,
-        [((11 * BLK, LANES), F32), ((BLK, LANES), F32)],
+        [((9 * BLK, LANES), F32), ((BLK, LANES), F32)],
         slot_row,
         *fine_args,
         spaces=(pltpu.VMEM, *[pltpu.HBM] * 5),
@@ -554,15 +614,15 @@
     coef2, level2 = call(pair_kernel, [five, level], coef1, exchange(coef1, 1), cost=beside)
     (levels,) = call(
         upper_kernel,
-        [((3 * PARTS * AGG, LANES), F32)],
+        [((2 * LEVEL_ROWS + PARTS * AGG, LANES), F32)],
         coef2,
         *[exchange(coef2, b) for b in (2, 6, 4)],
         scratch=vmem(5 * AGG, 5 * AGG, 5 * AGG),
         cost=beside,
     )
-    left1, below1, drive1, marks, own_edges = call(
+    left1, below1, marks, own_edges = call(
         restrict_kernel,
-        [two, two, two, ((8 + 2 * NARROW, LANES), F32), ((8, LANES), F32)],
+        [two, two, ((8 + 2 * NARROW, LANES), F32), ((8, LANES), F32)],
         narrow,
         recv,
         level1,
@@ -571,12 +631,12 @@
     )
     hot, edges = call(
         side_kernel,
-        [((NARROW * CAP + 2 * NARROW, 2 * LANES), BF16), ((11 * 8, LANES), F32)],
+        [((NARROW * CAP + 2 * NARROW, 2 * LANES), BF16), ((9 * 8, LANES), F32)],
         marks,
         own_edges,
     )
-    left2, below2, drive2 = call(
-        second_kernel, [two, two, two], left1, exchange(left1, 1), level2
+    left2, below2 = call(
+        second_kernel, [two, two], left1, exchange(left1, 1), level2
     )
     (back,) = call(
         top_kernel,
@@ -586,10 +646,8 @@
         levels,
         level2,
         below2,
-        drive2,
         level1,
         below1,
-        drive1,
         hot,
     )
     recv = to_all(back)

time: 68 us -> 68 us (level)
  waiting for transfers between devices: 15.4 us -> 13 us
  Pallas kernels: 10.3 us -> 12.7 us
    pallas_call x10, Pallas kernels: 10.3 us -> 12.7 us  [call(): pl.pallas_call(kernel, out_shape=[jax.ShapeDtypeStruct(s, k) for s, k in...]
    all_to_all x1, waiting for transfers between devices: 8.95 us -> 7.31 us  [to_all(): moved = lax.all_to_all(units.reshape(shape), 'narrow', 0, 0, tiled=True)]
    ppermute x8, waiting for transfers between devices: 6.44 us -> 5.68 us  [exchange(): lax.ppermute(value, 'wide', [(i, i ^ bits) for i in range(lax.axis_size('...]
  transfers between devices with their start and end apart: 9 -> 9, of which waited for: 5 -> 5; matrix products, arithmetic and copies ran while one was open for 0% -> 0% of each run, Pallas kernels for 7% -> 10%
where the time goes in v4:
time: 68 us; the launch traced here: 67.7 us
  blocking collectives  21.2 us (31%)
  starting transfers between devices  20.1 us (30%)
  waiting for transfers between devices  13 us (19%)
  Pallas kernels  12.7 us (19%)
    all_to_all x1, blocking collectives, to_all(): moved = lax.all_to_all(units.reshape(shape), 'narrow', 0, 0, tiled=True)  21.2 us
    pallas_call x10, Pallas kernels, call(): pl.pallas_call(kernel, out_shape=[jax.ShapeDtypeStruct(s, k) for s, k in...  12.7 us
    all_to_all x1, starting transfers between devices, to_all(): moved = lax.all_to_all(units.reshape(shape), 'narrow', 0, 0, tiled=True)  11.4 us
    ppermute x8, starting transfers between devices, exchange(): lax.ppermute(value, 'wide', [(i, i ^ bits) for i in range(lax.axis_size('...  8.72 us
    all_to_all x1, waiting for transfers between devices, to_all(): moved = lax.all_to_all(units.reshape(shape), 'narrow', 0, 0, tiled=True)  7.31 us
    ppermute x8, waiting for transfers between devices, exchange(): lax.ppermute(value, 'wide', [(i, i ^ bits) for i in range(lax.axis_size('...  5.68 us
  transfers between devices with their start and end apart: 9, of which 5 were waited for; matrix products, arithmetic and copies ran while one was open for 0% of the time, Pallas kernels for 10%

profile of v4, /device:TPU:32, one launch (start us, length us, event | category | flops | bytes accessed | tf_op | source)
XLA Modules:
  0.0 67.7 jit_solution(681675437821755671)
XLA Ops:
  0.0 3.0 %shard_map.91 = (f32[1056,128]{1,0:T(8,128)}, f32[8,256]{1,0:T(8,128)S(1)}) custom-call(s32[1]{0:T(128)} %bitcast.narrow, s32[1,256]{1,0:T(1,128)} %bitcast.27, f32[512,128]{1,0:T(8,128)} %bitcast.19, f32[512,128]{1,0:T(8,128)} %bitcast.21, f32[512,128]{1,0:T(8,128)} %bitcast.23, f32[256,128]{1,0:T(8,128)} %refs_3_.3, s32[256,128]{1,0:T(8,128)} %refs_4_.3), custom_call_target="tpu_custom_call" | custom-call | tf_op jit(solution)/shard_map/pallas_call | solution.py:545
  3.0 11.4 %all-to-all-start = ((f32[1056,1,128]{2,1,0:T(1,128)}), f32[1056,1,128]{2,1,0:T(1,128)S(1)}, u32[]{:S(2)}, u32[]{:S(2)}) async-start(f32[1056,1,128]{2,1,0:T(1,128)} %bitcast.6), calls=%async_computation | async-start | bytes 1081344 | tf_op jit(solution)/shard_map/all_to_all | solution.py:562
  14.4 1.2 %shard_map.93 = (f32[320,128]{1,0:T(8,128)S(1)}, f32[1728,128]{1,0:T(8,128)S(1)}) custom-call(f32[8,256]{1,0:T(8,128)S(1)} %get-tuple-element.21.slot_row.token, f32[128,128]{1,0:T(8,128)} %bitcast.25, f32[128,128]{1,0:T(8,128)} %bitcast.26, f32[64,128]{1,0:T(8,128)} %kap_hbm.1), custom_call_target="tpu_custom_call" | custom-call | bytes 4194304 | tf_op jit(solution)/shard_map/pallas_call | solution.py:545
  15.7 1.4 %collective-permute-done.1.other = f32[320,128]{1,0:T(8,128)S(1)} collective-permute-done((f32[320,128]{1,0:T(8,128)S(1)}, f32[320,128]{1,0:T(8,128)S(1)}, u32[]{:S(2)}, u32[]{:S(2)}) %collective-permute-start.1) | collective-permute-done | bytes 163872 | tf_op jit(solution)/shard_map/ppermute | solution.py:557
  17.1 0.9 %shard_map.95 = (f32[320,128]{1,0:T(8,128)}, f32[1728,128]{1,0:T(8,128)S(1)}) custom-call(f32[320,128]{1,0:T(8,128)S(1)} %get-tuple-element.27.mine, f32[320,128]{1,0:T(8,128)S(1)} %collective-permute-done.1.other), custom_call_target="tpu_custom_call" | custom-call | bytes 4194304 | tf_op jit(solution)/shard_map/pallas_call | solution.py:545
  18.0 1.5 %collective-permute-start.5 = (f32[320,128]{1,0:T(8,128)}, f32[320,128]{1,0:T(8,128)}, u32[]{:S(2)}, u32[]{:S(2)}) collective-permute-start(f32[320,128]{1,0:T(8,128)} %get-tuple-element.30.coef2), channel_id=1, source_target_pairs={{0,64},{32,96},{64,0},{96,32},{128,192},{160,224},{192,128},{224,1... | collective-permute-start | bytes 491528 | tf_op jit(solution)/shard_map/ppermute | solution.py:557
  19.5 2.1 %collective-permute-start.6 = (f32[320,128]{1,0:T(8,128)}, f32[320,128]{1,0:T(8,128)}, u32[]{:S(2)}, u32[]{:S(2)}) collective-permute-start(f32[320,128]{1,0:T(8,128)} %get-tuple-element.30.coef2), channel_id=1, source_target_pairs={{0,192},{32,224},{64,128},{96,160},{128,64},{160,96},{192,0},{224,... | collective-permute-start | bytes 491528 | tf_op jit(solution)/shard_map/ppermute | solution.py:557
  21.6 0.6 collective-permute-start.7
  22.2 1.7 %shard_map.92 = (f32[2304,128]{1,0:T(8,128)S(1)}, f32[256,128]{1,0:T(8,128)S(1)}) custom-call(f32[8,256]{1,0:T(8,128)S(1)} %get-tuple-element.21.slot_row.token, f32[512,128]{1,0:T(8,128)} %bitcast.20, f32[512,128]{1,0:T(8,128)} %bitcast.22, f32[512,128]{1,0:T(8,128)} %bitcast.24, f32[256,128]{1,0:T(8,128)} %refs_3_.3, s32[256,128]{1,0:T(8,128)} %refs_4_.3), custom_call_target="tpu_custom_call" | custom-call | bytes 4194304 | tf_op jit(solution)/shard_map/pallas_call | solution.py:545
  23.9 0.6 copy-done
  24.6 7.3 %all-to-all-done = f32[1056,1,128]{2,1,0:T(1,128)S(1)} async-done(((f32[1056,1,128]{2,1,0:T(1,128)}), f32[1056,1,128]{2,1,0:T(1,128)S(1)}, u32[]{:S(2)}, u32[]{:S(2)}) %all-to-all-start) | async-done | bytes 540704 | tf_op jit(solution)/shard_map/all_to_all | solution.py:562
  31.9 0.9 %shard_map.94 = (f32[128,128]{1,0:T(8,128)S(1)}, f32[128,128]{1,0:T(8,128)S(1)}, f32[72,128]{1,0:T(8,128)S(1)}, f32[8,128]{1,0:T(8,128)S(1)}) custom-call(s32[1]{0:T(128)} %bitcast.narrow, f32[1056,128]{1,0:T(8,128)S(1)} %bitcast.18, f32[1728,128]{1,0:T(8,128)S(1)} %get-tuple-element.25.level1, f32[2304,128]{1,0:T(8,128)S(1)} %get-tuple-element.22.token.fine), custom_call_target="tpu_custom_call" | custom-call | tf_op jit(solution)/shard_map/pallas_call | solution.py:545
  32.9 1.2 %collective-permute-done.other = f32[128,128]{1,0:T(8,128)S(1)} collective-permute-done((f32[128,128]{1,0:T(8,128)S(1)}, f32[128,128]{1,0:T(8,128)S(1)}, u32[]{:S(2)}, u32[]{:S(2)}) %collective-permute-start) | collective-permute-done | bytes 65568 | tf_op jit(solution)/shard_map/ppermute | solution.py:557
  34.1 0.2 shard_map.96
  34.3 1.6 %collective-permute-start.2 = (f32[128,128]{1,0:T(8,128)S(1)}, f32[128,128]{1,0:T(8,128)S(1)}, u32[]{:S(2)}, u32[]{:S(2)}) collective-permute-start(f32[128,128]{1,0:T(8,128)S(1)} %get-tuple-element.29.left2), channel_id=1, source_target_pairs={{0,64},{32,96},{64,0},{96,32},{128,192},{160,224},{192,128},{224,1... | collective-permute-start | bytes 196616 | tf_op jit(solution)/shard_map/ppermute | solution.py:557
  35.9 2.1 %collective-permute-start.3 = (f32[128,128]{1,0:T(8,128)S(1)}, f32[128,128]{1,0:T(8,128)S(1)}, u32[]{:S(2)}, u32[]{:S(2)}) collective-permute-start(f32[128,128]{1,0:T(8,128)S(1)} %get-tuple-element.29.left2), channel_id=1, source_target_pairs={{0,192},{32,224},{64,128},{96,160},{128,64},{160,96},{192,0},{224,... | collective-permute-start | bytes 196616 | tf_op jit(solution)/shard_map/ppermute | solution.py:557
  38.0 0.6 collective-permute-start.4
  38.7 1.7 %shard_map.97.levels = f32[3904,128]{1,0:T(8,128)S(1)} custom-call(f32[320,128]{1,0:T(8,128)} %get-tuple-element.30.coef2, f32[320,128]{1,0:T(8,128)} %collective-permute-done.5.coef2_a, f32[320,128]{1,0:T(8,128)} %collective-permute-done.6.coef2_b, f32[320,128]{1,0:T(8,128)} %collective-permute-done.7.coef2_c), custom_call_target="tpu_custom_call" | custom-call | bytes 4194304 | tf_op jit(solution)/shard_map/pallas_call | solution.py:545
  40.4 0.3 shard_map.98
  40.7 0.6 collective-permute-done.3.left2_b
  41.4 2.4 %collective-permute-done.4.left2_c = f32[128,128]{1,0:T(8,128)S(1)} collective-permute-done((f32[128,128]{1,0:T(8,128)S(1)}, f32[128,128]{1,0:T(8,128)S(1)}, u32[]{:S(2)}, u32[]{:S(2)}) %collective-permute-start.4) | collective-permute-done | bytes 65568 | tf_op jit(solution)/shard_map/ppermute | solution.py:557
  43.8 1.2 %shard_map.99 = f32[1056,128]{1,0:T(8,128)S(1)} custom-call(f32[128,128]{1,0:T(8,128)S(1)} %get-tuple-element.29.left2, f32[128,128]{1,0:T(8,128)S(1)} %collective-permute-done.2.left2_a, f32[128,128]{1,0:T(8,128)S(1)} %collective-permute-done.3.left2_b, f32[128,128]{1,0:T(8,128)S(1)} %collective-permute-done.4.left2_c, f32[3904,128]{1,0:T(8,128)S(1)} %shard_map.97.levels, ...), custom_call_target="tpu_custom_call" | custom-call | tf_op jit(solution)/shard_map/pallas_call | solution.py:545
  45.0 21.2 %all_to_all.10 = f32[1056,1,128]{2,1,0:T(1,128)S(1)} all-to-all(f32[1056,1,128]{2,1,0:T(1,128)S(1)} %bitcast.16), channel_id=1, replica_groups=mesh['wide'=8,'narrow'=32] {'narrow'}, dimensions={0} | all-to-all | bytes 1081344 | tf_op jit(solution)/shard_map/all_to_all | solution.py:562
  66.2 1.5 %shard_map.100 = f32[512,128]{1,0:T(8,128)} custom-call(s32[1]{0:T(128)} %bitcast.narrow, f32[2304,128]{1,0:T(8,128)S(1)} %get-tuple-element.22.token.fine, f32[256,128]{1,0:T(8,128)S(1)} %copy-done.1, f32[1056,128]{1,0:T(8,128)S(1)} %bitcast.17, f32[72,128]{1,0:T(8,128)S(1)} %get-tuple-element.36.edges), custom_call_target="tpu_custom_call" | custom-call | tf_op jit(solution)/shard_map/pallas_call | solution.py:545
  (9 shorter events, 0.2 us)
Async XLA Ops:
  3.0 28.9 %all-to-all-start = ((f32[1056,1,128]{2,1,0:T(1,128)}), f32[1056,1,128]{2,1,0:T(1,128)S(1)}, u32[]{:S(2)}, u32[]{:S(2)}) async-start(f32[1056,1,128]{2,1,0:T(1,128)} %bitcast.6), calls=%async_computation | async-start | bytes 1081344 | tf_op jit(solution)/shard_map/all_to_all | solution.py:562
  15.6 1.5 %collective-permute-start.1 = (f32[320,128]{1,0:T(8,128)S(1)}, f32[320,128]{1,0:T(8,128)S(1)}, u32[]{:S(2)}, u32[]{:S(2)}) collective-permute-start(f32[320,128]{1,0:T(8,128)S(1)} %get-tuple-element.27.mine), channel_id=1, source_target_pairs={{0,32},{32,0},{64,96},{96,64},{128,160},{160,128},{192,224},{224,1... | collective-permute-start | bytes 491528 | tf_op jit(solution)/shard_map/ppermute | solution.py:557
  18.0 20.0 %collective-permute-start.5 = (f32[320,128]{1,0:T(8,128)}, f32[320,128]{1,0:T(8,128)}, u32[]{:S(2)}, u32[]{:S(2)}) collective-permute-start(f32[320,128]{1,0:T(8,128)} %get-tuple-element.30.coef2), channel_id=1, source_target_pairs={{0,64},{32,96},{64,0},{96,32},{128,192},{160,224},{192,128},{224,1... | collective-permute-start | bytes 491528 | tf_op jit(solution)/shard_map/ppermute | solution.py:557
  19.5 19.2 %collective-permute-start.6 = (f32[320,128]{1,0:T(8,128)}, f32[320,128]{1,0:T(8,128)}, u32[]{:S(2)}, u32[]{:S(2)}) collective-permute-start(f32[320,128]{1,0:T(8,128)} %get-tuple-element.30.coef2), channel_id=1, source_target_pairs={{0,192},{32,224},{64,128},{96,160},{128,64},{160,96},{192,0},{224,... | collective-permute-start | bytes 491528 | tf_op jit(solution)/shard_map/ppermute | solution.py:557
  21.6 17.1 %collective-permute-start.7 = (f32[320,128]{1,0:T(8,128)}, f32[320,128]{1,0:T(8,128)}, u32[]{:S(2)}, u32[]{:S(2)}) collective-permute-start(f32[320,128]{1,0:T(8,128)} %get-tuple-element.30.coef2), channel_id=1, source_target_pairs={{0,128},{32,160},{64,192},{96,224},{128,0},{160,32},{192,64},{224,... | collective-permute-start | bytes 491528 | tf_op jit(solution)/shard_map/ppermute | solution.py:557
  23.9 0.7 copy-start
  32.8 1.3 %collective-permute-start = (f32[128,128]{1,0:T(8,128)S(1)}, f32[128,128]{1,0:T(8,128)S(1)}, u32[]{:S(2)}, u32[]{:S(2)}) collective-permute-start(f32[128,128]{1,0:T(8,128)S(1)} %get-tuple-element.26.mine), channel_id=1, source_target_pairs={{0,32},{32,0},{64,96},{96,64},{128,160},{160,128},{192,224},{224,1... | collective-permute-start | bytes 196616 | tf_op jit(solution)/shard_map/ppermute | solution.py:557
  34.3 6.4 %collective-permute-start.2 = (f32[128,128]{1,0:T(8,128)S(1)}, f32[128,128]{1,0:T(8,128)S(1)}, u32[]{:S(2)}, u32[]{:S(2)}) collective-permute-start(f32[128,128]{1,0:T(8,128)S(1)} %get-tuple-element.29.left2), channel_id=1, source_target_pairs={{0,64},{32,96},{64,0},{96,32},{128,192},{160,224},{192,128},{224,1... | collective-permute-start | bytes 196616 | tf_op jit(solution)/shard_map/ppermute | solution.py:557
  35.9 5.5 %collective-permute-start.3 = (f32[128,128]{1,0:T(8,128)S(1)}, f32[128,128]{1,0:T(8,128)S(1)}, u32[]{:S(2)}, u32[]{:S(2)}) collective-permute-start(f32[128,128]{1,0:T(8,128)S(1)} %get-tuple-element.29.left2), channel_id=1, source_target_pairs={{0,192},{32,224},{64,128},{96,160},{128,64},{160,96},{192,0},{224,... | collective-permute-start | bytes 196616 | tf_op jit(solution)/shard_map/ppermute | solution.py:557
  38.0 5.8 %collective-permute-start.4 = (f32[128,128]{1,0:T(8,128)S(1)}, f32[128,128]{1,0:T(8,128)S(1)}, u32[]{:S(2)}, u32[]{:S(2)}) collective-permute-start(f32[128,128]{1,0:T(8,128)S(1)} %get-tuple-element.29.left2), channel_id=1, source_target_pairs={{0,128},{32,160},{64,192},{96,224},{128,0},{160,32},{192,64},{224,... | collective-permute-start | bytes 196616 | tf_op jit(solution)/shard_map/ppermute | solution.py:557
  43.8 22.4 %copy-start.1 = (f32[256,128]{1,0:T(8,128)S(1)}, f32[256,128]{1,0:T(8,128)}, u32[]{:S(2)}) copy-start(f32[256,128]{1,0:T(8,128)} %copy-done) | copy-start | bytes 393220

commit v5 on v4

--- a/solution.py
+++ b/solution.py
@@ -248,7 +248,7 @@
 
 
 PARTS = 7
-REACH = (2, 1, 0, -1, -2)
+REACH = (2, 0, -2)
 TWICE = 4 * len(REACH)
 LEVEL_ROWS = (PARTS + TWICE) * AGG
 
@@ -277,16 +277,11 @@
 
 
 def apply_blocks(blocks, v):
-    total = [None, None]
-    terms = [[], []]
+    terms = []
     for k, cells in enumerate(REACH):
         block, at = blocks[4 * k : 4 * k + 4], [shifted(x, cells) for x in v]
-        for f in (0, 1):
-            terms[f].append(block[2 * f] * at[0] + block[2 * f + 1] * at[1])
-    for f in (0, 1):
-        a, b, c, d, e = terms[f]
-        total[f] = c + ((a + b) + (d + e))
-    return total
+        terms.append([block[2 * f] * at[0] + block[2 * f + 1] * at[1] for f in (0, 1)])
+    return plus(terms[1], plus(terms[0], terms[2]))
 
 
 class Coarse:
@@ -304,15 +299,12 @@
         left_after, right_after = ([chain_next(x) for x in b] for b in (from_left, from_right))
         keep = jnp.full_like(l0, KEEP * KEEP)
         zero = jnp.zeros_like(l0)
-        double = 2.0 * KEEP
         twice = [
             *product(from_left, left_before),
-            *[double * x for x in from_left],
             *plus(
                 [keep, zero, zero, keep],
                 plus(product(from_left, right_before), product(from_right, left_after)),
             ),
-            *[double * x for x in from_right],
             *product(from_right, right_after),
         ]
         store(out, twice, at * LEVEL_ROWS + PARTS * AGG)
@@ -326,7 +318,9 @@
         return field, self.level.leftover(source, inner)
 
     def again(self, v, field):
-        return plus(field, apply_blocks(load(self.ref, TWICE, AGG, self.at + PARTS * AGG), v))
+        near = self.level.step(self.level.flow(v))
+        far = apply_blocks(load(self.ref, TWICE, AGG, self.at + PARTS * AGG), v)
+        return [(field[f] + far[f]) + (2.0 * KEEP) * near[f] for f in (0, 1)]
 
 
 def store2(ref, v):

time: 68 us -> 67.8 us (level)
  Pallas kernels: 12.7 us -> 11.8 us
    pallas_call x10, Pallas kernels: 12.7 us -> 11.8 us  [call(): pl.pallas_call(kernel, out_shape=[jax.ShapeDtypeStruct(s, k) for s, k in...]
  transfers between devices with their start and end apart: 9 -> 9, of which waited for: 5 -> 4; matrix products, arithmetic and copies ran while one was open for 0% -> 0% of each run, Pallas kernels for 10% -> 9%
where the time goes in v5:
time: 67.8 us; the launch traced here: 67.1 us
  blocking collectives  21.5 us (32%)
  starting transfers between devices  20.1 us (30%)
  waiting for transfers between devices  13 us (19%)
  Pallas kernels  11.8 us (17%)
    all_to_all x1, blocking collectives, to_all(): moved = lax.all_to_all(units.reshape(shape), 'narrow', 0, 0, tiled=True)  21.5 us
    pallas_call x10, Pallas kernels, call(): pl.pallas_call(kernel, out_shape=[jax.ShapeDtypeStruct(s, k) for s, k in...  11.8 us
    all_to_all x1, starting transfers between devices, to_all(): moved = lax.all_to_all(units.reshape(shape), 'narrow', 0, 0, tiled=True)  11.4 us
    ppermute x8, starting transfers between devices, exchange(): lax.ppermute(value, 'wide', [(i, i ^ bits) for i in range(lax.axis_size('...  8.7 us
    all_to_all x1, waiting for transfers between devices, to_all(): moved = lax.all_to_all(units.reshape(shape), 'narrow', 0, 0, tiled=True)  7.88 us
    ppermute x8, waiting for transfers between devices, exchange(): lax.ppermute(value, 'wide', [(i, i ^ bits) for i in range(lax.axis_size('...  5.12 us
  transfers between devices with their start and end apart: 9, of which 4 were waited for; matrix products, arithmetic and copies ran while one was open for 0% of the time, Pallas kernels for 9%

profile of v5, /device:TPU:32, one launch (start us, length us, event | category | flops | bytes accessed | tf_op | source)
XLA Modules:
  0.0 67.1 jit_solution(7753258868830380980)
XLA Ops:
  0.0 3.0 %shard_map.91 = (f32[1056,128]{1,0:T(8,128)}, f32[8,256]{1,0:T(8,128)S(1)}) custom-call(s32[1]{0:T(128)} %bitcast.narrow, s32[1,256]{1,0:T(1,128)} %bitcast.27, f32[512,128]{1,0:T(8,128)} %bitcast.19, f32[512,128]{1,0:T(8,128)} %bitcast.21, f32[512,128]{1,0:T(8,128)} %bitcast.23, f32[256,128]{1,0:T(8,128)} %refs_3_.3, s32[256,128]{1,0:T(8,128)} %refs_4_.3), custom_call_target="tpu_custom_call" | custom-call | tf_op jit(solution)/shard_map/pallas_call | solution.py:539
  3.0 11.4 %all-to-all-start = ((f32[1056,1,128]{2,1,0:T(1,128)}), f32[1056,1,128]{2,1,0:T(1,128)S(1)}, u32[]{:S(2)}, u32[]{:S(2)}) async-start(f32[1056,1,128]{2,1,0:T(1,128)} %bitcast.6), calls=%async_computation | async-start | bytes 1081344 | tf_op jit(solution)/shard_map/all_to_all | solution.py:556
  14.4 1.2 %shard_map.93 = (f32[320,128]{1,0:T(8,128)S(1)}, f32[1216,128]{1,0:T(8,128)S(1)}) custom-call(f32[8,256]{1,0:T(8,128)S(1)} %get-tuple-element.21.slot_row.token, f32[128,128]{1,0:T(8,128)} %bitcast.25, f32[128,128]{1,0:T(8,128)} %bitcast.26, f32[64,128]{1,0:T(8,128)} %kap_hbm.1), custom_call_target="tpu_custom_call" | custom-call | bytes 4194304 | tf_op jit(solution)/shard_map/pallas_call | solution.py:539
  15.6 0.1 collective-permute-start.1
  15.7 1.4 %collective-permute-done.1.other = f32[320,128]{1,0:T(8,128)S(1)} collective-permute-done((f32[320,128]{1,0:T(8,128)S(1)}, f32[320,128]{1,0:T(8,128)S(1)}, u32[]{:S(2)}, u32[]{:S(2)}) %collective-permute-start.1) | collective-permute-done | bytes 163872 | tf_op jit(solution)/shard_map/ppermute | solution.py:551
  17.1 0.3 shard_map.95
  17.4 3.1 %collective-permute-start.7 = (f32[320,128]{1,0:T(8,128)S(1)}, f32[320,128]{1,0:T(8,128)S(1)}, u32[]{:S(2)}, u32[]{:S(2)}) collective-permute-start(f32[320,128]{1,0:T(8,128)S(1)} %get-tuple-element.30.coef2), channel_id=1, source_target_pairs={{0,128},{32,160},{64,192},{96,224},{128,0},{160,32},{192,64},{224,... | collective-permute-start | bytes 491528 | tf_op jit(solution)/shard_map/ppermute | solution.py:551
  20.5 1.1 %collective-permute-start.6 = (f32[320,128]{1,0:T(8,128)S(1)}, f32[320,128]{1,0:T(8,128)S(1)}, u32[]{:S(2)}, u32[]{:S(2)}) collective-permute-start(f32[320,128]{1,0:T(8,128)S(1)} %get-tuple-element.30.coef2), channel_id=1, source_target_pairs={{0,192},{32,224},{64,128},{96,160},{128,64},{160,96},{192,0},{224,... | collective-permute-start | bytes 491528 | tf_op jit(solution)/shard_map/ppermute | solution.py:551
  21.6 1.7 %shard_map.92 = (f32[2304,128]{1,0:T(8,128)S(1)}, f32[256,128]{1,0:T(8,128)S(1)}) custom-call(f32[8,256]{1,0:T(8,128)S(1)} %get-tuple-element.21.slot_row.token, f32[512,128]{1,0:T(8,128)} %bitcast.20, f32[512,128]{1,0:T(8,128)} %bitcast.22, f32[512,128]{1,0:T(8,128)} %bitcast.24, f32[256,128]{1,0:T(8,128)} %refs_3_.3, s32[256,128]{1,0:T(8,128)} %refs_4_.3), custom_call_target="tpu_custom_call" | custom-call | bytes 4194304 | tf_op jit(solution)/shard_map/pallas_call | solution.py:539
  23.3 0.0 copy-start
  23.4 0.6 copy-done
  24.0 7.9 %all-to-all-done = f32[1056,1,128]{2,1,0:T(1,128)S(1)} async-done(((f32[1056,1,128]{2,1,0:T(1,128)}), f32[1056,1,128]{2,1,0:T(1,128)S(1)}, u32[]{:S(2)}, u32[]{:S(2)}) %all-to-all-start) | async-done | bytes 540704 | tf_op jit(solution)/shard_map/all_to_all | solution.py:556
  31.9 0.9 %shard_map.94 = (f32[128,128]{1,0:T(8,128)S(1)}, f32[128,128]{1,0:T(8,128)S(1)}, f32[72,128]{1,0:T(8,128)S(1)}, f32[8,128]{1,0:T(8,128)S(1)}) custom-call(s32[1]{0:T(128)} %bitcast.narrow, f32[1056,128]{1,0:T(8,128)S(1)} %bitcast.16, f32[1216,128]{1,0:T(8,128)S(1)} %get-tuple-element.25.level1, f32[2304,128]{1,0:T(8,128)S(1)} %get-tuple-element.22.token.fine), custom_call_target="tpu_custom_call" | custom-call | tf_op jit(solution)/shard_map/pallas_call | solution.py:539
  32.8 0.1 collective-permute-start
  32.9 1.2 %collective-permute-done.other = f32[128,128]{1,0:T(8,128)S(1)} collective-permute-done((f32[128,128]{1,0:T(8,128)S(1)}, f32[128,128]{1,0:T(8,128)S(1)}, u32[]{:S(2)}, u32[]{:S(2)}) %collective-permute-start) | collective-permute-done | bytes 65568 | tf_op jit(solution)/shard_map/ppermute | solution.py:551
  34.1 0.2 shard_map.96
  34.3 3.1 %collective-permute-start.4 = (f32[128,128]{1,0:T(8,128)S(1)}, f32[128,128]{1,0:T(8,128)S(1)}, u32[]{:S(2)}, u32[]{:S(2)}) collective-permute-start(f32[128,128]{1,0:T(8,128)S(1)} %get-tuple-element.29.left2), channel_id=1, source_target_pairs={{0,128},{32,160},{64,192},{96,224},{128,0},{160,32},{192,64},{224,... | collective-permute-start | bytes 196616 | tf_op jit(solution)/shard_map/ppermute | solution.py:551
  37.4 1.1 %collective-permute-start.3 = (f32[128,128]{1,0:T(8,128)S(1)}, f32[128,128]{1,0:T(8,128)S(1)}, u32[]{:S(2)}, u32[]{:S(2)}) collective-permute-start(f32[128,128]{1,0:T(8,128)S(1)} %get-tuple-element.29.left2), channel_id=1, source_target_pairs={{0,192},{32,224},{64,128},{96,160},{128,64},{160,96},{192,0},{224,... | collective-permute-start | bytes 196616 | tf_op jit(solution)/shard_map/ppermute | solution.py:551
  38.6 1.5 %shard_map.97.levels = f32[2880,128]{1,0:T(8,128)S(1)} custom-call(f32[320,128]{1,0:T(8,128)S(1)} %get-tuple-element.30.coef2, f32[320,128]{1,0:T(8,128)} %collective-permute-done.5.coef2_a, f32[320,128]{1,0:T(8,128)S(1)} %collective-permute-done.6.coef2_b, f32[320,128]{1,0:T(8,128)S(1)} %collective-permute-done.7.coef2_c), custom_call_target="tpu_custom_call" | custom-call | bytes 4194304 | tf_op jit(solution)/shard_map/pallas_call | solution.py:539
  40.1 0.3 shard_map.98
  40.4 2.5 %collective-permute-done.3.left2_b = f32[128,128]{1,0:T(8,128)S(1)} collective-permute-done((f32[128,128]{1,0:T(8,128)S(1)}, f32[128,128]{1,0:T(8,128)S(1)}, u32[]{:S(2)}, u32[]{:S(2)}) %collective-permute-start.3) | collective-permute-done | bytes 65568 | tf_op jit(solution)/shard_map/ppermute | solution.py:551
  42.9 1.2 %shard_map.99 = f32[1056,128]{1,0:T(8,128)S(1)} custom-call(f32[128,128]{1,0:T(8,128)S(1)} %get-tuple-element.29.left2, f32[128,128]{1,0:T(8,128)S(1)} %collective-permute-done.2.left2_a, f32[128,128]{1,0:T(8,128)S(1)} %collective-permute-done.3.left2_b, f32[128,128]{1,0:T(8,128)S(1)} %collective-permute-done.4.left2_c, f32[2880,128]{1,0:T(8,128)S(1)} %shard_map.97.levels, ...), custom_call_target="tpu_custom_call" | custom-call | tf_op jit(solution)/shard_map/pallas_call | solution.py:539
  44.1 21.5 %all_to_all.10 = f32[1056,1,128]{2,1,0:T(1,128)S(1)} all-to-all(f32[1056,1,128]{2,1,0:T(1,128)S(1)} %bitcast.18), channel_id=1, replica_groups=mesh['wide'=8,'narrow'=32] {'narrow'}, dimensions={0} | all-to-all | bytes 1081344 | tf_op jit(solution)/shard_map/all_to_all | solution.py:556
  65.6 1.5 %shard_map.100 = f32[512,128]{1,0:T(8,128)} custom-call(s32[1]{0:T(128)} %bitcast.narrow, f32[2304,128]{1,0:T(8,128)S(1)} %get-tuple-element.22.token.fine, f32[256,128]{1,0:T(8,128)S(1)} %copy-done.1, f32[1056,128]{1,0:T(8,128)S(1)} %bitcast.17, f32[72,128]{1,0:T(8,128)S(1)} %get-tuple-element.36.edges), custom_call_target="tpu_custom_call" | custom-call | tf_op jit(solution)/shard_map/pallas_call | solution.py:539
  (9 shorter events, 0.0 us)
Async XLA Ops:
  3.0 28.9 %all-to-all-start = ((f32[1056,1,128]{2,1,0:T(1,128)}), f32[1056,1,128]{2,1,0:T(1,128)S(1)}, u32[]{:S(2)}, u32[]{:S(2)}) async-start(f32[1056,1,128]{2,1,0:T(1,128)} %bitcast.6), calls=%async_computation | async-start | bytes 1081344 | tf_op jit(solution)/shard_map/all_to_all | solution.py:556
  15.6 1.5 %collective-permute-start.1 = (f32[320,128]{1,0:T(8,128)S(1)}, f32[320,128]{1,0:T(8,128)S(1)}, u32[]{:S(2)}, u32[]{:S(2)}) collective-permute-start(f32[320,128]{1,0:T(8,128)S(1)} %get-tuple-element.27.mine), channel_id=1, source_target_pairs={{0,32},{32,0},{64,96},{96,64},{128,160},{160,128},{192,224},{224,1... | collective-permute-start | bytes 491528 | tf_op jit(solution)/shard_map/ppermute | solution.py:551
  17.4 21.2 %collective-permute-start.7 = (f32[320,128]{1,0:T(8,128)S(1)}, f32[320,128]{1,0:T(8,128)S(1)}, u32[]{:S(2)}, u32[]{:S(2)}) collective-permute-start(f32[320,128]{1,0:T(8,128)S(1)} %get-tuple-element.30.coef2), channel_id=1, source_target_pairs={{0,128},{32,160},{64,192},{96,224},{128,0},{160,32},{192,64},{224,... | collective-permute-start | bytes 491528 | tf_op jit(solution)/shard_map/ppermute | solution.py:551
  20.5 18.1 %collective-permute-start.6 = (f32[320,128]{1,0:T(8,128)S(1)}, f32[320,128]{1,0:T(8,128)S(1)}, u32[]{:S(2)}, u32[]{:S(2)}) collective-permute-start(f32[320,128]{1,0:T(8,128)S(1)} %get-tuple-element.30.coef2), channel_id=1, source_target_pairs={{0,192},{32,224},{64,128},{96,160},{128,64},{160,96},{192,0},{224,... | collective-permute-start | bytes 491528 | tf_op jit(solution)/shard_map/ppermute | solution.py:551
  21.6 17.0 %collective-permute-start.5 = (f32[320,128]{1,0:T(8,128)S(1)}, f32[320,128]{1,0:T(8,128)}, u32[]{:S(2)}, u32[]{:S(2)}) collective-permute-start(f32[320,128]{1,0:T(8,128)S(1)} %get-tuple-element.30.coef2), channel_id=1, source_target_pairs={{0,64},{32,96},{64,0},{96,32},{128,192},{160,224},{192,128},{224,1... | collective-permute-start | bytes 491528 | tf_op jit(solution)/shard_map/ppermute | solution.py:551
  23.3 0.7 copy-start
  32.8 1.3 %collective-permute-start = (f32[128,128]{1,0:T(8,128)S(1)}, f32[128,128]{1,0:T(8,128)S(1)}, u32[]{:S(2)}, u32[]{:S(2)}) collective-permute-start(f32[128,128]{1,0:T(8,128)S(1)} %get-tuple-element.26.mine), channel_id=1, source_target_pairs={{0,32},{32,0},{64,96},{96,64},{128,160},{160,128},{192,224},{224,1... | collective-permute-start | bytes 196616 | tf_op jit(solution)/shard_map/ppermute | solution.py:551
  34.3 6.1 %collective-permute-start.4 = (f32[128,128]{1,0:T(8,128)S(1)}, f32[128,128]{1,0:T(8,128)S(1)}, u32[]{:S(2)}, u32[]{:S(2)}) collective-permute-start(f32[128,128]{1,0:T(8,128)S(1)} %get-tuple-element.29.left2), channel_id=1, source_target_pairs={{0,128},{32,160},{64,192},{96,224},{128,0},{160,32},{192,64},{224,... | collective-permute-start | bytes 196616 | tf_op jit(solution)/shard_map/ppermute | solution.py:551
  37.4 5.5 %collective-permute-start.3 = (f32[128,128]{1,0:T(8,128)S(1)}, f32[128,128]{1,0:T(8,128)S(1)}, u32[]{:S(2)}, u32[]{:S(2)}) collective-permute-start(f32[128,128]{1,0:T(8,128)S(1)} %get-tuple-element.29.left2), channel_id=1, source_target_pairs={{0,192},{32,224},{64,128},{96,160},{128,64},{160,96},{192,0},{224,... | collective-permute-start | bytes 196616 | tf_op jit(solution)/shard_map/ppermute | solution.py:551
  38.6 4.3 %collective-permute-start.2 = (f32[128,128]{1,0:T(8,128)S(1)}, f32[128,128]{1,0:T(8,128)S(1)}, u32[]{:S(2)}, u32[]{:S(2)}) collective-permute-start(f32[128,128]{1,0:T(8,128)S(1)} %get-tuple-element.29.left2), channel_id=1, source_target_pairs={{0,64},{32,96},{64,0},{96,32},{128,192},{160,224},{192,128},{224,1... | collective-permute-start | bytes 196616 | tf_op jit(solution)/shard_map/ppermute | solution.py:551
  42.9 22.7 %copy-start.1 = (f32[256,128]{1,0:T(8,128)S(1)}, f32[256,128]{1,0:T(8,128)}, u32[]{:S(2)}) copy-start(f32[256,128]{1,0:T(8,128)} %copy-done) | copy-start | bytes 393220

commit v6 on v5

--- a/solution.py
+++ b/solution.py
@@ -143,13 +143,17 @@
 
 
 def ready_kernel(slot_row, *refs):
-    inputs, fine, slots, held, sems = refs[0:5], refs[5], refs[6], refs[7:12], refs[12]
+    inputs, fine, slots, held = refs[0:5], refs[5], refs[6], refs[7:12]
+    sems, stage = refs[12:14]
     copies = start_copies(inputs, held, sems)
     slots[...] = jnp.transpose(jnp.broadcast_to(slot_row[0:1, :], (LANES, BLK)), (1, 0))
     for copy in copies:
         copy.wait()
     data, _, _, field, _ = fine_start(*held)
-    store(fine, [*field, *data.parts()])
+    store(stage, [*field, *data.parts()])
+    push = pltpu.make_async_copy(stage, fine, sems.at[0])
+    push.start()
+    push.wait()
 
 
 def pre_kernel(narrow, agg_hbm, *refs):
@@ -250,7 +254,7 @@
 PARTS = 7
 REACH = (2, 0, -2)
 TWICE = 4 * len(REACH)
-LEVEL_ROWS = (PARTS + TWICE) * AGG
+LEVEL_ROWS = (PARTS + 2 * TWICE) * AGG
 
 
 def shifted(v, cells):
@@ -270,6 +274,10 @@
         a[2] * b[0] + a[3] * b[2],
         a[2] * b[1] + a[3] * b[3],
     ]
+
+
+def scaled(rows, b):
+    return [rows[0] * b[0], rows[0] * b[1], rows[1] * b[2], rows[1] * b[3]]
 
 
 def plus(a, b):
@@ -307,15 +315,27 @@
             ),
             *product(from_right, right_after),
         ]
-        store(out, twice, at * LEVEL_ROWS + PARTS * AGG)
+        left, right = (l0, l1), (r0, r1)
+        rest = [
+            *scaled(left, left_before),
+            *plus(scaled(left, right_before), scaled(right, left_after)),
+            *scaled(right, right_after),
+        ]
+        store(out, [*twice, *rest], at * LEVEL_ROWS + PARTS * AGG)
 
     def __init__(self, ref, at=0):
         self.ref, self.at = ref, at * LEVEL_ROWS
         self.level = Level.load(load(ref, PARTS, AGG, self.at), chain_prev, chain_next)
 
     def begin(self, source):
-        field, inner = self.level.begin(source)
-        return field, self.level.leftover(source, inner)
+        g = self.level.step(source)
+        near = self.level.flow(g)
+        field = [(1.0 + KEEP) * a + b for a, b in zip(g, self.level.step(near))]
+        far = apply_blocks(load(self.ref, TWICE, AGG, self.at + (PARTS + TWICE) * AGG), g)
+        rest = [
+            ((KEEP * KEEP) * a + b) + (2.0 * KEEP) * c for a, b, c in zip(source, far, near)
+        ]
+        return field, rest
 
     def again(self, v, field):
         near = self.level.step(self.level.flow(v))
@@ -454,7 +474,7 @@
     source3_far = [a + b for a, b in zip(load2(left2_b), load2(left2_c))]
     level3, level4, level3_far = [Coarse(levels, k) for k in range(3)]
     below3, rest = level3.begin(source3)
-    _, rest_far = level3_far.begin(source3_far)
+    rest_far = level3_far.level.leftover(source3_far, level3_far.level.begin(source3_far)[1])
     v, _ = level4.begin(plus(rest, rest_far))
     v = level4.again(v, v)
     for level, field in (
@@ -530,7 +550,7 @@
         )
 
 
-def call(kernel, outs, *args, spaces=(), scratch=(), cost=None):
+def call(kernel, outs, *args, spaces=(), scratch=(), cost=None, out_spaces=None):
     spaces = (*spaces, *[pltpu.VMEM] * (len(args) - len(spaces)))
     args = [
         pltpu.with_memory_space_constraint(a, s) if s == pltpu.HBM else a
@@ -538,9 +558,14 @@
     ]
     return pl.pallas_call(
         kernel,
-        out_shape=[jax.ShapeDtypeStruct(s, k) for s, k in outs],
+        out_shape=[
+            pltpu.HBM(s, k) if space == pltpu.HBM else jax.ShapeDtypeStruct(s, k)
+            for (s, k), space in zip(outs, out_spaces or [pltpu.VMEM] * len(outs))
+        ],
         in_specs=[pl.BlockSpec(memory_space=space) for space in spaces],
-        out_specs=[pl.BlockSpec(memory_space=pltpu.VMEM) for _ in outs],
+        out_specs=[
+            pl.BlockSpec(memory_space=space) for space in out_spaces or [pltpu.VMEM] * len(outs)
+        ],
         scratch_shapes=scratch,
         cost_estimate=cost,
         compiler_params=pltpu.CompilerParams(vmem_limit_bytes=32 * 1024 * 1024),
@@ -602,7 +627,8 @@
         slot_row,
         *fine_args,
         spaces=(pltpu.VMEM, *[pltpu.HBM] * 5),
-        scratch=held + [pltpu.SemaphoreType.DMA((5,))],
+        scratch=held + [pltpu.SemaphoreType.DMA((5,))] + vmem(9 * BLK),
+        out_spaces=(pltpu.HBM, pltpu.VMEM),
         cost=beside,
     )
     coef2, level2 = call(pair_kernel, [five, level], coef1, exchange(coef1, 1), cost=beside)
@@ -620,7 +646,7 @@
         narrow,
         recv,
         level1,
-        fine,
+        slots,
         spaces=(pltpu.SMEM,),
     )
     hot, edges = call(

time: 67.8 us -> 67.9 us (level)
  waiting for transfers between devices: 13 us -> 14.2 us
    ppermute x8, waiting for transfers between devices: 5.12 us -> 6.81 us  [exchange(): lax.ppermute(value, 'wide', [(i, i ^ bits) for i in range(lax.axis_size('...]
  transfers between devices with their start and end apart: 9 -> 9, of which waited for: 4 -> 5; matrix products, arithmetic and copies ran while one was open for 0% -> 0% of each run, Pallas kernels for 9% -> 9%
where the time goes in v6:
time: 67.9 us; the launch traced here: 67.6 us
  blocking collectives  21.2 us (31%)
  starting transfers between devices  20.2 us (30%)
  waiting for transfers between devices  14.2 us (21%)
  Pallas kernels  11.9 us (18%)
    all_to_all x1, blocking collectives, to_all(): moved = lax.all_to_all(units.reshape(shape), 'narrow', 0, 0, tiled=True)  21.2 us
    pallas_call x10, Pallas kernels, call(): pl.pallas_call(kernel, out_shape=[pltpu.HBM(s, k) if space == pltpu.HBM e...  11.9 us
    all_to_all x1, starting transfers between devices, to_all(): moved = lax.all_to_all(units.reshape(shape), 'narrow', 0, 0, tiled=True)  11.4 us
    ppermute x8, starting transfers between devices, exchange(): lax.ppermute(value, 'wide', [(i, i ^ bits) for i in range(lax.axis_size('...  8.81 us
    all_to_all x1, waiting for transfers between devices, to_all(): moved = lax.all_to_all(units.reshape(shape), 'narrow', 0, 0, tiled=True)  7.42 us
    ppermute x8, waiting for transfers between devices, exchange(): lax.ppermute(value, 'wide', [(i, i ^ bits) for i in range(lax.axis_size('...  6.81 us
  transfers between devices with their start and end apart: 9, of which 5 were waited for; matrix products, arithmetic and copies ran while one was open for 0% of the time, Pallas kernels for 9%

profile of v6, /device:TPU:32, one launch (start us, length us, event | category | flops | bytes accessed | tf_op | source)
XLA Modules:
  0.0 67.6 jit_solution(9651909004053440353)
XLA Ops:
  0.0 3.0 %shard_map.91 = (f32[1056,128]{1,0:T(8,128)}, f32[8,256]{1,0:T(8,128)S(1)}) custom-call(s32[1]{0:T(128)} %bitcast.narrow, s32[1,256]{1,0:T(1,128)} %bitcast.27, f32[512,128]{1,0:T(8,128)} %bitcast.19, f32[512,128]{1,0:T(8,128)} %bitcast.21, f32[512,128]{1,0:T(8,128)} %bitcast.23, f32[256,128]{1,0:T(8,128)} %refs_3_.3, s32[256,128]{1,0:T(8,128)} %refs_4_.3), custom_call_target="tpu_custom_call" | custom-call | tf_op jit(solution)/shard_map/pallas_call | solution.py:559
  3.0 11.4 %all-to-all-start = ((f32[1056,1,128]{2,1,0:T(1,128)}), f32[1056,1,128]{2,1,0:T(1,128)S(1)}, u32[]{:S(2)}, u32[]{:S(2)}) async-start(f32[1056,1,128]{2,1,0:T(1,128)} %bitcast.6), calls=%async_computation | async-start | bytes 1081344 | tf_op jit(solution)/shard_map/all_to_all | solution.py:581
  14.4 1.2 %shard_map.93 = (f32[320,128]{1,0:T(8,128)S(1)}, f32[1984,128]{1,0:T(8,128)S(1)}) custom-call(f32[8,256]{1,0:T(8,128)S(1)} %get-tuple-element.21.slot_row.token, f32[128,128]{1,0:T(8,128)} %bitcast.25, f32[128,128]{1,0:T(8,128)} %bitcast.26, f32[64,128]{1,0:T(8,128)} %kap_hbm.1), custom_call_target="tpu_custom_call" | custom-call | bytes 4194304 | tf_op jit(solution)/shard_map/pallas_call | solution.py:559
  15.6 0.1 collective-permute-start.1
  15.7 1.4 %collective-permute-done.1.other = f32[320,128]{1,0:T(8,128)S(1)} collective-permute-done((f32[320,128]{1,0:T(8,128)S(1)}, f32[320,128]{1,0:T(8,128)S(1)}, u32[]{:S(2)}, u32[]{:S(2)}) %collective-permute-start.1) | collective-permute-done | bytes 163872 | tf_op jit(solution)/shard_map/ppermute | solution.py:576
  17.1 0.3 shard_map.95
  17.4 1.6 %collective-permute-start.5 = (f32[320,128]{1,0:T(8,128)S(1)}, f32[320,128]{1,0:T(8,128)S(1)}, u32[]{:S(2)}, u32[]{:S(2)}) collective-permute-start(f32[320,128]{1,0:T(8,128)S(1)} %get-tuple-element.30.coef2), channel_id=1, source_target_pairs={{0,64},{32,96},{64,0},{96,32},{128,192},{160,224},{192,128},{224,1... | collective-permute-start | bytes 491528 | tf_op jit(solution)/shard_map/ppermute | solution.py:576
  19.0 2.1 %collective-permute-start.6 = (f32[320,128]{1,0:T(8,128)S(1)}, f32[320,128]{1,0:T(8,128)S(1)}, u32[]{:S(2)}, u32[]{:S(2)}) collective-permute-start(f32[320,128]{1,0:T(8,128)S(1)} %get-tuple-element.30.coef2), channel_id=1, source_target_pairs={{0,192},{32,224},{64,128},{96,160},{128,64},{160,96},{192,0},{224,... | collective-permute-start | bytes 491528 | tf_op jit(solution)/shard_map/ppermute | solution.py:576
  21.1 0.6 collective-permute-start.7
  21.7 2.7 %shard_map.92 = (f32[2304,128]{1,0:T(8,128)}, f32[256,128]{1,0:T(8,128)S(1)}) custom-call(f32[8,256]{1,0:T(8,128)S(1)} %get-tuple-element.21.slot_row.token, f32[512,128]{1,0:T(8,128)} %bitcast.20, f32[512,128]{1,0:T(8,128)} %bitcast.22, f32[512,128]{1,0:T(8,128)} %bitcast.24, f32[256,128]{1,0:T(8,128)} %refs_3_.3, s32[256,128]{1,0:T(8,128)} %refs_4_.3), custom_call_target="tpu_custom_call" | custom-call | bytes 4194304 | tf_op jit(solution)/shard_map/pallas_call | solution.py:559
  24.5 7.4 %all-to-all-done = f32[1056,1,128]{2,1,0:T(1,128)S(1)} async-done(((f32[1056,1,128]{2,1,0:T(1,128)}), f32[1056,1,128]{2,1,0:T(1,128)S(1)}, u32[]{:S(2)}, u32[]{:S(2)}) %all-to-all-start) | async-done | bytes 540704 | tf_op jit(solution)/shard_map/all_to_all | solution.py:581
  31.9 0.8 %shard_map.94 = (f32[128,128]{1,0:T(8,128)S(1)}, f32[128,128]{1,0:T(8,128)S(1)}, f32[72,128]{1,0:T(8,128)S(1)}, f32[8,128]{1,0:T(8,128)S(1)}) custom-call(s32[1]{0:T(128)} %bitcast.narrow, f32[1056,128]{1,0:T(8,128)S(1)} %bitcast.17, f32[1984,128]{1,0:T(8,128)S(1)} %get-tuple-element.25.level1, f32[256,128]{1,0:T(8,128)S(1)} %get-tuple-element.23.token.slots), custom_call_target="tpu_custom_call" | custom-call | tf_op jit(solution)/shard_map/pallas_call | solution.py:559
  32.8 1.2 %collective-permute-done.other = f32[128,128]{1,0:T(8,128)S(1)} collective-permute-done((f32[128,128]{1,0:T(8,128)S(1)}, f32[128,128]{1,0:T(8,128)S(1)}, u32[]{:S(2)}, u32[]{:S(2)}) %collective-permute-start) | collective-permute-done | bytes 65568 | tf_op jit(solution)/shard_map/ppermute | solution.py:576
  34.1 0.2 shard_map.96
  34.3 1.6 %collective-permute-start.2 = (f32[128,128]{1,0:T(8,128)S(1)}, f32[128,128]{1,0:T(8,128)S(1)}, u32[]{:S(2)}, u32[]{:S(2)}) collective-permute-start(f32[128,128]{1,0:T(8,128)S(1)} %get-tuple-element.29.left2), channel_id=1, source_target_pairs={{0,64},{32,96},{64,0},{96,32},{128,192},{160,224},{192,128},{224,1... | collective-permute-start | bytes 196616 | tf_op jit(solution)/shard_map/ppermute | solution.py:576
  35.8 2.1 %collective-permute-start.3 = (f32[128,128]{1,0:T(8,128)S(1)}, f32[128,128]{1,0:T(8,128)S(1)}, u32[]{:S(2)}, u32[]{:S(2)}) collective-permute-start(f32[128,128]{1,0:T(8,128)S(1)} %get-tuple-element.29.left2), channel_id=1, source_target_pairs={{0,192},{32,224},{64,128},{96,160},{128,64},{160,96},{192,0},{224,... | collective-permute-start | bytes 196616 | tf_op jit(solution)/shard_map/ppermute | solution.py:576
  37.9 0.6 collective-permute-start.4
  38.6 0.6 shard_map.97.levels
  39.2 0.3 shard_map.98
  39.5 1.8 %collective-permute-done.3.left2_b = f32[128,128]{1,0:T(8,128)S(1)} collective-permute-done((f32[128,128]{1,0:T(8,128)S(1)}, f32[128,128]{1,0:T(8,128)S(1)}, u32[]{:S(2)}, u32[]{:S(2)}) %collective-permute-start.3) | collective-permute-done | bytes 65568 | tf_op jit(solution)/shard_map/ppermute | solution.py:576
  41.3 2.4 %collective-permute-done.4.left2_c = f32[128,128]{1,0:T(8,128)S(1)} collective-permute-done((f32[128,128]{1,0:T(8,128)S(1)}, f32[128,128]{1,0:T(8,128)S(1)}, u32[]{:S(2)}, u32[]{:S(2)}) %collective-permute-start.4) | collective-permute-done | bytes 65568 | tf_op jit(solution)/shard_map/ppermute | solution.py:576
  43.7 1.2 %shard_map.99 = f32[1056,128]{1,0:T(8,128)S(1)} custom-call(f32[128,128]{1,0:T(8,128)S(1)} %get-tuple-element.29.left2, f32[128,128]{1,0:T(8,128)S(1)} %collective-permute-done.2.left2_a, f32[128,128]{1,0:T(8,128)S(1)} %collective-permute-done.3.left2_b, f32[128,128]{1,0:T(8,128)S(1)} %collective-permute-done.4.left2_c, f32[4416,128]{1,0:T(8,128)S(1)} %shard_map.97.levels, ...), custom_call_target="tpu_custom_call" | custom-call | tf_op jit(solution)/shard_map/pallas_call | solution.py:559
  44.9 21.2 %all_to_all.10 = f32[1056,1,128]{2,1,0:T(1,128)S(1)} all-to-all(f32[1056,1,128]{2,1,0:T(1,128)S(1)} %bitcast.18), channel_id=1, replica_groups=mesh['wide'=8,'narrow'=32] {'narrow'}, dimensions={0} | all-to-all | bytes 1081344 | tf_op jit(solution)/shard_map/all_to_all | solution.py:581
  66.1 1.5 %shard_map.100 = f32[512,128]{1,0:T(8,128)} custom-call(s32[1]{0:T(128)} %bitcast.narrow, f32[2304,128]{1,0:T(8,128)S(1)} %copy-done, f32[256,128]{1,0:T(8,128)S(1)} %get-tuple-element.23.token.slots, f32[1056,128]{1,0:T(8,128)S(1)} %bitcast.16, f32[72,128]{1,0:T(8,128)S(1)} %get-tuple-element.36.edges), custom_call_target="tpu_custom_call" | custom-call | tf_op jit(solution)/shard_map/pallas_call | solution.py:559
  (7 shorter events, 0.1 us)
Async XLA Ops:
  3.0 28.9 %all-to-all-start = ((f32[1056,1,128]{2,1,0:T(1,128)}), f32[1056,1,128]{2,1,0:T(1,128)S(1)}, u32[]{:S(2)}, u32[]{:S(2)}) async-start(f32[1056,1,128]{2,1,0:T(1,128)} %bitcast.6), calls=%async_computation | async-start | bytes 1081344 | tf_op jit(solution)/shard_map/all_to_all | solution.py:581
  15.6 1.5 %collective-permute-start.1 = (f32[320,128]{1,0:T(8,128)S(1)}, f32[320,128]{1,0:T(8,128)S(1)}, u32[]{:S(2)}, u32[]{:S(2)}) collective-permute-start(f32[320,128]{1,0:T(8,128)S(1)} %get-tuple-element.27.mine), channel_id=1, source_target_pairs={{0,32},{32,0},{64,96},{96,64},{128,160},{160,128},{192,224},{224,1... | collective-permute-start | bytes 491528 | tf_op jit(solution)/shard_map/ppermute | solution.py:576
  17.4 20.5 %collective-permute-start.5 = (f32[320,128]{1,0:T(8,128)S(1)}, f32[320,128]{1,0:T(8,128)S(1)}, u32[]{:S(2)}, u32[]{:S(2)}) collective-permute-start(f32[320,128]{1,0:T(8,128)S(1)} %get-tuple-element.30.coef2), channel_id=1, source_target_pairs={{0,64},{32,96},{64,0},{96,32},{128,192},{160,224},{192,128},{224,1... | collective-permute-start | bytes 491528 | tf_op jit(solution)/shard_map/ppermute | solution.py:576
  19.0 19.6 %collective-permute-start.6 = (f32[320,128]{1,0:T(8,128)S(1)}, f32[320,128]{1,0:T(8,128)S(1)}, u32[]{:S(2)}, u32[]{:S(2)}) collective-permute-start(f32[320,128]{1,0:T(8,128)S(1)} %get-tuple-element.30.coef2), channel_id=1, source_target_pairs={{0,192},{32,224},{64,128},{96,160},{128,64},{160,96},{192,0},{224,... | collective-permute-start | bytes 491528 | tf_op jit(solution)/shard_map/ppermute | solution.py:576
  21.1 17.5 %collective-permute-start.7 = (f32[320,128]{1,0:T(8,128)S(1)}, f32[320,128]{1,0:T(8,128)S(1)}, u32[]{:S(2)}, u32[]{:S(2)}) collective-permute-start(f32[320,128]{1,0:T(8,128)S(1)} %get-tuple-element.30.coef2), channel_id=1, source_target_pairs={{0,128},{32,160},{64,192},{96,224},{128,0},{160,32},{192,64},{224,... | collective-permute-start | bytes 491528 | tf_op jit(solution)/shard_map/ppermute | solution.py:576
  32.7 1.3 %collective-permute-start = (f32[128,128]{1,0:T(8,128)S(1)}, f32[128,128]{1,0:T(8,128)S(1)}, u32[]{:S(2)}, u32[]{:S(2)}) collective-permute-start(f32[128,128]{1,0:T(8,128)S(1)} %get-tuple-element.26.mine), channel_id=1, source_target_pairs={{0,32},{32,0},{64,96},{96,64},{128,160},{160,128},{192,224},{224,1... | collective-permute-start | bytes 196616 | tf_op jit(solution)/shard_map/ppermute | solution.py:576
  34.3 5.3 %collective-permute-start.2 = (f32[128,128]{1,0:T(8,128)S(1)}, f32[128,128]{1,0:T(8,128)S(1)}, u32[]{:S(2)}, u32[]{:S(2)}) collective-permute-start(f32[128,128]{1,0:T(8,128)S(1)} %get-tuple-element.29.left2), channel_id=1, source_target_pairs={{0,64},{32,96},{64,0},{96,32},{128,192},{160,224},{192,128},{224,1... | collective-permute-start | bytes 196616 | tf_op jit(solution)/shard_map/ppermute | solution.py:576
  35.8 5.5 %collective-permute-start.3 = (f32[128,128]{1,0:T(8,128)S(1)}, f32[128,128]{1,0:T(8,128)S(1)}, u32[]{:S(2)}, u32[]{:S(2)}) collective-permute-start(f32[128,128]{1,0:T(8,128)S(1)} %get-tuple-element.29.left2), channel_id=1, source_target_pairs={{0,192},{32,224},{64,128},{96,160},{128,64},{160,96},{192,0},{224,... | collective-permute-start | bytes 196616 | tf_op jit(solution)/shard_map/ppermute | solution.py:576
  37.9 5.8 %collective-permute-start.4 = (f32[128,128]{1,0:T(8,128)S(1)}, f32[128,128]{1,0:T(8,128)S(1)}, u32[]{:S(2)}, u32[]{:S(2)}) collective-permute-start(f32[128,128]{1,0:T(8,128)S(1)} %get-tuple-element.29.left2), channel_id=1, source_target_pairs={{0,128},{32,160},{64,192},{96,224},{128,0},{160,32},{192,64},{224,... | collective-permute-start | bytes 196616 | tf_op jit(solution)/shard_map/ppermute | solution.py:576
  43.7 22.4 %copy-start = (f32[2304,128]{1,0:T(8,128)S(1)}, f32[2304,128]{1,0:T(8,128)}, u32[]{:S(2)}) copy-start(f32[2304,128]{1,0:T(8,128)} %get-tuple-element.22.fine) | copy-start | bytes 3538948

commit v7 on v5

--- a/solution.py
+++ b/solution.py
@@ -99,17 +99,15 @@
     return (iota(shape, 0) == shape[0] - 1) & (iota(shape, 1) == LANES - 1)
 
 
-def split3(x):
+def split2(x):
     hi = x.astype(BF16)
-    rest = x - hi.astype(F32)
-    mid = rest.astype(BF16)
-    return hi, mid, (rest - mid.astype(F32)).astype(BF16)
+    return hi, (x - hi.astype(F32)).astype(BF16)
 
 
 def select_rows(onehot, x):
     return jnp.dot(
-        jnp.concatenate([onehot] * 3, axis=1),
-        jnp.concatenate(split3(x), axis=0),
+        jnp.concatenate([onehot] * 2, axis=1),
+        jnp.concatenate(split2(x), axis=0),
         preferred_element_type=F32,
     )
 
@@ -465,7 +463,7 @@
         v = level.again(plus(field, v), field)
 
     both = jnp.concatenate([v[0], v[1]], axis=1)
-    both = jnp.concatenate([*split3(both), jnp.zeros((AGG, 2 * LANES), BF16)], axis=0)
+    both = jnp.concatenate([*split2(both), jnp.zeros((2 * AGG, 2 * LANES), BF16)], axis=0)
     rows = jnp.dot(hot[...], both, preferred_element_type=F32)
     for s in range(NARROW):
         for f in (0, 1):

time: 67.8 us -> 67.6 us (level)
  no operation moved by 1% of the time
where the time goes in v7:
time: 67.6 us; the launch traced here: 67 us
  blocking collectives  21.5 us (32%)
  starting transfers between devices  20.1 us (30%)
  waiting for transfers between devices  13 us (19%)
  Pallas kernels  11.6 us (17%)
    all_to_all x1, blocking collectives, to_all(): moved = lax.all_to_all(units.reshape(shape), 'narrow', 0, 0, tiled=True)  21.5 us
    pallas_call x10, Pallas kernels, call(): pl.pallas_call(kernel, out_shape=[jax.ShapeDtypeStruct(s, k) for s, k in...  11.6 us
    all_to_all x1, starting transfers between devices, to_all(): moved = lax.all_to_all(units.reshape(shape), 'narrow', 0, 0, tiled=True)  11.4 us
    ppermute x8, starting transfers between devices, exchange(): lax.ppermute(value, 'wide', [(i, i ^ bits) for i in range(lax.axis_size('...  8.69 us
    all_to_all x1, waiting for transfers between devices, to_all(): moved = lax.all_to_all(units.reshape(shape), 'narrow', 0, 0, tiled=True)  7.89 us
    ppermute x8, waiting for transfers between devices, exchange(): lax.ppermute(value, 'wide', [(i, i ^ bits) for i in range(lax.axis_size('...  5.13 us
  transfers between devices with their start and end apart: 9, of which 4 were waited for; matrix products, arithmetic and copies ran while one was open for 0% of the time, Pallas kernels for 9%

profile of v7, /device:TPU:32, one launch (start us, length us, event | category | flops | bytes accessed | tf_op | source)
XLA Modules:
  0.0 67.0 jit_solution(5735714789078477767)
XLA Ops:
  0.0 2.9 %shard_map.91 = (f32[1056,128]{1,0:T(8,128)}, f32[8,256]{1,0:T(8,128)S(1)}) custom-call(s32[1]{0:T(128)} %bitcast.narrow, s32[1,256]{1,0:T(1,128)} %bitcast.27, f32[512,128]{1,0:T(8,128)} %bitcast.19, f32[512,128]{1,0:T(8,128)} %bitcast.21, f32[512,128]{1,0:T(8,128)} %bitcast.23, f32[256,128]{1,0:T(8,128)} %refs_3_.3, s32[256,128]{1,0:T(8,128)} %refs_4_.3), custom_call_target="tpu_custom_call" | custom-call | tf_op jit(solution)/shard_map/pallas_call | solution.py:537
  2.9 11.4 %all-to-all-start = ((f32[1056,1,128]{2,1,0:T(1,128)}), f32[1056,1,128]{2,1,0:T(1,128)S(1)}, u32[]{:S(2)}, u32[]{:S(2)}) async-start(f32[1056,1,128]{2,1,0:T(1,128)} %bitcast.6), calls=%async_computation | async-start | bytes 1081344 | tf_op jit(solution)/shard_map/all_to_all | solution.py:554
  14.3 1.2 %shard_map.93 = (f32[320,128]{1,0:T(8,128)S(1)}, f32[1216,128]{1,0:T(8,128)S(1)}) custom-call(f32[8,256]{1,0:T(8,128)S(1)} %get-tuple-element.21.slot_row.token, f32[128,128]{1,0:T(8,128)} %bitcast.25, f32[128,128]{1,0:T(8,128)} %bitcast.26, f32[64,128]{1,0:T(8,128)} %kap_hbm.1), custom_call_target="tpu_custom_call" | custom-call | bytes 4194304 | tf_op jit(solution)/shard_map/pallas_call | solution.py:537
  15.5 0.1 collective-permute-start.1
  15.6 1.4 %collective-permute-done.1.other = f32[320,128]{1,0:T(8,128)S(1)} collective-permute-done((f32[320,128]{1,0:T(8,128)S(1)}, f32[320,128]{1,0:T(8,128)S(1)}, u32[]{:S(2)}, u32[]{:S(2)}) %collective-permute-start.1) | collective-permute-done | bytes 163872 | tf_op jit(solution)/shard_map/ppermute | solution.py:549
  17.0 0.3 shard_map.95
  17.3 3.1 %collective-permute-start.7 = (f32[320,128]{1,0:T(8,128)S(1)}, f32[320,128]{1,0:T(8,128)S(1)}, u32[]{:S(2)}, u32[]{:S(2)}) collective-permute-start(f32[320,128]{1,0:T(8,128)S(1)} %get-tuple-element.30.coef2), channel_id=1, source_target_pairs={{0,128},{32,160},{64,192},{96,224},{128,0},{160,32},{192,64},{224,... | collective-permute-start | bytes 491528 | tf_op jit(solution)/shard_map/ppermute | solution.py:549
  20.4 1.1 %collective-permute-start.6 = (f32[320,128]{1,0:T(8,128)S(1)}, f32[320,128]{1,0:T(8,128)S(1)}, u32[]{:S(2)}, u32[]{:S(2)}) collective-permute-start(f32[320,128]{1,0:T(8,128)S(1)} %get-tuple-element.30.coef2), channel_id=1, source_target_pairs={{0,192},{32,224},{64,128},{96,160},{128,64},{160,96},{192,0},{224,... | collective-permute-start | bytes 491528 | tf_op jit(solution)/shard_map/ppermute | solution.py:549
  21.5 1.7 %shard_map.92 = (f32[2304,128]{1,0:T(8,128)S(1)}, f32[256,128]{1,0:T(8,128)S(1)}) custom-call(f32[8,256]{1,0:T(8,128)S(1)} %get-tuple-element.21.slot_row.token, f32[512,128]{1,0:T(8,128)} %bitcast.20, f32[512,128]{1,0:T(8,128)} %bitcast.22, f32[512,128]{1,0:T(8,128)} %bitcast.24, f32[256,128]{1,0:T(8,128)} %refs_3_.3, s32[256,128]{1,0:T(8,128)} %refs_4_.3), custom_call_target="tpu_custom_call" | custom-call | bytes 4194304 | tf_op jit(solution)/shard_map/pallas_call | solution.py:537
  23.3 0.0 copy-start
  23.3 0.6 copy-done
  23.9 7.9 %all-to-all-done = f32[1056,1,128]{2,1,0:T(1,128)S(1)} async-done(((f32[1056,1,128]{2,1,0:T(1,128)}), f32[1056,1,128]{2,1,0:T(1,128)S(1)}, u32[]{:S(2)}, u32[]{:S(2)}) %all-to-all-start) | async-done | bytes 540704 | tf_op jit(solution)/shard_map/all_to_all | solution.py:554
  31.8 0.9 %shard_map.94 = (f32[128,128]{1,0:T(8,128)S(1)}, f32[128,128]{1,0:T(8,128)S(1)}, f32[72,128]{1,0:T(8,128)S(1)}, f32[8,128]{1,0:T(8,128)S(1)}) custom-call(s32[1]{0:T(128)} %bitcast.narrow, f32[1056,128]{1,0:T(8,128)S(1)} %bitcast.16, f32[1216,128]{1,0:T(8,128)S(1)} %get-tuple-element.25.level1, f32[2304,128]{1,0:T(8,128)S(1)} %get-tuple-element.22.token.fine), custom_call_target="tpu_custom_call" | custom-call | tf_op jit(solution)/shard_map/pallas_call | solution.py:537
  32.7 0.1 collective-permute-start
  32.8 1.2 %collective-permute-done.other = f32[128,128]{1,0:T(8,128)S(1)} collective-permute-done((f32[128,128]{1,0:T(8,128)S(1)}, f32[128,128]{1,0:T(8,128)S(1)}, u32[]{:S(2)}, u32[]{:S(2)}) %collective-permute-start) | collective-permute-done | bytes 65568 | tf_op jit(solution)/shard_map/ppermute | solution.py:549
  34.0 0.2 shard_map.96
  34.3 3.1 %collective-permute-start.4 = (f32[128,128]{1,0:T(8,128)S(1)}, f32[128,128]{1,0:T(8,128)S(1)}, u32[]{:S(2)}, u32[]{:S(2)}) collective-permute-start(f32[128,128]{1,0:T(8,128)S(1)} %get-tuple-element.29.left2), channel_id=1, source_target_pairs={{0,128},{32,160},{64,192},{96,224},{128,0},{160,32},{192,64},{224,... | collective-permute-start | bytes 196616 | tf_op jit(solution)/shard_map/ppermute | solution.py:549
  37.4 1.1 %collective-permute-start.3 = (f32[128,128]{1,0:T(8,128)S(1)}, f32[128,128]{1,0:T(8,128)S(1)}, u32[]{:S(2)}, u32[]{:S(2)}) collective-permute-start(f32[128,128]{1,0:T(8,128)S(1)} %get-tuple-element.29.left2), channel_id=1, source_target_pairs={{0,192},{32,224},{64,128},{96,160},{128,64},{160,96},{192,0},{224,... | collective-permute-start | bytes 196616 | tf_op jit(solution)/shard_map/ppermute | solution.py:549
  38.5 1.5 %shard_map.97.levels = f32[2880,128]{1,0:T(8,128)S(1)} custom-call(f32[320,128]{1,0:T(8,128)S(1)} %get-tuple-element.30.coef2, f32[320,128]{1,0:T(8,128)} %collective-permute-done.5.coef2_a, f32[320,128]{1,0:T(8,128)S(1)} %collective-permute-done.6.coef2_b, f32[320,128]{1,0:T(8,128)S(1)} %collective-permute-done.7.coef2_c), custom_call_target="tpu_custom_call" | custom-call | bytes 4194304 | tf_op jit(solution)/shard_map/pallas_call | solution.py:537
  40.0 0.3 shard_map.98
  40.4 2.5 %collective-permute-done.3.left2_b = f32[128,128]{1,0:T(8,128)S(1)} collective-permute-done((f32[128,128]{1,0:T(8,128)S(1)}, f32[128,128]{1,0:T(8,128)S(1)}, u32[]{:S(2)}, u32[]{:S(2)}) %collective-permute-start.3) | collective-permute-done | bytes 65568 | tf_op jit(solution)/shard_map/ppermute | solution.py:549
  42.9 1.2 %shard_map.99 = f32[1056,128]{1,0:T(8,128)S(1)} custom-call(f32[128,128]{1,0:T(8,128)S(1)} %get-tuple-element.29.left2, f32[128,128]{1,0:T(8,128)S(1)} %collective-permute-done.2.left2_a, f32[128,128]{1,0:T(8,128)S(1)} %collective-permute-done.3.left2_b, f32[128,128]{1,0:T(8,128)S(1)} %collective-permute-done.4.left2_c, f32[2880,128]{1,0:T(8,128)S(1)} %shard_map.97.levels, ...), custom_call_target="tpu_custom_call" | custom-call | tf_op jit(solution)/shard_map/pallas_call | solution.py:537
  44.1 21.5 %all_to_all.10 = f32[1056,1,128]{2,1,0:T(1,128)S(1)} all-to-all(f32[1056,1,128]{2,1,0:T(1,128)S(1)} %bitcast.18), channel_id=1, replica_groups=mesh['wide'=8,'narrow'=32] {'narrow'}, dimensions={0} | all-to-all | bytes 1081344 | tf_op jit(solution)/shard_map/all_to_all | solution.py:554
  65.6 1.4 %shard_map.100 = f32[512,128]{1,0:T(8,128)} custom-call(s32[1]{0:T(128)} %bitcast.narrow, f32[2304,128]{1,0:T(8,128)S(1)} %get-tuple-element.22.token.fine, f32[256,128]{1,0:T(8,128)S(1)} %copy-done.1, f32[1056,128]{1,0:T(8,128)S(1)} %bitcast.17, f32[72,128]{1,0:T(8,128)S(1)} %get-tuple-element.36.edges), custom_call_target="tpu_custom_call" | custom-call | tf_op jit(solution)/shard_map/pallas_call | solution.py:537
  (9 shorter events, 0.0 us)
Async XLA Ops:
  2.9 28.9 %all-to-all-start = ((f32[1056,1,128]{2,1,0:T(1,128)}), f32[1056,1,128]{2,1,0:T(1,128)S(1)}, u32[]{:S(2)}, u32[]{:S(2)}) async-start(f32[1056,1,128]{2,1,0:T(1,128)} %bitcast.6), calls=%async_computation | async-start | bytes 1081344 | tf_op jit(solution)/shard_map/all_to_all | solution.py:554
  15.5 1.5 %collective-permute-start.1 = (f32[320,128]{1,0:T(8,128)S(1)}, f32[320,128]{1,0:T(8,128)S(1)}, u32[]{:S(2)}, u32[]{:S(2)}) collective-permute-start(f32[320,128]{1,0:T(8,128)S(1)} %get-tuple-element.27.mine), channel_id=1, source_target_pairs={{0,32},{32,0},{64,96},{96,64},{128,160},{160,128},{192,224},{224,1... | collective-permute-start | bytes 491528 | tf_op jit(solution)/shard_map/ppermute | solution.py:549
  17.3 21.2 %collective-permute-start.7 = (f32[320,128]{1,0:T(8,128)S(1)}, f32[320,128]{1,0:T(8,128)S(1)}, u32[]{:S(2)}, u32[]{:S(2)}) collective-permute-start(f32[320,128]{1,0:T(8,128)S(1)} %get-tuple-element.30.coef2), channel_id=1, source_target_pairs={{0,128},{32,160},{64,192},{96,224},{128,0},{160,32},{192,64},{224,... | collective-permute-start | bytes 491528 | tf_op jit(solution)/shard_map/ppermute | solution.py:549
  20.4 18.1 %collective-permute-start.6 = (f32[320,128]{1,0:T(8,128)S(1)}, f32[320,128]{1,0:T(8,128)S(1)}, u32[]{:S(2)}, u32[]{:S(2)}) collective-permute-start(f32[320,128]{1,0:T(8,128)S(1)} %get-tuple-element.30.coef2), channel_id=1, source_target_pairs={{0,192},{32,224},{64,128},{96,160},{128,64},{160,96},{192,0},{224,... | collective-permute-start | bytes 491528 | tf_op jit(solution)/shard_map/ppermute | solution.py:549
  21.5 17.0 %collective-permute-start.5 = (f32[320,128]{1,0:T(8,128)S(1)}, f32[320,128]{1,0:T(8,128)}, u32[]{:S(2)}, u32[]{:S(2)}) collective-permute-start(f32[320,128]{1,0:T(8,128)S(1)} %get-tuple-element.30.coef2), channel_id=1, source_target_pairs={{0,64},{32,96},{64,0},{96,32},{128,192},{160,224},{192,128},{224,1... | collective-permute-start | bytes 491528 | tf_op jit(solution)/shard_map/ppermute | solution.py:549
  23.3 0.7 copy-start
  32.7 1.3 %collective-permute-start = (f32[128,128]{1,0:T(8,128)S(1)}, f32[128,128]{1,0:T(8,128)S(1)}, u32[]{:S(2)}, u32[]{:S(2)}) collective-permute-start(f32[128,128]{1,0:T(8,128)S(1)} %get-tuple-element.26.mine), channel_id=1, source_target_pairs={{0,32},{32,0},{64,96},{96,64},{128,160},{160,128},{192,224},{224,1... | collective-permute-start | bytes 196616 | tf_op jit(solution)/shard_map/ppermute | solution.py:549
  34.3 6.1 %collective-permute-start.4 = (f32[128,128]{1,0:T(8,128)S(1)}, f32[128,128]{1,0:T(8,128)S(1)}, u32[]{:S(2)}, u32[]{:S(2)}) collective-permute-start(f32[128,128]{1,0:T(8,128)S(1)} %get-tuple-element.29.left2), channel_id=1, source_target_pairs={{0,128},{32,160},{64,192},{96,224},{128,0},{160,32},{192,64},{224,... | collective-permute-start | bytes 196616 | tf_op jit(solution)/shard_map/ppermute | solution.py:549
  37.4 5.5 %collective-permute-start.3 = (f32[128,128]{1,0:T(8,128)S(1)}, f32[128,128]{1,0:T(8,128)S(1)}, u32[]{:S(2)}, u32[]{:S(2)}) collective-permute-start(f32[128,128]{1,0:T(8,128)S(1)} %get-tuple-element.29.left2), channel_id=1, source_target_pairs={{0,192},{32,224},{64,128},{96,160},{128,64},{160,96},{192,0},{224,... | collective-permute-start | bytes 196616 | tf_op jit(solution)/shard_map/ppermute | solution.py:549
  38.5 4.3 %collective-permute-start.2 = (f32[128,128]{1,0:T(8,128)S(1)}, f32[128,128]{1,0:T(8,128)S(1)}, u32[]{:S(2)}, u32[]{:S(2)}) collective-permute-start(f32[128,128]{1,0:T(8,128)S(1)} %get-tuple-element.29.left2), channel_id=1, source_target_pairs={{0,64},{32,96},{64,0},{96,32},{128,192},{160,224},{192,128},{224,1... | collective-permute-start | bytes 196616 | tf_op jit(solution)/shard_map/ppermute | solution.py:549
  42.9 22.7 %copy-start.1 = (f32[256,128]{1,0:T(8,128)S(1)}, f32[256,128]{1,0:T(8,128)}, u32[]{:S(2)}) copy-start(f32[256,128]{1,0:T(8,128)} %copy-done) | copy-start | bytes 393220
